TPU v7x, 256 devices: a whole 4x4x8 slice. The times are simulated.
256 devices in a mesh: src: 32 (over x_lo, z, core), tgt: 8 (over x_hi, y).
Axes of the slice: x: 4 (x_hi: 2, x_lo: 2; x = x_hi * 2 + x_lo), y: 4, z: 8, core: 2. Of those that a mesh axis runs over, the one named last changes fastest.
Arguments:
- weights_in: bfloat16 [4, 32768, 32, 128], P(None, ('src', 'tgt')), may hold values from -6 to 6
- twiddles: float32 [4, 4, 32768, 128], P(None, None, ('src', 'tgt')), may hold values from -1 to 1, as said below
- kernels: bfloat16 [3, 2, 2, 128, 128], replicated, may hold values from -1 to 1
Outputs:
- weights_out: bfloat16 [4, 32768, 32, 128], P(None, ('src', 'tgt'))
Inputs may be any that keep to these rules, and one draw needn't show every extreme that they name: `twiddles`: entries j and j + 64 of each twiddle row are the cosine and sine of one angle.
All inputs are finite; a program needn't handle non-finite values.
Results may differ from a plain program's by a relative error of at most 0.018.
Values may be sent and summed in bfloat16 or wider, within the bound.
No kernel may reach another device: no remote copies, remote signals or barrier semaphores. Data moves between devices by JAX's collectives and lax.ppermute only.
A program may use at most 64 MiB of HBM per device.

v0:
```python
import jax
import jax.numpy as jnp
from jax import lax
from jax.sharding import PartitionSpec as P


def partner_2(block, axis, distance):
    count = lax.axis_size(axis)
    route = []
    for low in range(count):
        high = low | 1 << distance
        if high != low and high < count:
            route += [(low, high), (high, low)]
    return lax.ppermute(block, axis, route)


def rotate_phase(current, twiddle_row):
    half_width = twiddle_row.shape[-1] // 2
    cosine = twiddle_row[..., None, :half_width]
    sine_part = twiddle_row[..., None, half_width:]
    real_part = current[..., :half_width]
    imag_part = current[..., half_width:]
    return jnp.concatenate(
        [cosine * real_part - sine_part * imag_part, sine_part * real_part + cosine * imag_part], -1
    )


def apply_pair(own_slots, partner, level_kernels, child_bit):
    width = own_slots.shape[-1]
    own_term = jnp.dot(
        own_slots.reshape(-1, width),
        level_kernels[child_bit, child_bit],
        preferred_element_type=jnp.float32,
    )
    other_term = jnp.dot(
        partner.reshape(-1, width),
        level_kernels[child_bit, 1 - child_bit],
        preferred_element_type=jnp.float32,
    )
    return (own_term + other_term).reshape(own_slots.shape)


def body(weights_in, twiddles, kernels):
    src_top = lax.axis_size("src").bit_length() - 1
    tgt_top = lax.axis_size("tgt").bit_length() - 1
    current = weights_in
    for level_index in range(2):
        swap_bit = src_top - 1 - level_index
        child_bit = lax.axis_index("src") // 2**swap_bit % 2
        level_inputs = rotate_phase(current, twiddles[level_index]).astype(jnp.bfloat16)
        level_kernels = kernels[level_index]
        partner = partner_2(level_inputs, "src", swap_bit)
        current = apply_pair(level_inputs, partner, level_kernels, child_bit)
    inputs = rotate_phase(current, twiddles[2]).astype(jnp.bfloat16)
    swap_bit = tgt_top - 1
    child_bit = lax.axis_index("tgt") // 2**swap_bit % 2
    level_kernels = kernels[2]
    partner = partner_2(inputs, "tgt", swap_bit)
    current = apply_pair(inputs, partner, level_kernels, child_bit)
    return rotate_phase(current, twiddles[3]).astype(jnp.bfloat16)


def solution(mesh):
    return jax.shard_map(
        body,
        mesh=mesh,
        in_specs=(P(None, ("src", "tgt"), None, None), P(None, None, ("src", "tgt"), None), P()),
        out_specs=P(None, ("src", "tgt"), None, None),
        check_vma=False,
    )
```

profile of v0, /device:TPU:80, one launch (start us, length us, event | category | flops | bytes accessed | tf_op | source)
XLA Modules:
  0.0 420.4 jit_solution(8897611156760394915)
XLA Ops:
  0.0 1.3 slice_bitcast_fusion.3
  1.3 0.1 fusion.41
  1.4 6.6 %fusion.1 = (bf16[4,128,32,64]{3,2,1,0:T(8,128)(2,1)S(1)}, bf16[4,128,32,64]{3,2,1,0:T(8,128)(2,1)S(1)}) fusion(f32[4,128,64]{2,1,0:T(8,128)S(1)} %get-tuple-element.27, f32[4,128,64]{2,1,0:T(8,128)S(1)} %get-tuple-element.26, bf16[4,128,32,128]{3,2,1,0:T(8,128)(2,1)} %param.3), kind=kLoop, calls=%fused_computation.8 | loop fusion | flops 10485760 | bytes 8650752 | tf_op jit(solution)/shard_map/convert.19
  8.0 0.0 copy-start.5
  8.0 0.0 copy-start.6
  8.0 1.9 copy-done.4
  10.0 3.7 pad_maximum_fusion
  13.6 1.5 collective-permute-start
  15.2 0.1 fusion.40
  15.3 5.8 %fusion.4 = f32[16384,128]{1,0:T(8,128)S(1)} fusion(bf16[16384,64]{1,0:T(8,128)(2,1)} %bitcast.49, bf16[16384,64]{1,0:T(8,128)(2,1)} %bitcast.48, bf16[1,2,2,128,128]{4,3,2,1,0:T(8,128)(2,1)S(1)} %get-tuple-element.18, s32[]{:T(128)S(6)} %select_n.51), kind=kOutput, calls=%fused_computation.17 | convolution fusion | flops 545259520 | bytes 12615684 | tf_op jit(solution)/shard_map/dot_general | solution.py:30
  21.1 85.2 %collective-permute-done = bf16[4,128,32,128]{3,2,1,0:T(8,128)(2,1)} collective-permute-done((bf16[4,128,32,128]{3,2,1,0:T(8,128)(2,1)}, bf16[4,128,32,128]{3,2,1,0:T(8,128)(2,1)}, u32[]{:S(2)}, u32[]{:S(2)}) %collective-permute-start) | collective-permute-done | bytes 4194336 | tf_op jit(solution)/shard_map/ppermute | solution.py:14
  106.3 3.4 convolution_add_fusion.2
  109.7 3.0 subtract_convert_fusion.2
  112.7 0.0 copy-start.3
  112.8 1.9 copy-done.2
  114.7 3.7 pad_maximum_fusion.1
  118.4 5.4 %collective-permute-start.1 = (bf16[4,128,32,128]{3,2,1,0:T(8,128)(2,1)}, bf16[4,128,32,128]{3,2,1,0:T(8,128)(2,1)}, u32[]{:S(2)}, u32[]{:S(2)}) collective-permute-start(bf16[4,128,32,128]{3,2,1,0:T(8,128)(2,1)} %pad_maximum_fusion.1), channel_id=1, source_target_pairs={{0,64},{64,0},{8,72},{72,8},{16,80},{80,16},{24,88},{88,24},{32,96... | collective-permute-start | bytes 12582920 | tf_op jit(solution)/shard_map/ppermute | solution.py:14
  123.8 0.1 fusion.39
  123.9 5.8 %fusion.8 = f32[16384,128]{1,0:T(8,128)S(1)} fusion(bf16[16384,64]{1,0:T(8,128)(2,1)} %bitcast.47, bf16[16384,64]{1,0:T(8,128)(2,1)} %bitcast.46, bf16[1,2,2,128,128]{4,3,2,1,0:T(8,128)(2,1)S(1)} %get-tuple-element.19, s32[]{:T(128)S(6)} %select_n.55), kind=kOutput, calls=%fused_computation.22 | convolution fusion | flops 545259520 | bytes 12615684 | tf_op jit(solution)/shard_map/dot_general | solution.py:30
  129.7 174.9 %collective-permute-done.1 = bf16[4,128,32,128]{3,2,1,0:T(8,128)(2,1)} collective-permute-done((bf16[4,128,32,128]{3,2,1,0:T(8,128)(2,1)}, bf16[4,128,32,128]{3,2,1,0:T(8,128)(2,1)}, u32[]{:S(2)}, u32[]{:S(2)}) %collective-permute-start.1) | collective-permute-done | bytes 4194336 | tf_op jit(solution)/shard_map/ppermute | solution.py:14
  304.6 3.4 convolution_add_fusion.1
  308.0 3.0 subtract_convert_fusion.1
  311.1 0.0 copy-start.1
  311.1 1.9 copy-done
  313.0 3.7 pad_maximum_fusion.2
  316.7 3.0 collective-permute-start.2
  319.7 0.1 fusion.38
  319.9 5.8 %fusion.12 = f32[16384,128]{1,0:T(8,128)S(1)} fusion(bf16[16384,64]{1,0:T(8,128)(2,1)} %bitcast.45, bf16[16384,64]{1,0:T(8,128)(2,1)} %bitcast.44, bf16[1,2,2,128,128]{4,3,2,1,0:T(8,128)(2,1)S(1)} %get-tuple-element.17, s32[]{:T(128)S(6)} %select_n.59), kind=kOutput, calls=%fused_computation.27 | convolution fusion | flops 545259520 | bytes 12615684 | tf_op jit(solution)/shard_map/dot_general | solution.py:30
  325.7 84.6 %collective-permute-done.2 = bf16[4,128,32,128]{3,2,1,0:T(8,128)(2,1)} collective-permute-done((bf16[4,128,32,128]{3,2,1,0:T(8,128)(2,1)}, bf16[4,128,32,128]{3,2,1,0:T(8,128)(2,1)}, u32[]{:S(2)}, u32[]{:S(2)}) %collective-permute-start.2) | collective-permute-done | bytes 4194336 | tf_op jit(solution)/shard_map/ppermute | solution.py:14
  410.2 3.4 convolution_add_fusion
  413.7 3.0 subtract_convert_fusion
  416.7 3.7 pad_maximum_fusion.3
  (8 shorter events, 0.0 us)
Async XLA Ops:
  8.0 2.0 copy-start.4
  8.0 5.6 %copy-start.5 = (bf16[4,128,32,64]{3,2,1,0:T(8,128)(2,1)}, bf16[4,128,32,64]{3,2,1,0:T(8,128)(2,1)S(1)}, u32[]{:S(2)}) copy-start(bf16[4,128,32,64]{3,2,1,0:T(8,128)(2,1)S(1)} %get-tuple-element.12) | copy-start | bytes 6291460
  8.0 7.1 %copy-start.6 = (bf16[3,2,2,128,128]{4,3,2,1,0:T(8,128)(2,1)S(1)}, bf16[3,2,2,128,128]{4,3,2,1,0:T(8,128)(2,1)}, u32[]{:S(2)}) copy-start(bf16[3,2,2,128,128]{4,3,2,1,0:T(8,128)(2,1)} %param.5) | copy-start | bytes 1179652
  13.6 92.6 %collective-permute-start = (bf16[4,128,32,128]{3,2,1,0:T(8,128)(2,1)}, bf16[4,128,32,128]{3,2,1,0:T(8,128)(2,1)}, u32[]{:S(2)}, u32[]{:S(2)}) collective-permute-start(bf16[4,128,32,128]{3,2,1,0:T(8,128)(2,1)} %pad_maximum_fusion), channel_id=1, source_target_pairs={{0,128},{128,0},{8,136},{136,8},{16,144},{144,16},{24,152},{152,24... | collective-permute-start | bytes 12582920 | tf_op jit(solution)/shard_map/ppermute | solution.py:14
  112.7 2.0 copy-start.2
  112.7 5.6 %copy-start.3 = (bf16[4,128,32,64]{3,2,1,0:T(8,128)(2,1)}, bf16[4,128,32,64]{3,2,1,0:T(8,128)(2,1)S(1)}, u32[]{:S(2)}) copy-start(bf16[4,128,32,64]{3,2,1,0:T(8,128)(2,1)S(1)} %get-tuple-element.10) | copy-start | bytes 6291460
  118.4 186.2 %collective-permute-start.1 = (bf16[4,128,32,128]{3,2,1,0:T(8,128)(2,1)}, bf16[4,128,32,128]{3,2,1,0:T(8,128)(2,1)}, u32[]{:S(2)}, u32[]{:S(2)}) collective-permute-start(bf16[4,128,32,128]{3,2,1,0:T(8,128)(2,1)} %pad_maximum_fusion.1), channel_id=1, source_target_pairs={{0,64},{64,0},{8,72},{72,8},{16,80},{80,16},{24,88},{88,24},{32,96... | collective-permute-start | bytes 12582920 | tf_op jit(solution)/shard_map/ppermute | solution.py:14
  311.1 2.0 copy-start
  311.1 5.6 %copy-start.1 = (bf16[4,128,32,64]{3,2,1,0:T(8,128)(2,1)}, bf16[4,128,32,64]{3,2,1,0:T(8,128)(2,1)S(1)}, u32[]{:S(2)}) copy-start(bf16[4,128,32,64]{3,2,1,0:T(8,128)(2,1)S(1)} %get-tuple-element.8) | copy-start | bytes 6291460
  316.7 93.5 %collective-permute-start.2 = (bf16[4,128,32,128]{3,2,1,0:T(8,128)(2,1)}, bf16[4,128,32,128]{3,2,1,0:T(8,128)(2,1)}, u32[]{:S(2)}, u32[]{:S(2)}) collective-permute-start(bf16[4,128,32,128]{3,2,1,0:T(8,128)(2,1)} %pad_maximum_fusion.2), channel_id=1, source_target_pairs={{0,4},{4,0},{1,5},{5,1},{2,6},{6,2},{3,7},{7,3},{8,12},{12,8},{9,1... | collective-permute-start | bytes 12582920 | tf_op jit(solution)/shard_map/ppermute | solution.py:14
where the time goes:
time: 421 us; the launch traced here: 420 us
  waiting for transfers between devices  345 us (82%)
  other arithmetic  30.4 us (7%)
  matrix products  27.6 us (7%)
  starting transfers between devices  9.91 us (2%)
  local copies, waits for them, and re-layouts  7.62 us (2%)
    ppermute x3, waiting for transfers between devices, partner_2(): return lax.ppermute(block, axis, route)  345 us
    dot_general x3, matrix products, apply_pair(): jnp.dot(own_slots.reshape(-1, width), level_kernels[child_bit, child_bit]...  17.4 us
    another operation x4, other arithmetic  15.7 us
    concatenate x4, other arithmetic, rotate_phase(): jnp.concatenate([cosine * real_part - sine_part * imag_part, sine_part *...  14.7 us
    dot_general x3, matrix products, apply_pair(): jnp.dot(partner.reshape(-1, width), level_kernels[child_bit, 1 - child_bi...  10.3 us
    ppermute x3, starting transfers between devices, partner_2(): return lax.ppermute(block, axis, route)  9.91 us
  transfers between devices with their start and end apart: 3, of which 3 were waited for; matrix products, arithmetic and copies ran while one was open for 4% of the time, Pallas kernels for 0%

commit v1 on v0

v1 whole, which is shorter than its diff:
```python
import functools

import jax
import jax.numpy as jnp
from jax import lax
from jax.experimental import pallas as pl
from jax.experimental.pallas import tpu as pltpu
from jax.sharding import PartitionSpec as P

FIRST, SECOND, THIRD = 4, 2, 1
GATHERED = 2
TILE = 32
VMEM = 48 * 2**20


def swap(block, mask):
    n_src, n_tgt = lax.axis_size("src"), lax.axis_size("tgt")
    flip_src = (n_src // 2 if mask & FIRST else 0) + (n_src // 4 if mask & SECOND else 0)
    flip_tgt = n_tgt // 2 if mask & THIRD else 0
    if not flip_tgt:
        return lax.ppermute(block, "src", [(i, i ^ flip_src) for i in range(n_src)])
    if not flip_src:
        return lax.ppermute(block, "tgt", [(i, i ^ flip_tgt) for i in range(n_tgt)])
    route = []
    for i in range(n_src):
        for j in range(n_tgt):
            route.append((i * n_tgt + j, (i ^ flip_src) * n_tgt + (j ^ flip_tgt)))
    return lax.ppermute(block, ("src", "tgt"), route)


def my_order():
    n_src, n_tgt = lax.axis_size("src"), lax.axis_size("tgt")
    place = lax.axis_index("src") // (n_src // 4) * 2 + lax.axis_index("tgt") // (n_tgt // 2)
    return jnp.bitwise_xor(place.astype(jnp.int32), jnp.arange(8, dtype=jnp.int32))


def roll_half(block):
    return pltpu.roll(block, block.shape[-1] // 2, 1)


def phases(rows):
    turned = roll_half(rows)
    low = lax.broadcasted_iota(jnp.int32, rows.shape, 1) < rows.shape[-1] // 2
    return jnp.where(low, rows, turned)[:, None, :], jnp.where(low, -turned, rows)[:, None, :]


def twist(plain, turned, rows):
    co, si = phases(rows)
    shape = (rows.shape[0], plain.shape[0] // rows.shape[0], plain.shape[1])
    return (plain.reshape(shape) * co + turned.reshape(shape) * si).reshape(plain.shape)


def twist_16(block, rows):
    wide = block.astype(jnp.float32)
    return twist(wide, roll_half(wide), rows)


def call(kernel, out_shape, grid, in_specs, out_specs, args, order, scratch=(), aliases=None, flops=0, nbytes=0):
    return pl.pallas_call(
        kernel,
        out_shape=out_shape,
        grid_spec=pltpu.PrefetchScalarGridSpec(
            num_scalar_prefetch=1, grid=grid, in_specs=in_specs, out_specs=out_specs, scratch_shapes=list(scratch)
        ),
        input_output_aliases=aliases or {},
        compiler_params=pltpu.CompilerParams(vmem_limit_bytes=VMEM),
        cost_estimate=pl.CostEstimate(flops=flops, bytes_accessed=nbytes, transcendentals=0),
    )(order, *args)


def first_kernel(order, w, t, _, out):
    slots, laws, width = out.shape
    out[...] = twist_16(w[0].reshape(slots * laws, width), t[0, 0]).astype(out.dtype).reshape(out.shape)


def first_twist(order, weights, twiddles, target, after):
    _, slots, laws, width = weights.shape
    tile = min(TILE, slots)
    return call(
        first_kernel,
        jax.ShapeDtypeStruct((slots, laws, width), weights.dtype),
        (slots // tile,),
        [
            pl.BlockSpec((1, tile, laws, width), lambda i, o: (target, i, 0, 0)),
            pl.BlockSpec((1, 1, tile, width), lambda i, o: (0, target, i, 0)),
            pl.BlockSpec(memory_space=pl.ANY),
        ],
        pl.BlockSpec((tile, laws, width), lambda i, o: (i, 0, 0)),
        (weights, twiddles, after),
        order,
        nbytes=4 * slots * laws * width,
    )


def level_kernel(bit, order, own, other, maps, t, *rest):
    out, both = rest[-2], rest[-1]
    slots, laws, width = own.shape

    @pl.when(pl.program_id(0) == 0)
    def _():
        child = lax.div(order[0], bit) & 1
        for source in range(2):
            part = maps[0, child, child if source == 0 else 1 - child]
            both[source * width : (source + 1) * width, :width] = part
            turned = roll_half(part.astype(jnp.float32)).astype(part.dtype)
            both[source * width : (source + 1) * width, width:] = turned

    rows = slots * laws
    state = jnp.dot(own[...].reshape(rows, width), both[:width, :], preferred_element_type=jnp.float32)
    state += jnp.dot(other[...].reshape(rows, width), both[width:, :], preferred_element_type=jnp.float32)
    out[...] = twist(state[:, :width], state[:, width:], t[0, 0]).astype(out.dtype).reshape(out.shape)


def level(order, own, other, kernels, twiddles, index, bit, target, whole=None, last=False):
    slots, laws, width = own.shape
    tile = min(TILE, slots)
    block = pl.BlockSpec((tile, laws, width), lambda i, o: (i, 0, 0))
    in_specs = [
        block,
        block,
        pl.BlockSpec((1, 2, 2, width, width), lambda i, o: (index, 0, 0, 0, 0)),
        pl.BlockSpec((1, 1, tile, width), lambda i, o: (index + 1, target, i, 0)),
    ]
    args, aliases = [own, other, kernels, twiddles], {}
    out_shape, out_spec = jax.ShapeDtypeStruct(own.shape, own.dtype), block
    if last:
        out_shape = jax.ShapeDtypeStruct((twiddles.shape[1], *own.shape), own.dtype)
        out_spec = pl.BlockSpec((None, tile, laws, width), lambda i, o: (target, i, 0, 0))
        if whole is not None:
            args.append(whole)
            in_specs.append(pl.BlockSpec(memory_space=pl.ANY))
            aliases = {5: 0}
    return call(
        functools.partial(level_kernel, bit),
        out_shape,
        (slots // tile,),
        in_specs,
        out_spec,
        args,
        order,
        scratch=[pltpu.VMEM((2 * width, 2 * width), own.dtype)],
        aliases=aliases,
        flops=8 * slots * laws * width * width,
        nbytes=6 * slots * laws * width,
    )


PLANE = (0, THIRD, FIRST, FIRST | THIRD)


def pack_kernel(order, w, t, out):
    targets, slots, laws, width = w.shape
    rows = slots * laws
    for target in range(targets):
        block = twist_16(w[target].reshape(rows, width), t[0, target])
        out[0, target * rows : (target + 1) * rows, :] = block.astype(out.dtype)
        for later in range(2):
            start = targets * rows + (later * targets + target) * slots
            out[0, start : start + slots, :] = t[1 + later, target].astype(out.dtype)


def pack(order, weights, twiddles, far):
    _, slots, laws, width = weights.shape
    eighth = slots // 8
    rows = GATHERED * eighth * (laws + 2)

    def which(i, o):
        return o[lax.div(i, 2) * FIRST + lax.rem(i, 2) * THIRD + far]

    return call(
        pack_kernel,
        jax.ShapeDtypeStruct((4, rows, width), weights.dtype),
        (4,),
        [
            pl.BlockSpec((GATHERED, eighth, laws, width), lambda i, o: (0, which(i, o), 0, 0)),
            pl.BlockSpec((3, GATHERED, eighth, width), lambda i, o: (0, 0, which(i, o), 0)),
        ],
        pl.BlockSpec((1, rows, width), lambda i, o: (i, 0, 0)),
        (weights, twiddles),
        order,
        nbytes=16 * rows * width,
    )


def pair_kernel(order, near, far, *rest):
    outs = rest[-3:]
    for i, out in enumerate(outs):
        out[0] = near[i + 1]
        out[1] = far[i + 1]


def pair_up(order, near, far, after):
    _, rows, width = near.shape
    whole = pl.BlockSpec((4, rows, width), lambda i, o: (0, 0, 0))
    return call(
        pair_kernel,
        [jax.ShapeDtypeStruct((2, rows, width), near.dtype)] * 3,
        (1,),
        [whole, whole, *[pl.BlockSpec(memory_space=pl.ANY)] * len(after)],
        [pl.BlockSpec((2, rows, width), lambda i, o: (0, 0, 0))] * 3,
        (near, far, *after),
        order,
        nbytes=24 * rows * width,
    )


def gathered_kernel(laws, order, near, far, one, two, three, maps, *rest):
    *_, out_0, out_1, out_2, out_3, both = rest
    width = maps.shape[-1]
    outs = (out_0, out_1, out_2, out_3)
    slots = near.shape[1] // (laws + 2)
    for index, bit in enumerate((FIRST, SECOND, THIRD)):
        child = lax.div(order[0], bit) & 1
        for source in range(2):
            for goal in range(2):
                part = maps[index, child ^ goal, child ^ source]
                turned = roll_half(part.astype(jnp.float32)).astype(part.dtype)
                at = slice(source * width, (source + 1) * width)
                both[index, at, goal * width : (goal + 1) * width] = part
                both[index, at, (2 + goal) * width : (3 + goal) * width] = turned

    def piece(place, start, size):
        at = pl.ds(pl.multiple_of(start, 16), size)
        plane = PLANE.index(place & (FIRST | THIRD))
        if plane == 0:
            return (far if place & SECOND else near)[0, at, :]
        return (one, two, three)[plane - 1][1 if place & SECOND else 0, at, :]

    step_slots = 16

    def step(i, carry):
        rows = step_slots * laws
        values = [piece(place, i * rows, rows) for place in range(8)]
        for index, bit in enumerate((FIRST, SECOND, THIRD)):
            for place in range(8):
                if place & bit:
                    continue
                joint = jnp.concatenate([values[place], values[place | bit]], axis=1)
                state = jnp.dot(joint, both[index], preferred_element_type=jnp.float32)
                for goal in range(2):
                    mine = place | bit if goal else place
                    plain = state[:, goal * width : (goal + 1) * width]
                    if index < 2:
                        turned = state[:, (2 + goal) * width : (3 + goal) * width]
                        start = slots * laws + index * slots + i * step_slots
                        factors = piece(mine, start, step_slots).astype(jnp.float32)
                        values[mine] = twist(plain, turned, factors).astype(jnp.bfloat16)
                    else:
                        out = outs[PLANE.index(mine & (FIRST | THIRD))]
                        at = pl.ds(pl.multiple_of(i * rows, 16), rows)
                        out[1 if mine & SECOND else 0, at, :] = plain.astype(out.dtype)
        return carry

    lax.fori_loop(0, slots // step_slots, step, 0)


def gathered_levels(order, near, far, received, kernels, laws, after):
    _, rows, width = near.shape
    full = rows // (laws + 2) * laws
    first = pl.BlockSpec((1, rows, width), lambda i, o: (0, 0, 0))
    pair = pl.BlockSpec((2, rows, width), lambda i, o: (0, 0, 0))
    return call(
        functools.partial(gathered_kernel, laws),
        [jax.ShapeDtypeStruct((2, full, width), near.dtype)] * 4,
        (1,),
        [
            *(first, first, pair, pair, pair),
            pl.BlockSpec(kernels.shape, lambda i, o: (0, 0, 0, 0, 0)),
            *[pl.BlockSpec(memory_space=pl.ANY)] * len(after),
        ],
        [pl.BlockSpec((2, full, width), lambda i, o: (0, 0, 0))] * 4,
        (near, far, *received, kernels, *after),
        order,
        scratch=[pltpu.VMEM((3, 2 * width, 4 * width), near.dtype)],
        flops=3 * 8 * full * 4 * width * width,
        nbytes=32 * full * width,
    )


def far_kernel(order, a, b, c, d, out):
    for i, block in enumerate((a, b, c, d)):
        out[i] = block[0]


def far_part(order, blocks):
    _, rows, width = blocks[0].shape
    return call(
        far_kernel,
        jax.ShapeDtypeStruct((4, rows, width), blocks[0].dtype),
        (1,),
        [pl.BlockSpec((1, rows, width), lambda i, o: (1, 0, 0))] * 4,
        pl.BlockSpec((4, rows, width), lambda i, o: (0, 0, 0)),
        blocks,
        order,
        nbytes=16 * rows * width,
    )


def unpack_kernel(order, *refs):
    *blocks, t, _, out = refs
    targets, slots, laws, width = out.shape
    rows = slots * laws

    def write(block):
        for target in range(targets):
            state = block[0, target * rows : (target + 1) * rows, :]
            out[target] = twist_16(state, t[0, target]).astype(out.dtype).reshape(out.shape[1:])

    if len(blocks) == 1:
        write(blocks[0])
    else:
        for i, block in enumerate(blocks):
            pl.when(pl.program_id(0) == i)(functools.partial(write, block))


def unpack(order, blocks, twiddles, whole, far):
    _, slots, laws, width = whole.shape
    eighth = slots // 8
    rows = GATHERED * eighth * laws

    def which(i, o):
        return o[lax.div(i, 2) * FIRST + lax.rem(i, 2) * THIRD + far]

    if len(blocks) == 1:
        block_specs = [pl.BlockSpec((1, rows, width), lambda i, o: (i, 0, 0))]
    else:
        block_specs = [pl.BlockSpec((1, rows, width), lambda i, o: (0, 0, 0))] * 4
    return call(
        unpack_kernel,
        jax.ShapeDtypeStruct(whole.shape, whole.dtype),
        (4,),
        [
            *block_specs,
            pl.BlockSpec((1, GATHERED, eighth, width), lambda i, o: (3, 0, which(i, o), 0)),
            pl.BlockSpec(memory_space=pl.ANY),
        ],
        pl.BlockSpec((GATHERED, eighth, laws, width), lambda i, o: (0, which(i, o), 0, 0)),
        (*blocks, twiddles, whole),
        order,
        aliases={len(blocks) + 2: 0},
        nbytes=16 * rows * width,
    )


def body(weights_in, twiddles, kernels):
    targets, _, laws, _ = weights_in.shape
    order = my_order()
    far_send = pack(order, weights_in, twiddles, SECOND)
    far = swap(far_send, SECOND)
    near = pack(order, weights_in, twiddles, 0)
    swapped = list(range(GATHERED, targets))
    state = {}
    for target in swapped:
        own = first_twist(order, weights_in, twiddles, target, far_send)
        state[target] = own, swap(own, FIRST)
    for target in swapped:
        own = level(order, *state[target], kernels, twiddles, 0, FIRST, target)
        state[target] = own, swap(own, SECOND)
    pairs = pair_up(order, near, far, [state[target][0] for target in swapped])
    received = [swap(pair, place) for pair, place in zip(pairs, PLANE[1:])]
    for target in swapped:
        own = level(order, *state[target], kernels, twiddles, 1, SECOND, target)
        state[target] = own, swap(own, THIRD)
    done = gathered_levels(order, near, far, received, kernels, laws, [state[swapped[0]][0]])
    back = [done[0], *[swap(block, place) for block, place in zip(done[1:], PLANE[1:])]]
    far_back = swap(far_part(order, back), SECOND)
    whole = None
    for target in swapped:
        whole = level(order, *state[target], kernels, twiddles, 2, THIRD, target, whole, True)
    whole = unpack(order, back, twiddles, whole, 0)
    return unpack(order, [far_back], twiddles, whole, SECOND)


def solution(mesh):
    return jax.shard_map(
        body,
        mesh=mesh,
        in_specs=(P(None, ("src", "tgt"), None, None), P(None, None, ("src", "tgt"), None), P()),
        out_specs=P(None, ("src", "tgt"), None, None),
        check_vma=False,
    )
```

time: 421 us -> 218 us (0.52)
  waiting for transfers between devices: 345 us -> 139 us
  Pallas kernels: 0 us -> 40.6 us
  other arithmetic: 30.4 us -> 0.01 us
  matrix products: 27.6 us -> 0 us
  starting transfers between devices: 9.91 us -> 36.8 us
  local copies, waits for them, and re-layouts: 7.62 us -> 1.25 us
    ppermute x3 -> x14, waiting for transfers between devices: 345 us -> 139 us  [the longest x8 105 us: swap(): return lax.ppermute(block, 'src', [(i, i ^ flip_src) for i in range(n_src)])]
    pallas_call x0 -> x15, Pallas kernels: none -> 40.6 us  [call(): pl.pallas_call(kernel, out_shape=out_shape, grid_spec=pltpu.PrefetchScala...]
    dot_general x6 -> x0, matrix products: 27.6 us -> none  [the longest x3 17.4 us: apply_pair(): jnp.dot(own_slots.reshape(-1, width), level_kernels[child_bit, child_bit]...]
    ppermute x3 -> x14, starting transfers between devices: 9.91 us -> 36.8 us  [the longest x8 23.3 us: swap(): return lax.ppermute(block, 'src', [(i, i ^ flip_src) for i in range(n_src)])]
    another operation x4 -> x0, other arithmetic: 15.7 us -> none
    concatenate x4 -> x0, other arithmetic: 14.7 us -> none  [rotate_phase(): jnp.concatenate([cosine * real_part - sine_part * imag_part, sine_part *...]
    unnamed x14 -> x10, local copies, waits for them, and re-layouts: 5.81 us -> 1.25 us
  transfers between devices with their start and end apart: 3 -> 14, of which waited for: 3 -> 9; matrix products, arithmetic and copies ran while one was open for 4% -> 0% of each run, Pallas kernels for 0% -> 14%
where the time goes in v1:
time: 218 us
  waiting for transfers between devices  139 us (64%)
  Pallas kernels  40.6 us (19%)
  starting transfers between devices  36.8 us (17%)
    ppermute x8, waiting for transfers between devices, swap(): return lax.ppermute(block, 'src', [(i, i ^ flip_src) for i in range(n_src)])  105 us
    pallas_call x15, Pallas kernels, call(): pl.pallas_call(kernel, out_shape=out_shape, grid_spec=pltpu.PrefetchScala...  40.6 us
    ppermute x4, waiting for transfers between devices, swap(): return lax.ppermute(block, 'tgt', [(i, i ^ flip_tgt) for i in range(n_tgt)])  33.6 us
    ppermute x8, starting transfers between devices, swap(): return lax.ppermute(block, 'src', [(i, i ^ flip_src) for i in range(n_src)])  23.3 us
    ppermute x4, starting transfers between devices, swap(): return lax.ppermute(block, 'tgt', [(i, i ^ flip_tgt) for i in range(n_tgt)])  11.3 us
  transfers between devices with their start and end apart: 14, of which 9 were waited for; matrix products, arithmetic and copies ran while one was open for 0% of the time, Pallas kernels for 14%

profile of v1, /device:TPU:80, one launch (start us, length us, event | category | flops | bytes accessed | tf_op | source)
XLA Modules:
  0.0 217.8 jit_solution(6247439833391106345)
XLA Ops:
  0.0 1.2 copy-done
  1.2 3.2 %shard_map.38._ = bf16[4,1088,128]{2,1,0:T(8,128)(2,1)S(1)} custom-call(s32[8]{0:T(128)S(1)} %iota_xor_fusion.order, bf16[4,128,32,128]{3,2,1,0:T(8,128)(2,1)} %w.7, f32[4,4,128,128]{3,2,1,0:T(8,128)S(1)} %copy-done), custom_call_target="tpu_custom_call" | custom-call | bytes 2228224 | tf_op jit(solution)/shard_map/pallas_call | solution.py:59
  4.5 3.2 %shard_map.39.own = bf16[128,32,128]{2,1,0:T(8,128)(2,1)S(1)} custom-call(s32[8]{0:T(128)S(1)} %iota_xor_fusion.order, bf16[4,128,32,128]{3,2,1,0:T(8,128)(2,1)} %w.7, f32[4,4,128,128]{3,2,1,0:T(8,128)S(1)} %copy-done, bf16[4,1088,128]{2,1,0:T(8,128)(2,1)S(1)} %shard_map.38._), custom_call_target="tpu_custom_call" | custom-call | bytes 2097152 | tf_op jit(solution)/shard_map/pallas_call | solution.py:59
  7.7 1.6 collective-permute-start.1
  9.3 5.4 %collective-permute-start = (bf16[4,1088,128]{2,1,0:T(8,128)(2,1)S(1)}, bf16[4,1088,128]{2,1,0:T(8,128)(2,1)S(1)}, u32[]{:S(2)}, u32[]{:S(2)}) collective-permute-start(bf16[4,1088,128]{2,1,0:T(8,128)(2,1)S(1)} %shard_map.38._), channel_id=1, source_target_pairs={{0,64},{8,72},{16,80},{24,88},{32,96},{40,104},{48,112},{56,120},{... | collective-permute-start | bytes 3342344 | tf_op jit(solution)/shard_map/ppermute | solution.py:21
  14.7 3.2 %shard_map.41.own = bf16[128,32,128]{2,1,0:T(8,128)(2,1)S(1)} custom-call(s32[8]{0:T(128)S(1)} %iota_xor_fusion.order, bf16[4,128,32,128]{3,2,1,0:T(8,128)(2,1)} %w.7, f32[4,4,128,128]{3,2,1,0:T(8,128)S(1)} %copy-done, bf16[4,1088,128]{2,1,0:T(8,128)(2,1)S(1)} %shard_map.38._), custom_call_target="tpu_custom_call" | custom-call | bytes 2097152 | tf_op jit(solution)/shard_map/pallas_call | solution.py:59
  18.5 15.3 %collective-permute-done.1.other = bf16[128,32,128]{2,1,0:T(8,128)(2,1)S(1)} collective-permute-done((bf16[128,32,128]{2,1,0:T(8,128)(2,1)S(1)}, bf16[128,32,128]{2,1,0:T(8,128)(2,1)S(1)}, u32[]{:S(2)}, u32[]{:S(2)}) %collective-permute-start.1) | collective-permute-done | bytes 1048608 | tf_op jit(solution)/shard_map/ppermute | solution.py:21
  33.8 2.4 %shard_map.40.rest_0_.own = bf16[128,32,128]{2,1,0:T(8,128)(2,1)S(1)} custom-call(s32[8]{0:T(128)S(1)} %iota_xor_fusion.order, bf16[128,32,128]{2,1,0:T(8,128)(2,1)S(1)} %shard_map.39.own, bf16[128,32,128]{2,1,0:T(8,128)(2,1)S(1)} %collective-permute-done.1.other, bf16[3,2,2,128,128]{4,3,2,1,0:T(8,128)(2,1)S(1)} %copy-done.2, f32[4,4,128,128]{3,2,1,0:T(8,128)S(1)} %copy-done), custom_call_target="tpu_custom_call" | custom-call | flops 536870912 | bytes 3145728 | tf_op jit(solution)/shard_map/pallas_call | solution.py:59
  36.2 5.5 %collective-permute-start.6 = (bf16[128,32,128]{2,1,0:T(8,128)(2,1)S(1)}, bf16[128,32,128]{2,1,0:T(8,128)(2,1)S(1)}, u32[]{:S(2)}, u32[]{:S(2)}) collective-permute-start(bf16[128,32,128]{2,1,0:T(8,128)(2,1)S(1)} %shard_map.40.rest_0_.own), channel_id=1, source_target_pairs={{0,64},{8,72},{16,80},{24,88},{32,96},{40,104},{48,112},{56,120},{... | collective-permute-start | bytes 3145736 | tf_op jit(solution)/shard_map/ppermute | solution.py:21
  41.7 3.2 %shard_map.37.near = bf16[4,1088,128]{2,1,0:T(8,128)(2,1)S(1)} custom-call(s32[8]{0:T(128)S(1)} %iota_xor_fusion.order, bf16[4,128,32,128]{3,2,1,0:T(8,128)(2,1)} %w.7, f32[4,4,128,128]{3,2,1,0:T(8,128)S(1)} %copy-done), custom_call_target="tpu_custom_call" | custom-call | bytes 2228224 | tf_op jit(solution)/shard_map/pallas_call | solution.py:59
  45.0 10.2 %collective-permute-done.2.other = bf16[128,32,128]{2,1,0:T(8,128)(2,1)S(1)} collective-permute-done((bf16[128,32,128]{2,1,0:T(8,128)(2,1)S(1)}, bf16[128,32,128]{2,1,0:T(8,128)(2,1)S(1)}, u32[]{:S(2)}, u32[]{:S(2)}) %collective-permute-start.2) | collective-permute-done | bytes 1048608 | tf_op jit(solution)/shard_map/ppermute | solution.py:21
  55.2 2.4 %shard_map.42.rest_1_.own = bf16[128,32,128]{2,1,0:T(8,128)(2,1)S(1)} custom-call(s32[8]{0:T(128)S(1)} %iota_xor_fusion.order, bf16[128,32,128]{2,1,0:T(8,128)(2,1)S(1)} %shard_map.41.own, bf16[128,32,128]{2,1,0:T(8,128)(2,1)S(1)} %collective-permute-done.2.other, bf16[3,2,2,128,128]{4,3,2,1,0:T(8,128)(2,1)S(1)} %copy-done.2, f32[4,4,128,128]{3,2,1,0:T(8,128)S(1)} %copy-done), custom_call_target="tpu_custom_call" | custom-call | flops 536870912 | bytes 3145728 | tf_op jit(solution)/shard_map/pallas_call | solution.py:59
  57.5 37.7 %collective-permute-done.far = bf16[4,1088,128]{2,1,0:T(8,128)(2,1)S(1)} collective-permute-done((bf16[4,1088,128]{2,1,0:T(8,128)(2,1)S(1)}, bf16[4,1088,128]{2,1,0:T(8,128)(2,1)S(1)}, u32[]{:S(2)}, u32[]{:S(2)}) %collective-permute-start) | collective-permute-done | bytes 1114144 | tf_op jit(solution)/shard_map/ppermute | solution.py:21
  95.9 2.8 %collective-permute-start.3 = (bf16[2,1088,128]{2,1,0:T(8,128)(2,1)S(1)}, bf16[2,1088,128]{2,1,0:T(8,128)(2,1)S(1)}, u32[]{:S(2)}, u32[]{:S(2)}) collective-permute-start(bf16[2,1088,128]{2,1,0:T(8,128)(2,1)S(1)} %get-tuple-element.12), channel_id=1, source_target_pairs={{0,4},{1,5},{2,6},{3,7},{4,0},{5,1},{6,2},{7,3},{8,12},{9,13},{10,... | collective-permute-start | bytes 1671176 | tf_op jit(solution)/shard_map/ppermute | solution.py:23
  98.9 1.1 collective-permute-start.5
  100.1 5.0 %collective-permute-start.11 = (bf16[128,32,128]{2,1,0:T(8,128)(2,1)S(1)}, bf16[128,32,128]{2,1,0:T(8,128)(2,1)S(1)}, u32[]{:S(2)}, u32[]{:S(2)}) collective-permute-start(bf16[128,32,128]{2,1,0:T(8,128)(2,1)S(1)} %shard_map.42.rest_1_.own), channel_id=1, source_target_pairs={{0,64},{8,72},{16,80},{24,88},{32,96},{40,104},{48,112},{56,120},{... | collective-permute-start | bytes 3145736 | tf_op jit(solution)/shard_map/ppermute | solution.py:21
  105.1 26.6 %collective-permute-done.6.other = bf16[128,32,128]{2,1,0:T(8,128)(2,1)S(1)} collective-permute-done((bf16[128,32,128]{2,1,0:T(8,128)(2,1)S(1)}, bf16[128,32,128]{2,1,0:T(8,128)(2,1)S(1)}, u32[]{:S(2)}, u32[]{:S(2)}) %collective-permute-start.6) | collective-permute-done | bytes 1048608 | tf_op jit(solution)/shard_map/ppermute | solution.py:21
  131.7 2.4 %shard_map.44.rest_0_.own = bf16[128,32,128]{2,1,0:T(8,128)(2,1)S(1)} custom-call(s32[8]{0:T(128)S(1)} %iota_xor_fusion.order, bf16[128,32,128]{2,1,0:T(8,128)(2,1)S(1)} %shard_map.40.rest_0_.own, bf16[128,32,128]{2,1,0:T(8,128)(2,1)S(1)} %collective-permute-done.6.other, bf16[3,2,2,128,128]{4,3,2,1,0:T(8,128)(2,1)S(1)} %copy-done.2, ...), custom_call_target="tpu_custom_call" | custom-call | flops 536870912 | bytes 3145728 | tf_op jit(solution)/shard_map/pallas_call | solution.py:59
  134.1 4.9 %shard_map.45 = (bf16[2,1024,128]{2,1,0:T(8,128)(2,1)S(1)}, bf16[2,1024,128]{2,1,0:T(8,128)(2,1)S(1)}, bf16[2,1024,128]{2,1,0:T(8,128)(2,1)S(1)}, bf16[2,1024,128]{2,1,0:T(8,128)(2,1)S(1)}) custom-call(s32[8]{0:T(128)S(1)} %iota_xor_fusion.order, bf16[4,1088,128]{2,1,0:T(8,128)(2,1)} %copy-done.3, bf16[4,1088,128]{2,1,0:T(8,128)(2,1)} %copy-done.4, ...), custom_call_target="tpu_custom_call" | custom-call | flops 1610612736 | bytes 4194304 | tf_op jit(solution)/shard_map/pallas_call | solution.py:59
  138.9 2.9 %collective-permute-start.7 = (bf16[2,1024,128]{2,1,0:T(8,128)(2,1)S(1)}, bf16[2,1024,128]{2,1,0:T(8,128)(2,1)S(1)}, u32[]{:S(2)}, u32[]{:S(2)}) collective-permute-start(bf16[2,1024,128]{2,1,0:T(8,128)(2,1)S(1)} %get-tuple-element.16), channel_id=1, source_target_pairs={{0,4},{1,5},{2,6},{3,7},{4,0},{5,1},{6,2},{7,3},{8,12},{9,13},{10,... | collective-permute-start | bytes 1572872 | tf_op jit(solution)/shard_map/ppermute | solution.py:23
  143.1 2.8 %collective-permute-start.13 = (bf16[128,32,128]{2,1,0:T(8,128)(2,1)S(1)}, bf16[128,32,128]{2,1,0:T(8,128)(2,1)S(1)}, u32[]{:S(2)}, u32[]{:S(2)}) collective-permute-start(bf16[128,32,128]{2,1,0:T(8,128)(2,1)S(1)} %shard_map.44.rest_0_.own), channel_id=1, source_target_pairs={{0,4},{1,5},{2,6},{3,7},{4,0},{5,1},{6,2},{7,3},{8,12},{9,13},{10,... | collective-permute-start | bytes 3145736 | tf_op jit(solution)/shard_map/ppermute | solution.py:23
  145.9 7.5 %collective-permute-done.11.other = bf16[128,32,128]{2,1,0:T(8,128)(2,1)S(1)} collective-permute-done((bf16[128,32,128]{2,1,0:T(8,128)(2,1)S(1)}, bf16[128,32,128]{2,1,0:T(8,128)(2,1)S(1)}, u32[]{:S(2)}, u32[]{:S(2)}) %collective-permute-start.11) | collective-permute-done | bytes 1048608 | tf_op jit(solution)/shard_map/ppermute | solution.py:21
  153.4 2.4 %shard_map.47.own = bf16[128,32,128]{2,1,0:T(8,128)(2,1)S(1)} custom-call(s32[8]{0:T(128)S(1)} %iota_xor_fusion.order, bf16[128,32,128]{2,1,0:T(8,128)(2,1)S(1)} %shard_map.42.rest_1_.own, bf16[128,32,128]{2,1,0:T(8,128)(2,1)S(1)} %collective-permute-done.11.other, bf16[3,2,2,128,128]{4,3,2,1,0:T(8,128)(2,1)S(1)} %copy-done.2, f32[4,4,128,128]{3,2,1,0:T(8,128)S(1)} %copy-done.1), custom_call_target="tpu_custom_call" | custom-call | flops 536870912 | bytes 3145728 | tf_op jit(solution)/shard_map/pallas_call | solution.py:59
  155.8 2.8 %collective-permute-start.12 = (bf16[128,32,128]{2,1,0:T(8,128)(2,1)S(1)}, bf16[128,32,128]{2,1,0:T(8,128)(2,1)S(1)}, u32[]{:S(2)}, u32[]{:S(2)}) collective-permute-start(bf16[128,32,128]{2,1,0:T(8,128)(2,1)S(1)} %shard_map.47.own), channel_id=1, source_target_pairs={{0,4},{1,5},{2,6},{3,7},{4,0},{5,1},{6,2},{7,3},{8,12},{9,13},{10,... | collective-permute-start | bytes 3145736 | tf_op jit(solution)/shard_map/ppermute | solution.py:23
  158.6 7.5 %collective-permute-done.8.c.refs_2_ = bf16[2,1024,128]{2,1,0:T(8,128)(2,1)S(1)} collective-permute-done((bf16[2,1024,128]{2,1,0:T(8,128)(2,1)S(1)}, bf16[2,1024,128]{2,1,0:T(8,128)(2,1)S(1)}, u32[]{:S(2)}, u32[]{:S(2)}) %collective-permute-start.8) | collective-permute-done | bytes 524320 | tf_op jit(solution)/shard_map/ppermute | solution.py:21
  167.2 4.8 %collective-permute-start.10 = (bf16[4,1024,128]{2,1,0:T(8,128)(2,1)S(1)}, bf16[4,1024,128]{2,1,0:T(8,128)(2,1)S(1)}, u32[]{:S(2)}, u32[]{:S(2)}) collective-permute-start(bf16[4,1024,128]{2,1,0:T(8,128)(2,1)S(1)} %shard_map.46), channel_id=1, source_target_pairs={{0,64},{8,72},{16,80},{24,88},{32,96},{40,104},{48,112},{56,120},{... | collective-permute-start | bytes 3145736 | tf_op jit(solution)/shard_map/ppermute | solution.py:21
  172.0 17.1 %collective-permute-done.13.other = bf16[128,32,128]{2,1,0:T(8,128)(2,1)S(1)} collective-permute-done((bf16[128,32,128]{2,1,0:T(8,128)(2,1)S(1)}, bf16[128,32,128]{2,1,0:T(8,128)(2,1)S(1)}, u32[]{:S(2)}, u32[]{:S(2)}) %collective-permute-start.13) | collective-permute-done | bytes 1048608 | tf_op jit(solution)/shard_map/ppermute | solution.py:23
  189.1 3.3 %shard_map.48.rest_0_ = bf16[4,128,32,128]{3,2,1,0:T(8,128)(2,1)} custom-call(s32[8]{0:T(128)S(1)} %iota_xor_fusion.order, bf16[128,32,128]{2,1,0:T(8,128)(2,1)S(1)} %shard_map.44.rest_0_.own, bf16[128,32,128]{2,1,0:T(8,128)(2,1)S(1)} %collective-permute-done.13.other, bf16[3,2,2,128,128]{4,3,2,1,0:T(8,128)(2,1)S(1)} %copy-done.2, ...), custom_call_target="tpu_custom_call" | custom-call | flops 536870912 | bytes 3145728 | tf_op jit(solution)/shard_map/pallas_call | solution.py:59
  192.5 16.5 %collective-permute-done.12.other = bf16[128,32,128]{2,1,0:T(8,128)(2,1)S(1)} collective-permute-done((bf16[128,32,128]{2,1,0:T(8,128)(2,1)S(1)}, bf16[128,32,128]{2,1,0:T(8,128)(2,1)S(1)}, u32[]{:S(2)}, u32[]{:S(2)}) %collective-permute-start.12) | collective-permute-done | bytes 1048608 | tf_op jit(solution)/shard_map/ppermute | solution.py:23
  209.0 3.3 %shard_map.49.refs_5_ = bf16[4,128,32,128]{3,2,1,0:T(8,128)(2,1)} custom-call(s32[8]{0:T(128)S(1)} %iota_xor_fusion.order, bf16[128,32,128]{2,1,0:T(8,128)(2,1)S(1)} %shard_map.47.own, bf16[128,32,128]{2,1,0:T(8,128)(2,1)S(1)} %collective-permute-done.12.other, bf16[3,2,2,128,128]{4,3,2,1,0:T(8,128)(2,1)S(1)} %copy-done.2, ...), custom_call_target="tpu_custom_call", output_to_operand_aliasing={{}: (5, {})} | custom-call | flops 536870912 | bytes 3145728 | tf_op jit(solution)/shard_map/pallas_call | solution.py:59
  212.3 2.8 %shard_map.50.refs_2_ = bf16[4,128,32,128]{3,2,1,0:T(8,128)(2,1)} custom-call(s32[8]{0:T(128)S(1)} %iota_xor_fusion.order, bf16[2,1024,128]{2,1,0:T(8,128)(2,1)S(1)} %get-tuple-element.15.a.refs_0_, bf16[2,1024,128]{2,1,0:T(8,128)(2,1)S(1)} %collective-permute-done.7.b.refs_1_, ...), custom_call_target="tpu_custom_call", output_to_operand_aliasing={{}: (6, {})} | custom-call | bytes 2097152 | tf_op jit(solution)/shard_map/pallas_call | solution.py:59
  215.1 2.7 %shard_map.51 = bf16[4,128,32,128]{3,2,1,0:T(8,128)(2,1)} custom-call(s32[8]{0:T(128)S(1)} %iota_xor_fusion.order, bf16[4,1024,128]{2,1,0:T(8,128)(2,1)S(1)} %collective-permute-done.10.refs_0_, f32[4,4,128,128]{3,2,1,0:T(8,128)S(1)} %copy-done.1, bf16[4,128,32,128]{3,2,1,0:T(8,128)(2,1)} %shard_map.50.refs_2_), custom_call_target="tpu_custom_call", output_to_operand_aliasing={{}: (3, {})} | custom-call | bytes 2097152 | tf_op jit(solution)/shard_map/pallas_call | solution.py:59
  (22 shorter events, 3.9 us)
Async XLA Ops:
  0.0 1.2 copy-start
  7.7 26.1 %copy-start.2 = (bf16[3,2,2,128,128]{4,3,2,1,0:T(8,128)(2,1)S(1)}, bf16[3,2,2,128,128]{4,3,2,1,0:T(8,128)(2,1)}, u32[]{:S(2)}) copy-start(bf16[3,2,2,128,128]{4,3,2,1,0:T(8,128)(2,1)} %maps.13) | copy-start | bytes 1179652
  7.7 26.1 %collective-permute-start.1 = (bf16[128,32,128]{2,1,0:T(8,128)(2,1)S(1)}, bf16[128,32,128]{2,1,0:T(8,128)(2,1)S(1)}, u32[]{:S(2)}, u32[]{:S(2)}) collective-permute-start(bf16[128,32,128]{2,1,0:T(8,128)(2,1)S(1)} %shard_map.39.own), channel_id=1, source_target_pairs={{0,128},{8,136},{16,144},{24,152},{32,160},{40,168},{48,176},{56,1... | collective-permute-start | bytes 3145736 | tf_op jit(solution)/shard_map/ppermute | solution.py:21
  9.3 85.9 %collective-permute-start = (bf16[4,1088,128]{2,1,0:T(8,128)(2,1)S(1)}, bf16[4,1088,128]{2,1,0:T(8,128)(2,1)S(1)}, u32[]{:S(2)}, u32[]{:S(2)}) collective-permute-start(bf16[4,1088,128]{2,1,0:T(8,128)(2,1)S(1)} %shard_map.38._), channel_id=1, source_target_pairs={{0,64},{8,72},{16,80},{24,88},{32,96},{40,104},{48,112},{56,120},{... | collective-permute-start | bytes 3342344 | tf_op jit(solution)/shard_map/ppermute | solution.py:21
  17.9 37.3 %collective-permute-start.2 = (bf16[128,32,128]{2,1,0:T(8,128)(2,1)S(1)}, bf16[128,32,128]{2,1,0:T(8,128)(2,1)S(1)}, u32[]{:S(2)}, u32[]{:S(2)}) collective-permute-start(bf16[128,32,128]{2,1,0:T(8,128)(2,1)S(1)} %shard_map.41.own), channel_id=1, source_target_pairs={{0,128},{8,136},{16,144},{24,152},{32,160},{40,168},{48,176},{56,1... | collective-permute-start | bytes 3145736 | tf_op jit(solution)/shard_map/ppermute | solution.py:21
  36.2 95.4 %collective-permute-start.6 = (bf16[128,32,128]{2,1,0:T(8,128)(2,1)S(1)}, bf16[128,32,128]{2,1,0:T(8,128)(2,1)S(1)}, u32[]{:S(2)}, u32[]{:S(2)}) collective-permute-start(bf16[128,32,128]{2,1,0:T(8,128)(2,1)S(1)} %shard_map.40.rest_0_.own), channel_id=1, source_target_pairs={{0,64},{8,72},{16,80},{24,88},{32,96},{40,104},{48,112},{56,120},{... | collective-permute-start | bytes 3145736 | tf_op jit(solution)/shard_map/ppermute | solution.py:21
  44.9 50.9 %copy-start.3 = (bf16[4,1088,128]{2,1,0:T(8,128)(2,1)}, bf16[4,1088,128]{2,1,0:T(8,128)(2,1)S(1)}, u32[]{:S(2)}) copy-start(bf16[4,1088,128]{2,1,0:T(8,128)(2,1)S(1)} %shard_map.37.near) | copy-start | bytes 3342340
  45.0 86.7 %copy-start.1 = (f32[4,4,128,128]{3,2,1,0:T(8,128)S(1)}, f32[4,4,128,128]{3,2,1,0:T(8,128)}, u32[]{:S(2)}) copy-start(f32[4,4,128,128]{3,2,1,0:T(8,128)} %refs_1_.1) | copy-start | bytes 3145732
  95.2 38.8 %copy-start.4 = (bf16[4,1088,128]{2,1,0:T(8,128)(2,1)}, bf16[4,1088,128]{2,1,0:T(8,128)(2,1)S(1)}, u32[]{:S(2)}) copy-start(bf16[4,1088,128]{2,1,0:T(8,128)(2,1)S(1)} %collective-permute-done.far) | copy-start | bytes 3342340
  95.9 38.2 %collective-permute-start.3 = (bf16[2,1088,128]{2,1,0:T(8,128)(2,1)S(1)}, bf16[2,1088,128]{2,1,0:T(8,128)(2,1)S(1)}, u32[]{:S(2)}, u32[]{:S(2)}) collective-permute-start(bf16[2,1088,128]{2,1,0:T(8,128)(2,1)S(1)} %get-tuple-element.12), channel_id=1, source_target_pairs={{0,4},{1,5},{2,6},{3,7},{4,0},{5,1},{6,2},{7,3},{8,12},{9,13},{10,... | collective-permute-start | bytes 1671176 | tf_op jit(solution)/shard_map/ppermute | solution.py:23
  98.7 35.4 %collective-permute-start.4 = (bf16[2,1088,128]{2,1,0:T(8,128)(2,1)S(1)}, bf16[2,1088,128]{2,1,0:T(8,128)(2,1)S(1)}, u32[]{:S(2)}, u32[]{:S(2)}) collective-permute-start(bf16[2,1088,128]{2,1,0:T(8,128)(2,1)S(1)} %get-tuple-element.13), channel_id=1, source_target_pairs={{0,128},{8,136},{16,144},{24,152},{32,160},{40,168},{48,176},{56,1... | collective-permute-start | bytes 1671176 | tf_op jit(solution)/shard_map/ppermute | solution.py:21
  98.9 35.1 %collective-permute-start.5 = (bf16[2,1088,128]{2,1,0:T(8,128)(2,1)S(1)}, bf16[2,1088,128]{2,1,0:T(8,128)(2,1)S(1)}, u32[]{:S(2)}, u32[]{:S(2)}) collective-permute-start(bf16[2,1088,128]{2,1,0:T(8,128)(2,1)S(1)} %get-tuple-element.14), channel_id=1, source_target_pairs={{0,132},{1,133},{2,134},{3,135},{4,128},{5,129},{6,130},{7,131},{8... | collective-permute-start | bytes 1671176 | tf_op jit(solution)/shard_map/ppermute | solution.py:28
  100.1 53.3 %collective-permute-start.11 = (bf16[128,32,128]{2,1,0:T(8,128)(2,1)S(1)}, bf16[128,32,128]{2,1,0:T(8,128)(2,1)S(1)}, u32[]{:S(2)}, u32[]{:S(2)}) collective-permute-start(bf16[128,32,128]{2,1,0:T(8,128)(2,1)S(1)} %shard_map.42.rest_1_.own), channel_id=1, source_target_pairs={{0,64},{8,72},{16,80},{24,88},{32,96},{40,104},{48,112},{56,120},{... | collective-permute-start | bytes 3145736 | tf_op jit(solution)/shard_map/ppermute | solution.py:21
  138.9 19.6 %collective-permute-start.7 = (bf16[2,1024,128]{2,1,0:T(8,128)(2,1)S(1)}, bf16[2,1024,128]{2,1,0:T(8,128)(2,1)S(1)}, u32[]{:S(2)}, u32[]{:S(2)}) collective-permute-start(bf16[2,1024,128]{2,1,0:T(8,128)(2,1)S(1)} %get-tuple-element.16), channel_id=1, source_target_pairs={{0,4},{1,5},{2,6},{3,7},{4,0},{5,1},{6,2},{7,3},{8,12},{9,13},{10,... | collective-permute-start | bytes 1572872 | tf_op jit(solution)/shard_map/ppermute | solution.py:23
  141.8 24.3 %collective-permute-start.8 = (bf16[2,1024,128]{2,1,0:T(8,128)(2,1)S(1)}, bf16[2,1024,128]{2,1,0:T(8,128)(2,1)S(1)}, u32[]{:S(2)}, u32[]{:S(2)}) collective-permute-start(bf16[2,1024,128]{2,1,0:T(8,128)(2,1)S(1)} %get-tuple-element.17), channel_id=1, source_target_pairs={{0,128},{8,136},{16,144},{24,152},{32,160},{40,168},{48,176},{56,1... | collective-permute-start | bytes 1572872 | tf_op jit(solution)/shard_map/ppermute | solution.py:21
  142.0 24.6 %collective-permute-start.9 = (bf16[2,1024,128]{2,1,0:T(8,128)(2,1)S(1)}, bf16[2,1024,128]{2,1,0:T(8,128)(2,1)S(1)}, u32[]{:S(2)}, u32[]{:S(2)}) collective-permute-start(bf16[2,1024,128]{2,1,0:T(8,128)(2,1)S(1)} %get-tuple-element.18), channel_id=1, source_target_pairs={{0,132},{1,133},{2,134},{3,135},{4,128},{5,129},{6,130},{7,131},{8... | collective-permute-start | bytes 1572872 | tf_op jit(solution)/shard_map/ppermute | solution.py:28
  143.1 46.0 %collective-permute-start.13 = (bf16[128,32,128]{2,1,0:T(8,128)(2,1)S(1)}, bf16[128,32,128]{2,1,0:T(8,128)(2,1)S(1)}, u32[]{:S(2)}, u32[]{:S(2)}) collective-permute-start(bf16[128,32,128]{2,1,0:T(8,128)(2,1)S(1)} %shard_map.44.rest_0_.own), channel_id=1, source_target_pairs={{0,4},{1,5},{2,6},{3,7},{4,0},{5,1},{6,2},{7,3},{8,12},{9,13},{10,... | collective-permute-start | bytes 3145736 | tf_op jit(solution)/shard_map/ppermute | solution.py:23
  155.8 53.2 %collective-permute-start.12 = (bf16[128,32,128]{2,1,0:T(8,128)(2,1)S(1)}, bf16[128,32,128]{2,1,0:T(8,128)(2,1)S(1)}, u32[]{:S(2)}, u32[]{:S(2)}) collective-permute-start(bf16[128,32,128]{2,1,0:T(8,128)(2,1)S(1)} %shard_map.47.own), channel_id=1, source_target_pairs={{0,4},{1,5},{2,6},{3,7},{4,0},{5,1},{6,2},{7,3},{8,12},{9,13},{10,... | collective-permute-start | bytes 3145736 | tf_op jit(solution)/shard_map/ppermute | solution.py:23
  167.2 47.9 %collective-permute-start.10 = (bf16[4,1024,128]{2,1,0:T(8,128)(2,1)S(1)}, bf16[4,1024,128]{2,1,0:T(8,128)(2,1)S(1)}, u32[]{:S(2)}, u32[]{:S(2)}) collective-permute-start(bf16[4,1024,128]{2,1,0:T(8,128)(2,1)S(1)} %shard_map.46), channel_id=1, source_target_pairs={{0,64},{8,72},{16,80},{24,88},{32,96},{40,104},{48,112},{56,120},{... | collective-permute-start | bytes 3145736 | tf_op jit(solution)/shard_map/ppermute | solution.py:21

commit v2 on v1

--- a/solution.py
+++ b/solution.py
@@ -9,7 +9,8 @@
 
 FIRST, SECOND, THIRD = 4, 2, 1
 GATHERED = 2
-TILE = 32
+PIECES = (2, 3, 3)
+COST = 4
 VMEM = 48 * 2**20
 
 
@@ -64,43 +65,54 @@
         ),
         input_output_aliases=aliases or {},
         compiler_params=pltpu.CompilerParams(vmem_limit_bytes=VMEM),
-        cost_estimate=pl.CostEstimate(flops=flops, bytes_accessed=nbytes, transcendentals=0),
+        cost_estimate=pl.CostEstimate(flops=COST * flops, bytes_accessed=COST * nbytes, transcendentals=0),
     )(order, *args)
+
+
+def pieces(targets, slots):
+    per_target = sum(PIECES) // (targets - GATHERED)
+    starts = [GATHERED * per_target + sum(PIECES[:i]) for i in range(len(PIECES))]
+    return [(start, count, per_target) for start, count in zip(starts, PIECES)]
+
+
+def spot(i, piece):
+    start, _, per_target = piece
+    return lax.div(start + i, per_target), lax.rem(start + i, per_target)
 
 
 def first_kernel(order, w, t, _, out):
     slots, laws, width = out.shape
-    out[...] = twist_16(w[0].reshape(slots * laws, width), t[0, 0]).astype(out.dtype).reshape(out.shape)
-
-
-def first_twist(order, weights, twiddles, target, after):
+    out[...] = twist_16(w[...].reshape(slots * laws, width), t[...]).astype(out.dtype).reshape(out.shape)
+
+
+def first_twist(order, weights, twiddles, piece, after):
     _, slots, laws, width = weights.shape
-    tile = min(TILE, slots)
+    tile, tiles = slots // piece[2], piece[1]
     return call(
         first_kernel,
-        jax.ShapeDtypeStruct((slots, laws, width), weights.dtype),
-        (slots // tile,),
+        jax.ShapeDtypeStruct((tiles * tile, laws, width), weights.dtype),
+        (tiles,),
         [
-            pl.BlockSpec((1, tile, laws, width), lambda i, o: (target, i, 0, 0)),
-            pl.BlockSpec((1, 1, tile, width), lambda i, o: (0, target, i, 0)),
+            pl.BlockSpec((None, tile, laws, width), lambda i, o: (*spot(i, piece), 0, 0)),
+            pl.BlockSpec((None, None, tile, width), lambda i, o: (0, *spot(i, piece), 0)),
             pl.BlockSpec(memory_space=pl.ANY),
         ],
         pl.BlockSpec((tile, laws, width), lambda i, o: (i, 0, 0)),
         (weights, twiddles, after),
         order,
-        nbytes=4 * slots * laws * width,
+        nbytes=4 * tiles * tile * laws * width,
     )
 
 
 def level_kernel(bit, order, own, other, maps, t, *rest):
-    out, both = rest[-2], rest[-1]
+    out, both = rest[-2:]
     slots, laws, width = own.shape
 
     @pl.when(pl.program_id(0) == 0)
     def _():
         child = lax.div(order[0], bit) & 1
         for source in range(2):
-            part = maps[0, child, child if source == 0 else 1 - child]
+            part = maps[child, child if source == 0 else 1 - child]
             both[source * width : (source + 1) * width, :width] = part
             turned = roll_half(part.astype(jnp.float32)).astype(part.dtype)
             both[source * width : (source + 1) * width, width:] = turned
@@ -108,32 +120,33 @@
     rows = slots * laws
     state = jnp.dot(own[...].reshape(rows, width), both[:width, :], preferred_element_type=jnp.float32)
     state += jnp.dot(other[...].reshape(rows, width), both[width:, :], preferred_element_type=jnp.float32)
-    out[...] = twist(state[:, :width], state[:, width:], t[0, 0]).astype(out.dtype).reshape(out.shape)
-
-
-def level(order, own, other, kernels, twiddles, index, bit, target, whole=None, last=False):
+    out[...] = twist(state[:, :width], state[:, width:], t[...]).astype(out.dtype).reshape(out.shape)
+
+
+def level(order, own, other, kernels, twiddles, index, bit, piece, whole=None):
     slots, laws, width = own.shape
-    tile = min(TILE, slots)
+    tiles = piece[1]
+    tile = slots // tiles
     block = pl.BlockSpec((tile, laws, width), lambda i, o: (i, 0, 0))
     in_specs = [
         block,
         block,
-        pl.BlockSpec((1, 2, 2, width, width), lambda i, o: (index, 0, 0, 0, 0)),
-        pl.BlockSpec((1, 1, tile, width), lambda i, o: (index + 1, target, i, 0)),
+        pl.BlockSpec((None, 2, 2, width, width), lambda i, o: (index, 0, 0, 0, 0)),
+        pl.BlockSpec((None, None, tile, width), lambda i, o: (index + 1, *spot(i, piece), 0)),
     ]
     args, aliases = [own, other, kernels, twiddles], {}
     out_shape, out_spec = jax.ShapeDtypeStruct(own.shape, own.dtype), block
-    if last:
-        out_shape = jax.ShapeDtypeStruct((twiddles.shape[1], *own.shape), own.dtype)
-        out_spec = pl.BlockSpec((None, tile, laws, width), lambda i, o: (target, i, 0, 0))
-        if whole is not None:
-            args.append(whole)
-            in_specs.append(pl.BlockSpec(memory_space=pl.ANY))
-            aliases = {5: 0}
+    if index == 2:
+        out_shape = jax.ShapeDtypeStruct((*twiddles.shape[1:3], laws, width), own.dtype)
+        out_spec = pl.BlockSpec((None, tile, laws, width), lambda i, o: (*spot(i, piece), 0, 0))
+    if whole is not None:
+        args.append(whole)
+        in_specs.append(pl.BlockSpec(memory_space=pl.ANY))
+        aliases = {5: 0}
     return call(
         functools.partial(level_kernel, bit),
         out_shape,
-        (slots // tile,),
+        (tiles,),
         in_specs,
         out_spec,
         args,
@@ -277,20 +290,21 @@
     )
 
 
-def far_kernel(order, a, b, c, d, out):
+def far_kernel(order, a, b, c, d, *rest):
+    out = rest[-1]
     for i, block in enumerate((a, b, c, d)):
         out[i] = block[0]
 
 
-def far_part(order, blocks):
+def far_part(order, blocks, after):
     _, rows, width = blocks[0].shape
     return call(
         far_kernel,
         jax.ShapeDtypeStruct((4, rows, width), blocks[0].dtype),
         (1,),
-        [pl.BlockSpec((1, rows, width), lambda i, o: (1, 0, 0))] * 4,
+        [*[pl.BlockSpec((1, rows, width), lambda i, o: (1, 0, 0))] * 4, *[pl.BlockSpec(memory_space=pl.ANY)] * len(after)],
         pl.BlockSpec((4, rows, width), lambda i, o: (0, 0, 0)),
-        blocks,
+        (*blocks, *after),
         order,
         nbytes=16 * rows * width,
     )
@@ -343,30 +357,28 @@
 
 
 def body(weights_in, twiddles, kernels):
-    targets, _, laws, _ = weights_in.shape
+    targets, slots, laws, _ = weights_in.shape
     order = my_order()
     far_send = pack(order, weights_in, twiddles, SECOND)
     far = swap(far_send, SECOND)
     near = pack(order, weights_in, twiddles, 0)
-    swapped = list(range(GATHERED, targets))
-    state = {}
-    for target in swapped:
-        own = first_twist(order, weights_in, twiddles, target, far_send)
-        state[target] = own, swap(own, FIRST)
-    for target in swapped:
-        own = level(order, *state[target], kernels, twiddles, 0, FIRST, target)
-        state[target] = own, swap(own, SECOND)
-    pairs = pair_up(order, near, far, [state[target][0] for target in swapped])
+    cuts = pieces(targets, slots)
+    own = [first_twist(order, weights_in, twiddles, piece, far_send) for piece in cuts]
+
+    def next_level(index, bit, own, other):
+        return [level(order, *pair, kernels, twiddles, index, bit, piece) for *pair, piece in zip(own, other, cuts)]
+
+    own = next_level(0, FIRST, own, [swap(block, FIRST) for block in own])
+    pairs = pair_up(order, near, far, own)
     received = [swap(pair, place) for pair, place in zip(pairs, PLANE[1:])]
-    for target in swapped:
-        own = level(order, *state[target], kernels, twiddles, 1, SECOND, target)
-        state[target] = own, swap(own, THIRD)
-    done = gathered_levels(order, near, far, received, kernels, laws, [state[swapped[0]][0]])
+    own = next_level(1, SECOND, own, [swap(block, SECOND) for block in own])
+    other = [swap(block, THIRD) for block in own]
+    whole = level(order, own[0], other[0], kernels, twiddles, 2, THIRD, cuts[0])
+    done = gathered_levels(order, near, far, received, kernels, laws, own[:1])
     back = [done[0], *[swap(block, place) for block, place in zip(done[1:], PLANE[1:])]]
-    far_back = swap(far_part(order, back), SECOND)
-    whole = None
-    for target in swapped:
-        whole = level(order, *state[target], kernels, twiddles, 2, THIRD, target, whole, True)
+    far_back = swap(far_part(order, back, [own[-2], whole]), SECOND)
+    for *pair, piece in list(zip(own, other, cuts))[1:]:
+        whole = level(order, *pair, kernels, twiddles, 2, THIRD, piece, whole)
     whole = unpack(order, back, twiddles, whole, 0)
     return unpack(order, [far_back], twiddles, whole, SECOND)
 

time: 218 us -> 206 us (0.945)
  waiting for transfers between devices: 139 us -> 120 us
  Pallas kernels: 40.6 us -> 44.9 us
    ppermute x8 -> x10, waiting for transfers between devices: 105 us -> 90.9 us  [swap(): return lax.ppermute(block, 'src', [(i, i ^ flip_src) for i in range(n_src)])]
    ppermute x4 -> x5, waiting for transfers between devices: 33.6 us -> 21.9 us  [swap(): return lax.ppermute(block, 'tgt', [(i, i ^ flip_tgt) for i in range(n_tgt)])]
    ppermute x2, waiting for transfers between devices: 0.45 us -> 7.48 us  [swap(): return lax.ppermute(block, ('src', 'tgt'), route)]
    pallas_call x15 -> x19, Pallas kernels: 40.6 us -> 44.9 us  [call(): pl.pallas_call(kernel, out_shape=out_shape, grid_spec=pltpu.PrefetchScala...]
    ppermute x4 -> x5, starting transfers between devices: 11.3 us -> 13.4 us  [swap(): return lax.ppermute(block, 'tgt', [(i, i ^ flip_tgt) for i in range(n_tgt)])]
    ppermute x8 -> x10, starting transfers between devices: 23.3 us -> 23.1 us  [swap(): return lax.ppermute(block, 'src', [(i, i ^ flip_src) for i in range(n_src)])]
  transfers between devices with their start and end apart: 14 -> 17, of which waited for: 9 -> 9; matrix products, arithmetic and copies ran while one was open for 0% -> 0% of each run, Pallas kernels for 14% -> 19%
where the time goes in v2:
time: 206 us; the launch traced here: 205 us
  waiting for transfers between devices  120 us (58%)
  Pallas kernels  44.9 us (22%)
  starting transfers between devices  38.3 us (19%)
    ppermute x10, waiting for transfers between devices, swap(): return lax.ppermute(block, 'src', [(i, i ^ flip_src) for i in range(n_src)])  90.9 us
    pallas_call x19, Pallas kernels, call(): pl.pallas_call(kernel, out_shape=out_shape, grid_spec=pltpu.PrefetchScala...  44.9 us
    ppermute x10, starting transfers between devices, swap(): return lax.ppermute(block, 'src', [(i, i ^ flip_src) for i in range(n_src)])  23.1 us
    ppermute x5, waiting for transfers between devices, swap(): return lax.ppermute(block, 'tgt', [(i, i ^ flip_tgt) for i in range(n_tgt)])  21.9 us
    ppermute x5, starting transfers between devices, swap(): return lax.ppermute(block, 'tgt', [(i, i ^ flip_tgt) for i in range(n_tgt)])  13.4 us
    ppermute x2, waiting for transfers between devices, swap(): return lax.ppermute(block, ('src', 'tgt'), route)  7.48 us
  transfers between devices with their start and end apart: 17, of which 9 were waited for; matrix products, arithmetic and copies ran while one was open for 0% of the time, Pallas kernels for 19%

profile of v2, /device:TPU:80, one launch (start us, length us, event | category | flops | bytes accessed | tf_op | source)
XLA Modules:
  0.0 204.9 jit_solution(17308355510665411284)
XLA Ops:
  1.2 3.2 %shard_map.38._ = bf16[4,1088,128]{2,1,0:T(8,128)(2,1)S(1)} custom-call(s32[8]{0:T(128)S(1)} %iota_xor_fusion.order, bf16[4,128,32,128]{3,2,1,0:T(8,128)(2,1)} %w.9, f32[4,4,128,128]{3,2,1,0:T(8,128)S(1)} %copy-done), custom_call_target="tpu_custom_call" | custom-call | bytes 8912896 | tf_op jit(solution)/shard_map/pallas_call | solution.py:60
  4.5 5.5 %collective-permute-start = (bf16[4,1088,128]{2,1,0:T(8,128)(2,1)S(1)}, bf16[4,1088,128]{2,1,0:T(8,128)(2,1)S(1)}, u32[]{:S(2)}, u32[]{:S(2)}) collective-permute-start(bf16[4,1088,128]{2,1,0:T(8,128)(2,1)S(1)} %shard_map.38._), channel_id=1, source_target_pairs={{0,64},{8,72},{16,80},{24,88},{32,96},{40,104},{48,112},{56,120},{... | collective-permute-start | bytes 3342344 | tf_op jit(solution)/shard_map/ppermute | solution.py:22
  10.0 3.0 %shard_map.41.own = bf16[96,32,128]{2,1,0:T(8,128)(2,1)S(1)} custom-call(s32[8]{0:T(128)S(1)} %iota_xor_fusion.order, bf16[4,128,32,128]{3,2,1,0:T(8,128)(2,1)} %w.9, f32[4,4,128,128]{3,2,1,0:T(8,128)S(1)} %copy-done, bf16[4,1088,128]{2,1,0:T(8,128)(2,1)S(1)} %shard_map.38._), custom_call_target="tpu_custom_call" | custom-call | bytes 6291456 | tf_op jit(solution)/shard_map/pallas_call | solution.py:60
  12.9 1.6 collective-permute-start.2
  14.5 3.0 %shard_map.43.own = bf16[96,32,128]{2,1,0:T(8,128)(2,1)S(1)} custom-call(s32[8]{0:T(128)S(1)} %iota_xor_fusion.order, bf16[4,128,32,128]{3,2,1,0:T(8,128)(2,1)} %w.9, f32[4,4,128,128]{3,2,1,0:T(8,128)S(1)} %copy-done, bf16[4,1088,128]{2,1,0:T(8,128)(2,1)S(1)} %shard_map.38._), custom_call_target="tpu_custom_call" | custom-call | bytes 6291456 | tf_op jit(solution)/shard_map/pallas_call | solution.py:60
  18.1 2.0 shard_map.39.own
  21.7 3.2 %shard_map.37.near = bf16[4,1088,128]{2,1,0:T(8,128)(2,1)S(1)} custom-call(s32[8]{0:T(128)S(1)} %iota_xor_fusion.order, bf16[4,128,32,128]{3,2,1,0:T(8,128)(2,1)} %w.9, f32[4,4,128,128]{3,2,1,0:T(8,128)S(1)} %copy-done), custom_call_target="tpu_custom_call" | custom-call | bytes 8912896 | tf_op jit(solution)/shard_map/pallas_call | solution.py:60
  24.9 35.2 %collective-permute-done.1.other = bf16[64,32,128]{2,1,0:T(8,128)(2,1)S(1)} collective-permute-done((bf16[64,32,128]{2,1,0:T(8,128)(2,1)S(1)}, bf16[64,32,128]{2,1,0:T(8,128)(2,1)S(1)}, u32[]{:S(2)}, u32[]{:S(2)}) %collective-permute-start.1) | collective-permute-done | bytes 524320 | tf_op jit(solution)/shard_map/ppermute | solution.py:22
  62.3 2.0 shard_map.42.rest_1_.own
  64.2 2.0 shard_map.44.rest_2_.own
  66.9 3.1 %collective-permute-start.4 = (bf16[2,1088,128]{2,1,0:T(8,128)(2,1)S(1)}, bf16[2,1088,128]{2,1,0:T(8,128)(2,1)S(1)}, u32[]{:S(2)}, u32[]{:S(2)}) collective-permute-start(bf16[2,1088,128]{2,1,0:T(8,128)(2,1)S(1)} %get-tuple-element.12), channel_id=1, source_target_pairs={{0,4},{1,5},{2,6},{3,7},{4,0},{5,1},{6,2},{7,3},{8,12},{9,13},{10,... | collective-permute-start | bytes 1671176 | tf_op jit(solution)/shard_map/ppermute | solution.py:24
  71.2 5.4 %collective-permute-start.11 = (bf16[96,32,128]{2,1,0:T(8,128)(2,1)S(1)}, bf16[96,32,128]{2,1,0:T(8,128)(2,1)S(1)}, u32[]{:S(2)}, u32[]{:S(2)}) collective-permute-start(bf16[96,32,128]{2,1,0:T(8,128)(2,1)S(1)} %shard_map.42.rest_1_.own), channel_id=1, source_target_pairs={{0,64},{8,72},{16,80},{24,88},{32,96},{40,104},{48,112},{56,120},{... | collective-permute-start | bytes 2359304 | tf_op jit(solution)/shard_map/ppermute | solution.py:22
  76.5 37.1 %collective-permute-done.7.other = bf16[64,32,128]{2,1,0:T(8,128)(2,1)S(1)} collective-permute-done((bf16[64,32,128]{2,1,0:T(8,128)(2,1)S(1)}, bf16[64,32,128]{2,1,0:T(8,128)(2,1)S(1)}, u32[]{:S(2)}, u32[]{:S(2)}) %collective-permute-start.7) | collective-permute-done | bytes 524320 | tf_op jit(solution)/shard_map/ppermute | solution.py:22
  115.9 3.0 %collective-permute-start.12 = (bf16[64,32,128]{2,1,0:T(8,128)(2,1)S(1)}, bf16[64,32,128]{2,1,0:T(8,128)(2,1)S(1)}, u32[]{:S(2)}, u32[]{:S(2)}) collective-permute-start(bf16[64,32,128]{2,1,0:T(8,128)(2,1)S(1)} %shard_map.46.rest_0_.own), channel_id=1, source_target_pairs={{0,4},{1,5},{2,6},{3,7},{4,0},{5,1},{6,2},{7,3},{8,12},{9,13},{10,... | collective-permute-start | bytes 1572872 | tf_op jit(solution)/shard_map/ppermute | solution.py:24
  118.9 4.8 %shard_map.47 = (bf16[2,1024,128]{2,1,0:T(8,128)(2,1)S(1)}, bf16[2,1024,128]{2,1,0:T(8,128)(2,1)S(1)}, bf16[2,1024,128]{2,1,0:T(8,128)(2,1)S(1)}, bf16[2,1024,128]{2,1,0:T(8,128)(2,1)S(1)}) custom-call(s32[8]{0:T(128)S(1)} %iota_xor_fusion.order, bf16[4,1088,128]{2,1,0:T(8,128)(2,1)S(1)} %shard_map.37.near, bf16[4,1088,128]{2,1,0:T(8,128)(2,1)} %copy-done.3, ...), custom_call_target="tpu_custom_call" | custom-call | flops 6442450944 | bytes 16777216 | tf_op jit(solution)/shard_map/pallas_call | solution.py:60
  126.5 4.8 %collective-permute-done.12.other = bf16[64,32,128]{2,1,0:T(8,128)(2,1)S(1)} collective-permute-done((bf16[64,32,128]{2,1,0:T(8,128)(2,1)S(1)}, bf16[64,32,128]{2,1,0:T(8,128)(2,1)S(1)}, u32[]{:S(2)}, u32[]{:S(2)}) %collective-permute-start.12) | collective-permute-done | bytes 524320 | tf_op jit(solution)/shard_map/ppermute | solution.py:24
  131.3 2.5 %collective-permute-start.9 = (bf16[2,1024,128]{2,1,0:T(8,128)(2,1)S(1)}, bf16[2,1024,128]{2,1,0:T(8,128)(2,1)S(1)}, u32[]{:S(2)}, u32[]{:S(2)}) collective-permute-start(bf16[2,1024,128]{2,1,0:T(8,128)(2,1)S(1)} %get-tuple-element.17), channel_id=1, source_target_pairs={{0,128},{8,136},{16,144},{24,152},{32,160},{40,168},{48,176},{56,1... | collective-permute-start | bytes 1572872 | tf_op jit(solution)/shard_map/ppermute | solution.py:22
  133.8 2.2 %shard_map.49.rest_1_.rest_0_ = bf16[4,128,32,128]{3,2,1,0:T(8,128)(2,1)} custom-call(s32[8]{0:T(128)S(1)} %iota_xor_fusion.order, bf16[64,32,128]{2,1,0:T(8,128)(2,1)S(1)} %shard_map.46.rest_0_.own, bf16[64,32,128]{2,1,0:T(8,128)(2,1)S(1)} %collective-permute-done.12.other, bf16[3,2,2,128,128]{4,3,2,1,0:T(8,128)(2,1)S(1)} %copy-done.2, ...), custom_call_target="tpu_custom_call" | custom-call | flops 1073741824 | bytes 6291456 | tf_op jit(solution)/shard_map/pallas_call | solution.py:60
  136.0 4.9 %collective-permute-done.11.other = bf16[96,32,128]{2,1,0:T(8,128)(2,1)S(1)} collective-permute-done((bf16[96,32,128]{2,1,0:T(8,128)(2,1)S(1)}, bf16[96,32,128]{2,1,0:T(8,128)(2,1)S(1)}, u32[]{:S(2)}, u32[]{:S(2)}) %collective-permute-start.11) | collective-permute-done | bytes 786464 | tf_op jit(solution)/shard_map/ppermute | solution.py:22
  140.9 1.9 shard_map.48.rest_0_.own
  142.8 3.0 %collective-permute-start.16 = (bf16[96,32,128]{2,1,0:T(8,128)(2,1)S(1)}, bf16[96,32,128]{2,1,0:T(8,128)(2,1)S(1)}, u32[]{:S(2)}, u32[]{:S(2)}) collective-permute-start(bf16[96,32,128]{2,1,0:T(8,128)(2,1)S(1)} %shard_map.48.rest_0_.own), channel_id=1, source_target_pairs={{0,4},{1,5},{2,6},{3,7},{4,0},{5,1},{6,2},{7,3},{8,12},{9,13},{10,... | collective-permute-start | bytes 2359304 | tf_op jit(solution)/shard_map/ppermute | solution.py:24
  145.9 7.5 %collective-permute-done.10.d.refs_3_ = bf16[2,1024,128]{2,1,0:T(8,128)(2,1)S(1)} collective-permute-done((bf16[2,1024,128]{2,1,0:T(8,128)(2,1)S(1)}, bf16[2,1024,128]{2,1,0:T(8,128)(2,1)S(1)}, u32[]{:S(2)}, u32[]{:S(2)}) %collective-permute-start.10) | collective-permute-done | bytes 524320 | tf_op jit(solution)/shard_map/ppermute | solution.py:29
  154.1 4.1 %collective-permute-start.13 = (bf16[4,1024,128]{2,1,0:T(8,128)(2,1)S(1)}, bf16[4,1024,128]{2,1,0:T(8,128)(2,1)S(1)}, u32[]{:S(2)}, u32[]{:S(2)}) collective-permute-start(bf16[4,1024,128]{2,1,0:T(8,128)(2,1)S(1)} %shard_map.50), channel_id=1, source_target_pairs={{0,64},{8,72},{16,80},{24,88},{32,96},{40,104},{48,112},{56,120},{... | collective-permute-start | bytes 3145736 | tf_op jit(solution)/shard_map/ppermute | solution.py:22
  158.2 1.9 shard_map.51.own
  160.2 2.7 %collective-permute-start.15 = (bf16[96,32,128]{2,1,0:T(8,128)(2,1)S(1)}, bf16[96,32,128]{2,1,0:T(8,128)(2,1)S(1)}, u32[]{:S(2)}, u32[]{:S(2)}) collective-permute-start(bf16[96,32,128]{2,1,0:T(8,128)(2,1)S(1)} %shard_map.51.own), channel_id=1, source_target_pairs={{0,4},{1,5},{2,6},{3,7},{4,0},{5,1},{6,2},{7,3},{8,12},{9,13},{10,... | collective-permute-start | bytes 2359304 | tf_op jit(solution)/shard_map/ppermute | solution.py:24
  162.9 7.4 %collective-permute-done.16.other = bf16[96,32,128]{2,1,0:T(8,128)(2,1)S(1)} collective-permute-done((bf16[96,32,128]{2,1,0:T(8,128)(2,1)S(1)}, bf16[96,32,128]{2,1,0:T(8,128)(2,1)S(1)}, u32[]{:S(2)}, u32[]{:S(2)}) %collective-permute-start.16) | collective-permute-done | bytes 786464 | tf_op jit(solution)/shard_map/ppermute | solution.py:24
  170.3 2.9 %shard_map.52.rest_0_ = bf16[4,128,32,128]{3,2,1,0:T(8,128)(2,1)} custom-call(s32[8]{0:T(128)S(1)} %iota_xor_fusion.order, bf16[96,32,128]{2,1,0:T(8,128)(2,1)S(1)} %shard_map.48.rest_0_.own, bf16[96,32,128]{2,1,0:T(8,128)(2,1)S(1)} %collective-permute-done.16.other, bf16[3,2,2,128,128]{4,3,2,1,0:T(8,128)(2,1)S(1)} %copy-done.2, ...), custom_call_target="tpu_custom_call", output_to_operand_aliasing={{}: (5, {})} | custom-call | flops 1610612736 | bytes 9437184 | tf_op jit(solution)/shard_map/pallas_call | solution.py:60
  173.2 9.7 %collective-permute-done.15.other = bf16[96,32,128]{2,1,0:T(8,128)(2,1)S(1)} collective-permute-done((bf16[96,32,128]{2,1,0:T(8,128)(2,1)S(1)}, bf16[96,32,128]{2,1,0:T(8,128)(2,1)S(1)}, u32[]{:S(2)}, u32[]{:S(2)}) %collective-permute-start.15) | collective-permute-done | bytes 786464 | tf_op jit(solution)/shard_map/ppermute | solution.py:24
  182.9 2.9 %shard_map.53.refs_5_ = bf16[4,128,32,128]{3,2,1,0:T(8,128)(2,1)} custom-call(s32[8]{0:T(128)S(1)} %iota_xor_fusion.order, bf16[96,32,128]{2,1,0:T(8,128)(2,1)S(1)} %shard_map.51.own, bf16[96,32,128]{2,1,0:T(8,128)(2,1)S(1)} %collective-permute-done.15.other, bf16[3,2,2,128,128]{4,3,2,1,0:T(8,128)(2,1)S(1)} %copy-done.2, ...), custom_call_target="tpu_custom_call", output_to_operand_aliasing={{}: (5, {})} | custom-call | flops 1610612736 | bytes 9437184 | tf_op jit(solution)/shard_map/pallas_call | solution.py:60
  185.8 2.8 %shard_map.54.refs_2_ = bf16[4,128,32,128]{3,2,1,0:T(8,128)(2,1)} custom-call(s32[8]{0:T(128)S(1)} %iota_xor_fusion.order, bf16[2,1024,128]{2,1,0:T(8,128)(2,1)S(1)} %get-tuple-element.15.a.refs_0_, bf16[2,1024,128]{2,1,0:T(8,128)(2,1)S(1)} %collective-permute-done.8.b.refs_1_, ...), custom_call_target="tpu_custom_call", output_to_operand_aliasing={{}: (6, {})} | custom-call | bytes 8388608 | tf_op jit(solution)/shard_map/pallas_call | solution.py:60
  188.5 13.6 %collective-permute-done.13.refs_0_ = bf16[4,1024,128]{2,1,0:T(8,128)(2,1)S(1)} collective-permute-done((bf16[4,1024,128]{2,1,0:T(8,128)(2,1)S(1)}, bf16[4,1024,128]{2,1,0:T(8,128)(2,1)S(1)}, u32[]{:S(2)}, u32[]{:S(2)}) %collective-permute-start.13) | collective-permute-done | bytes 1048608 | tf_op jit(solution)/shard_map/ppermute | solution.py:22
  202.1 2.7 %shard_map.55 = bf16[4,128,32,128]{3,2,1,0:T(8,128)(2,1)} custom-call(s32[8]{0:T(128)S(1)} %iota_xor_fusion.order, bf16[4,1024,128]{2,1,0:T(8,128)(2,1)S(1)} %collective-permute-done.13.refs_0_, f32[4,4,128,128]{3,2,1,0:T(8,128)S(1)} %copy-done.1, bf16[4,128,32,128]{3,2,1,0:T(8,128)(2,1)} %shard_map.54.refs_2_), custom_call_target="tpu_custom_call", output_to_operand_aliasing={{}: (3, {})} | custom-call | bytes 8388608 | tf_op jit(solution)/shard_map/pallas_call | solution.py:60
  (30 shorter events, 13.1 us)
Async XLA Ops:
  0.0 1.2 copy-start
  4.5 61.7 %collective-permute-start = (bf16[4,1088,128]{2,1,0:T(8,128)(2,1)S(1)}, bf16[4,1088,128]{2,1,0:T(8,128)(2,1)S(1)}, u32[]{:S(2)}, u32[]{:S(2)}) collective-permute-start(bf16[4,1088,128]{2,1,0:T(8,128)(2,1)S(1)} %shard_map.38._), channel_id=1, source_target_pairs={{0,64},{8,72},{16,80},{24,88},{32,96},{40,104},{48,112},{56,120},{... | collective-permute-start | bytes 3342344 | tf_op jit(solution)/shard_map/ppermute | solution.py:22
  12.9 49.3 %collective-permute-start.2 = (bf16[96,32,128]{2,1,0:T(8,128)(2,1)S(1)}, bf16[96,32,128]{2,1,0:T(8,128)(2,1)S(1)}, u32[]{:S(2)}, u32[]{:S(2)}) collective-permute-start(bf16[96,32,128]{2,1,0:T(8,128)(2,1)S(1)} %shard_map.41.own), channel_id=1, source_target_pairs={{0,128},{8,136},{16,144},{24,152},{32,160},{40,168},{48,176},{56,1... | collective-permute-start | bytes 2359304 | tf_op jit(solution)/shard_map/ppermute | solution.py:22
  17.5 46.8 %collective-permute-start.3 = (bf16[96,32,128]{2,1,0:T(8,128)(2,1)S(1)}, bf16[96,32,128]{2,1,0:T(8,128)(2,1)S(1)}, u32[]{:S(2)}, u32[]{:S(2)}) collective-permute-start(bf16[96,32,128]{2,1,0:T(8,128)(2,1)S(1)} %shard_map.43.own), channel_id=1, source_target_pairs={{0,128},{8,136},{16,144},{24,152},{32,160},{40,168},{48,176},{56,1... | collective-permute-start | bytes 2359304 | tf_op jit(solution)/shard_map/ppermute | solution.py:22
  20.1 40.0 %copy-start.2 = (bf16[3,2,2,128,128]{4,3,2,1,0:T(8,128)(2,1)S(1)}, bf16[3,2,2,128,128]{4,3,2,1,0:T(8,128)(2,1)}, u32[]{:S(2)}) copy-start(bf16[3,2,2,128,128]{4,3,2,1,0:T(8,128)(2,1)} %maps.19) | copy-start | bytes 1179652
  20.1 40.0 %collective-permute-start.1 = (bf16[64,32,128]{2,1,0:T(8,128)(2,1)S(1)}, bf16[64,32,128]{2,1,0:T(8,128)(2,1)S(1)}, u32[]{:S(2)}, u32[]{:S(2)}) collective-permute-start(bf16[64,32,128]{2,1,0:T(8,128)(2,1)S(1)} %shard_map.39.own), channel_id=1, source_target_pairs={{0,128},{8,136},{16,144},{24,152},{32,160},{40,168},{48,176},{56,1... | collective-permute-start | bytes 1572872 | tf_op jit(solution)/shard_map/ppermute | solution.py:22
  61.6 52.0 %collective-permute-start.7 = (bf16[64,32,128]{2,1,0:T(8,128)(2,1)S(1)}, bf16[64,32,128]{2,1,0:T(8,128)(2,1)S(1)}, u32[]{:S(2)}, u32[]{:S(2)}) collective-permute-start(bf16[64,32,128]{2,1,0:T(8,128)(2,1)S(1)} %shard_map.40.rest_0_.own), channel_id=1, source_target_pairs={{0,64},{8,72},{16,80},{24,88},{32,96},{40,104},{48,112},{56,120},{... | collective-permute-start | bytes 1572872 | tf_op jit(solution)/shard_map/ppermute | solution.py:22
  64.2 50.1 %copy-start.1 = (f32[4,4,128,128]{3,2,1,0:T(8,128)S(1)}, f32[4,4,128,128]{3,2,1,0:T(8,128)}, u32[]{:S(2)}) copy-start(f32[4,4,128,128]{3,2,1,0:T(8,128)} %refs_1_.1) | copy-start | bytes 3145732
  66.2 52.7 %copy-start.3 = (bf16[4,1088,128]{2,1,0:T(8,128)(2,1)}, bf16[4,1088,128]{2,1,0:T(8,128)(2,1)S(1)}, u32[]{:S(2)}) copy-start(bf16[4,1088,128]{2,1,0:T(8,128)(2,1)S(1)} %collective-permute-done.far) | copy-start | bytes 3342340
  66.9 49.0 %collective-permute-start.4 = (bf16[2,1088,128]{2,1,0:T(8,128)(2,1)S(1)}, bf16[2,1088,128]{2,1,0:T(8,128)(2,1)S(1)}, u32[]{:S(2)}, u32[]{:S(2)}) collective-permute-start(bf16[2,1088,128]{2,1,0:T(8,128)(2,1)S(1)} %get-tuple-element.12), channel_id=1, source_target_pairs={{0,4},{1,5},{2,6},{3,7},{4,0},{5,1},{6,2},{7,3},{8,12},{9,13},{10,... | collective-permute-start | bytes 1671176 | tf_op jit(solution)/shard_map/ppermute | solution.py:24
  70.0 48.9 %collective-permute-start.5 = (bf16[2,1088,128]{2,1,0:T(8,128)(2,1)S(1)}, bf16[2,1088,128]{2,1,0:T(8,128)(2,1)S(1)}, u32[]{:S(2)}, u32[]{:S(2)}) collective-permute-start(bf16[2,1088,128]{2,1,0:T(8,128)(2,1)S(1)} %get-tuple-element.13), channel_id=1, source_target_pairs={{0,128},{8,136},{16,144},{24,152},{32,160},{40,168},{48,176},{56,1... | collective-permute-start | bytes 1671176 | tf_op jit(solution)/shard_map/ppermute | solution.py:22
  70.6 48.3 %collective-permute-start.6 = (bf16[2,1088,128]{2,1,0:T(8,128)(2,1)S(1)}, bf16[2,1088,128]{2,1,0:T(8,128)(2,1)S(1)}, u32[]{:S(2)}, u32[]{:S(2)}) collective-permute-start(bf16[2,1088,128]{2,1,0:T(8,128)(2,1)S(1)} %get-tuple-element.14), channel_id=1, source_target_pairs={{0,132},{1,133},{2,134},{3,135},{4,128},{5,129},{6,130},{7,131},{8... | collective-permute-start | bytes 1671176 | tf_op jit(solution)/shard_map/ppermute | solution.py:29
  71.2 69.7 %collective-permute-start.11 = (bf16[96,32,128]{2,1,0:T(8,128)(2,1)S(1)}, bf16[96,32,128]{2,1,0:T(8,128)(2,1)S(1)}, u32[]{:S(2)}, u32[]{:S(2)}) collective-permute-start(bf16[96,32,128]{2,1,0:T(8,128)(2,1)S(1)} %shard_map.42.rest_1_.own), channel_id=1, source_target_pairs={{0,64},{8,72},{16,80},{24,88},{32,96},{40,104},{48,112},{56,120},{... | collective-permute-start | bytes 2359304 | tf_op jit(solution)/shard_map/ppermute | solution.py:22
  113.7 44.5 %collective-permute-start.14 = (bf16[96,32,128]{2,1,0:T(8,128)(2,1)S(1)}, bf16[96,32,128]{2,1,0:T(8,128)(2,1)S(1)}, u32[]{:S(2)}, u32[]{:S(2)}) collective-permute-start(bf16[96,32,128]{2,1,0:T(8,128)(2,1)S(1)} %shard_map.44.rest_2_.own), channel_id=1, source_target_pairs={{0,64},{8,72},{16,80},{24,88},{32,96},{40,104},{48,112},{56,120},{... | collective-permute-start | bytes 2359304 | tf_op jit(solution)/shard_map/ppermute | solution.py:22
  115.9 15.4 %collective-permute-start.12 = (bf16[64,32,128]{2,1,0:T(8,128)(2,1)S(1)}, bf16[64,32,128]{2,1,0:T(8,128)(2,1)S(1)}, u32[]{:S(2)}, u32[]{:S(2)}) collective-permute-start(bf16[64,32,128]{2,1,0:T(8,128)(2,1)S(1)} %shard_map.46.rest_0_.own), channel_id=1, source_target_pairs={{0,4},{1,5},{2,6},{3,7},{4,0},{5,1},{6,2},{7,3},{8,12},{9,13},{10,... | collective-permute-start | bytes 1572872 | tf_op jit(solution)/shard_map/ppermute | solution.py:24
  123.7 29.6 %collective-permute-start.10 = (bf16[2,1024,128]{2,1,0:T(8,128)(2,1)S(1)}, bf16[2,1024,128]{2,1,0:T(8,128)(2,1)S(1)}, u32[]{:S(2)}, u32[]{:S(2)}) collective-permute-start(bf16[2,1024,128]{2,1,0:T(8,128)(2,1)S(1)} %get-tuple-element.18), channel_id=1, source_target_pairs={{0,132},{1,133},{2,134},{3,135},{4,128},{5,129},{6,130},{7,131},{8... | collective-permute-start | bytes 1572872 | tf_op jit(solution)/shard_map/ppermute | solution.py:29
  125.0 28.4 %collective-permute-start.8 = (bf16[2,1024,128]{2,1,0:T(8,128)(2,1)S(1)}, bf16[2,1024,128]{2,1,0:T(8,128)(2,1)S(1)}, u32[]{:S(2)}, u32[]{:S(2)}) collective-permute-start(bf16[2,1024,128]{2,1,0:T(8,128)(2,1)S(1)} %get-tuple-element.16), channel_id=1, source_target_pairs={{0,4},{1,5},{2,6},{3,7},{4,0},{5,1},{6,2},{7,3},{8,12},{9,13},{10,... | collective-permute-start | bytes 1572872 | tf_op jit(solution)/shard_map/ppermute | solution.py:24
  131.3 22.2 %collective-permute-start.9 = (bf16[2,1024,128]{2,1,0:T(8,128)(2,1)S(1)}, bf16[2,1024,128]{2,1,0:T(8,128)(2,1)S(1)}, u32[]{:S(2)}, u32[]{:S(2)}) collective-permute-start(bf16[2,1024,128]{2,1,0:T(8,128)(2,1)S(1)} %get-tuple-element.17), channel_id=1, source_target_pairs={{0,128},{8,136},{16,144},{24,152},{32,160},{40,168},{48,176},{56,1... | collective-permute-start | bytes 1572872 | tf_op jit(solution)/shard_map/ppermute | solution.py:22
  142.8 27.5 %collective-permute-start.16 = (bf16[96,32,128]{2,1,0:T(8,128)(2,1)S(1)}, bf16[96,32,128]{2,1,0:T(8,128)(2,1)S(1)}, u32[]{:S(2)}, u32[]{:S(2)}) collective-permute-start(bf16[96,32,128]{2,1,0:T(8,128)(2,1)S(1)} %shard_map.48.rest_0_.own), channel_id=1, source_target_pairs={{0,4},{1,5},{2,6},{3,7},{4,0},{5,1},{6,2},{7,3},{8,12},{9,13},{10,... | collective-permute-start | bytes 2359304 | tf_op jit(solution)/shard_map/ppermute | solution.py:24
  154.1 48.0 %collective-permute-start.13 = (bf16[4,1024,128]{2,1,0:T(8,128)(2,1)S(1)}, bf16[4,1024,128]{2,1,0:T(8,128)(2,1)S(1)}, u32[]{:S(2)}, u32[]{:S(2)}) collective-permute-start(bf16[4,1024,128]{2,1,0:T(8,128)(2,1)S(1)} %shard_map.50), channel_id=1, source_target_pairs={{0,64},{8,72},{16,80},{24,88},{32,96},{40,104},{48,112},{56,120},{... | collective-permute-start | bytes 3145736 | tf_op jit(solution)/shard_map/ppermute | solution.py:22
  160.2 22.7 %collective-permute-start.15 = (bf16[96,32,128]{2,1,0:T(8,128)(2,1)S(1)}, bf16[96,32,128]{2,1,0:T(8,128)(2,1)S(1)}, u32[]{:S(2)}, u32[]{:S(2)}) collective-permute-start(bf16[96,32,128]{2,1,0:T(8,128)(2,1)S(1)} %shard_map.51.own), channel_id=1, source_target_pairs={{0,4},{1,5},{2,6},{3,7},{4,0},{5,1},{6,2},{7,3},{8,12},{9,13},{10,... | collective-permute-start | bytes 2359304 | tf_op jit(solution)/shard_map/ppermute | solution.py:24

commit v3 on v2

--- a/solution.py
+++ b/solution.py
@@ -10,7 +10,12 @@
 FIRST, SECOND, THIRD = 4, 2, 1
 GATHERED = 2
 PIECES = (2, 3, 3)
+FIRST_ORDER = (0, 1, 2)
+LEVEL_ORDER = (0, 1, 2)
 COST = 4
+TCOST = 0
+LCOST = 12
+NCOST = 4
 VMEM = 48 * 2**20
 
 
@@ -52,11 +57,15 @@
 
 
 def twist_16(block, rows):
-    wide = block.astype(jnp.float32)
-    return twist(wide, roll_half(wide), rows)
-
-
-def call(kernel, out_shape, grid, in_specs, out_specs, args, order, scratch=(), aliases=None, flops=0, nbytes=0):
+    width = block.shape[-1]
+    row = lax.broadcasted_iota(jnp.int32, (width, width), 0)
+    column = lax.broadcasted_iota(jnp.int32, (width, width), 1)
+    exchange = (jnp.abs(row - column) == width // 2).astype(jnp.float32).astype(block.dtype)
+    turned = jnp.dot(block, exchange, preferred_element_type=jnp.float32)
+    return twist(block.astype(jnp.float32), turned, rows)
+
+
+def call(kernel, out_shape, grid, in_specs, out_specs, args, order, scratch=(), aliases=None, cost=COST, flops=0, nbytes=0):
     return pl.pallas_call(
         kernel,
         out_shape=out_shape,
@@ -65,7 +74,7 @@
         ),
         input_output_aliases=aliases or {},
         compiler_params=pltpu.CompilerParams(vmem_limit_bytes=VMEM),
-        cost_estimate=pl.CostEstimate(flops=COST * flops, bytes_accessed=COST * nbytes, transcendentals=0),
+        cost_estimate=pl.CostEstimate(flops=cost * flops, bytes_accessed=cost * nbytes, transcendentals=0),
     )(order, *args)
 
 
@@ -100,6 +109,7 @@
         pl.BlockSpec((tile, laws, width), lambda i, o: (i, 0, 0)),
         (weights, twiddles, after),
         order,
+        cost=TCOST,
         nbytes=4 * tiles * tile * laws * width,
     )
 
@@ -123,7 +133,7 @@
     out[...] = twist(state[:, :width], state[:, width:], t[...]).astype(out.dtype).reshape(out.shape)
 
 
-def level(order, own, other, kernels, twiddles, index, bit, piece, whole=None):
+def level(order, own, other, kernels, twiddles, index, bit, piece, whole=None, after=()):
     slots, laws, width = own.shape
     tiles = piece[1]
     tile = slots // tiles
@@ -143,6 +153,8 @@
         args.append(whole)
         in_specs.append(pl.BlockSpec(memory_space=pl.ANY))
         aliases = {5: 0}
+    args += after
+    in_specs += [pl.BlockSpec(memory_space=pl.ANY)] * len(after)
     return call(
         functools.partial(level_kernel, bit),
         out_shape,
@@ -153,6 +165,7 @@
         order,
         scratch=[pltpu.VMEM((2 * width, 2 * width), own.dtype)],
         aliases=aliases,
+        cost=COST if index else (LCOST if piece[1] == PIECES[0] else 0),
         flops=8 * slots * laws * width * width,
         nbytes=6 * slots * laws * width,
     )
@@ -161,7 +174,8 @@
 PLANE = (0, THIRD, FIRST, FIRST | THIRD)
 
 
-def pack_kernel(order, w, t, out):
+def pack_kernel(order, w, t, *rest):
+    out = rest[-1]
     targets, slots, laws, width = w.shape
     rows = slots * laws
     for target in range(targets):
@@ -172,7 +186,7 @@
             out[0, start : start + slots, :] = t[1 + later, target].astype(out.dtype)
 
 
-def pack(order, weights, twiddles, far):
+def pack(order, weights, twiddles, far, after=()):
     _, slots, laws, width = weights.shape
     eighth = slots // 8
     rows = GATHERED * eighth * (laws + 2)
@@ -187,10 +201,12 @@
         [
             pl.BlockSpec((GATHERED, eighth, laws, width), lambda i, o: (0, which(i, o), 0, 0)),
             pl.BlockSpec((3, GATHERED, eighth, width), lambda i, o: (0, 0, which(i, o), 0)),
+            *[pl.BlockSpec(memory_space=pl.ANY)] * len(after),
         ],
         pl.BlockSpec((1, rows, width), lambda i, o: (i, 0, 0)),
-        (weights, twiddles),
-        order,
+        (weights, twiddles, *after),
+        order,
+        cost=NCOST,
         nbytes=16 * rows * width,
     )
 
@@ -361,14 +377,21 @@
     order = my_order()
     far_send = pack(order, weights_in, twiddles, SECOND)
     far = swap(far_send, SECOND)
-    near = pack(order, weights_in, twiddles, 0)
+    near = pack(order, weights_in, twiddles, 0, [far_send])
     cuts = pieces(targets, slots)
-    own = [first_twist(order, weights_in, twiddles, piece, far_send) for piece in cuts]
+    own, after = [None] * len(cuts), far_send
+    for i in FIRST_ORDER:
+        own[i] = after = first_twist(order, weights_in, twiddles, cuts[i], after)
+    other = [swap(block, FIRST) for block in own]
+    first, after = [None] * len(cuts), []
+    for i in LEVEL_ORDER:
+        first[i] = level(order, own[i], other[i], kernels, twiddles, 0, FIRST, cuts[i], None, after)
+        after = [first[i]]
+    own = first
 
     def next_level(index, bit, own, other):
         return [level(order, *pair, kernels, twiddles, index, bit, piece) for *pair, piece in zip(own, other, cuts)]
 
-    own = next_level(0, FIRST, own, [swap(block, FIRST) for block in own])
     pairs = pair_up(order, near, far, own)
     received = [swap(pair, place) for pair, place in zip(pairs, PLANE[1:])]
     own = next_level(1, SECOND, own, [swap(block, SECOND) for block in own])

time: 206 us -> 201 us (0.976)
  waiting for transfers between devices: 120 us -> 111 us
  starting transfers between devices: 38.3 us -> 43.5 us
    ppermute x10, waiting for transfers between devices: 90.9 us -> 75.9 us  [swap(): return lax.ppermute(block, 'src', [(i, i ^ flip_src) for i in range(n_src)])]
    ppermute x2, waiting for transfers between devices: 7.48 us -> 14.1 us  [swap(): return lax.ppermute(block, ('src', 'tgt'), route)]
    ppermute x10, starting transfers between devices: 23.1 us -> 27.7 us  [swap(): return lax.ppermute(block, 'src', [(i, i ^ flip_src) for i in range(n_src)])]
  transfers between devices with their start and end apart: 17 -> 17, of which waited for: 9 -> 12; matrix products, arithmetic and copies ran while one was open for 0% -> 0% of each run, Pallas kernels for 19% -> 19%
where the time goes in v3:
time: 201 us
  waiting for transfers between devices  111 us (55%)
  Pallas kernels  44.7 us (22%)
  starting transfers between devices  43.5 us (22%)
    ppermute x10, waiting for transfers between devices, swap(): return lax.ppermute(block, 'src', [(i, i ^ flip_src) for i in range(n_src)])  75.9 us
    pallas_call x19, Pallas kernels, call(): pl.pallas_call(kernel, out_shape=out_shape, grid_spec=pltpu.PrefetchScala...  44.7 us
    ppermute x10, starting transfers between devices, swap(): return lax.ppermute(block, 'src', [(i, i ^ flip_src) for i in range(n_src)])  27.7 us
    ppermute x5, waiting for transfers between devices, swap(): return lax.ppermute(block, 'tgt', [(i, i ^ flip_tgt) for i in range(n_tgt)])  21 us
    ppermute x2, waiting for transfers between devices, swap(): return lax.ppermute(block, ('src', 'tgt'), route)  14.1 us
    ppermute x5, starting transfers between devices, swap(): return lax.ppermute(block, 'tgt', [(i, i ^ flip_tgt) for i in range(n_tgt)])  12.7 us
  transfers between devices with their start and end apart: 17, of which 12 were waited for; matrix products, arithmetic and copies ran while one was open for 0% of the time, Pallas kernels for 19%

profile of v3, /device:TPU:80, one launch (start us, length us, event | category | flops | bytes accessed | tf_op | source)
XLA Modules:
  0.0 200.6 jit_solution(4020811706274493254)
XLA Ops:
  1.2 3.2 %shard_map.37.rest_0_._ = bf16[4,1088,128]{2,1,0:T(8,128)(2,1)S(1)} custom-call(s32[8]{0:T(128)S(1)} %iota_xor_fusion.order, bf16[4,128,32,128]{3,2,1,0:T(8,128)(2,1)} %w.9, f32[4,4,128,128]{3,2,1,0:T(8,128)S(1)} %copy-done), custom_call_target="tpu_custom_call" | custom-call | bytes 8912896 | tf_op jit(solution)/shard_map/pallas_call | solution.py:69
  4.5 5.5 %collective-permute-start = (bf16[4,1088,128]{2,1,0:T(8,128)(2,1)S(1)}, bf16[4,1088,128]{2,1,0:T(8,128)(2,1)S(1)}, u32[]{:S(2)}, u32[]{:S(2)}) collective-permute-start(bf16[4,1088,128]{2,1,0:T(8,128)(2,1)S(1)} %shard_map.37.rest_0_._), channel_id=1, source_target_pairs={{0,64},{8,72},{16,80},{24,88},{32,96},{40,104},{48,112},{56,120},{... | collective-permute-start | bytes 3342344 | tf_op jit(solution)/shard_map/ppermute | solution.py:27
  9.9 2.0 shard_map.39.own._
  13.5 2.9 %shard_map.41.own._ = bf16[96,32,128]{2,1,0:T(8,128)(2,1)S(1)} custom-call(s32[8]{0:T(128)S(1)} %iota_xor_fusion.order, bf16[4,128,32,128]{3,2,1,0:T(8,128)(2,1)} %w.9, f32[4,4,128,128]{3,2,1,0:T(8,128)S(1)} %copy-done, bf16[64,32,128]{2,1,0:T(8,128)(2,1)S(1)} %shard_map.39.own._), custom_call_target="tpu_custom_call" | custom-call | tf_op jit(solution)/shard_map/pallas_call | solution.py:69
  17.1 2.9 %shard_map.43.own = bf16[96,32,128]{2,1,0:T(8,128)(2,1)S(1)} custom-call(s32[8]{0:T(128)S(1)} %iota_xor_fusion.order, bf16[4,128,32,128]{3,2,1,0:T(8,128)(2,1)} %w.9, f32[4,4,128,128]{3,2,1,0:T(8,128)S(1)} %copy-done, bf16[96,32,128]{2,1,0:T(8,128)(2,1)S(1)} %shard_map.41.own._), custom_call_target="tpu_custom_call" | custom-call | tf_op jit(solution)/shard_map/pallas_call | solution.py:69
  21.6 5.3 %collective-permute-done.1.other = bf16[64,32,128]{2,1,0:T(8,128)(2,1)S(1)} collective-permute-done((bf16[64,32,128]{2,1,0:T(8,128)(2,1)S(1)}, bf16[64,32,128]{2,1,0:T(8,128)(2,1)S(1)}, u32[]{:S(2)}, u32[]{:S(2)}) %collective-permute-start.1) | collective-permute-done | bytes 524320 | tf_op jit(solution)/shard_map/ppermute | solution.py:27
  29.0 3.2 %shard_map.38.near = bf16[4,1088,128]{2,1,0:T(8,128)(2,1)S(1)} custom-call(s32[8]{0:T(128)S(1)} %iota_xor_fusion.order, bf16[4,128,32,128]{3,2,1,0:T(8,128)(2,1)} %w.9, f32[4,4,128,128]{3,2,1,0:T(8,128)S(1)} %copy-done, bf16[4,1088,128]{2,1,0:T(8,128)(2,1)S(1)} %shard_map.37.rest_0_._), custom_call_target="tpu_custom_call" | custom-call | bytes 8912896 | tf_op jit(solution)/shard_map/pallas_call | solution.py:69
  32.3 11.5 %collective-permute-done.2.other = bf16[96,32,128]{2,1,0:T(8,128)(2,1)S(1)} collective-permute-done((bf16[96,32,128]{2,1,0:T(8,128)(2,1)S(1)}, bf16[96,32,128]{2,1,0:T(8,128)(2,1)S(1)}, u32[]{:S(2)}, u32[]{:S(2)}) %collective-permute-start.2) | collective-permute-done | bytes 786464 | tf_op jit(solution)/shard_map/ppermute | solution.py:27
  43.7 1.9 shard_map.42.rest_0_.rest_1_.own
  45.7 13.4 %collective-permute-done.3.other = bf16[96,32,128]{2,1,0:T(8,128)(2,1)S(1)} collective-permute-done((bf16[96,32,128]{2,1,0:T(8,128)(2,1)S(1)}, bf16[96,32,128]{2,1,0:T(8,128)(2,1)S(1)}, u32[]{:S(2)}, u32[]{:S(2)}) %collective-permute-start.3) | collective-permute-done | bytes 786464 | tf_op jit(solution)/shard_map/ppermute | solution.py:27
  61.1 9.7 %collective-permute-done.far = bf16[4,1088,128]{2,1,0:T(8,128)(2,1)S(1)} collective-permute-done((bf16[4,1088,128]{2,1,0:T(8,128)(2,1)S(1)}, bf16[4,1088,128]{2,1,0:T(8,128)(2,1)S(1)}, u32[]{:S(2)}, u32[]{:S(2)}) %collective-permute-start) | collective-permute-done | bytes 1114144 | tf_op jit(solution)/shard_map/ppermute | solution.py:27
  71.4 3.1 %collective-permute-start.4 = (bf16[2,1088,128]{2,1,0:T(8,128)(2,1)S(1)}, bf16[2,1088,128]{2,1,0:T(8,128)(2,1)S(1)}, u32[]{:S(2)}, u32[]{:S(2)}) collective-permute-start(bf16[2,1088,128]{2,1,0:T(8,128)(2,1)S(1)} %get-tuple-element.12), channel_id=1, source_target_pairs={{0,4},{1,5},{2,6},{3,7},{4,0},{5,1},{6,2},{7,3},{8,12},{9,13},{10,... | collective-permute-start | bytes 1671176 | tf_op jit(solution)/shard_map/ppermute | solution.py:29
  75.7 5.2 %collective-permute-start.11 = (bf16[96,32,128]{2,1,0:T(8,128)(2,1)S(1)}, bf16[96,32,128]{2,1,0:T(8,128)(2,1)S(1)}, u32[]{:S(2)}, u32[]{:S(2)}) collective-permute-start(bf16[96,32,128]{2,1,0:T(8,128)(2,1)S(1)} %shard_map.42.rest_0_.rest_1_.own), channel_id=1, source_target_pairs={{0,64},{8,72},{16,80},{24,88},{32,96},{40,104},{48,112},{56,120},{... | collective-permute-start | bytes 2359304 | tf_op jit(solution)/shard_map/ppermute | solution.py:27
  82.1 5.1 %collective-permute-start.14 = (bf16[96,32,128]{2,1,0:T(8,128)(2,1)S(1)}, bf16[96,32,128]{2,1,0:T(8,128)(2,1)S(1)}, u32[]{:S(2)}, u32[]{:S(2)}) collective-permute-start(bf16[96,32,128]{2,1,0:T(8,128)(2,1)S(1)} %shard_map.44.rest_2_.own), channel_id=1, source_target_pairs={{0,64},{8,72},{16,80},{24,88},{32,96},{40,104},{48,112},{56,120},{... | collective-permute-start | bytes 2359304 | tf_op jit(solution)/shard_map/ppermute | solution.py:27
  88.7 3.1 %collective-permute-start.12 = (bf16[64,32,128]{2,1,0:T(8,128)(2,1)S(1)}, bf16[64,32,128]{2,1,0:T(8,128)(2,1)S(1)}, u32[]{:S(2)}, u32[]{:S(2)}) collective-permute-start(bf16[64,32,128]{2,1,0:T(8,128)(2,1)S(1)} %shard_map.46.rest_0_.own), channel_id=1, source_target_pairs={{0,4},{1,5},{2,6},{3,7},{4,0},{5,1},{6,2},{7,3},{8,12},{9,13},{10,... | collective-permute-start | bytes 1572872 | tf_op jit(solution)/shard_map/ppermute | solution.py:29
  91.8 8.8 %collective-permute-done.5.two = bf16[2,1088,128]{2,1,0:T(8,128)(2,1)S(1)} collective-permute-done((bf16[2,1088,128]{2,1,0:T(8,128)(2,1)S(1)}, bf16[2,1088,128]{2,1,0:T(8,128)(2,1)S(1)}, u32[]{:S(2)}, u32[]{:S(2)}) %collective-permute-start.5) | collective-permute-done | bytes 557088 | tf_op jit(solution)/shard_map/ppermute | solution.py:27
  100.7 4.8 %shard_map.47 = (bf16[2,1024,128]{2,1,0:T(8,128)(2,1)S(1)}, bf16[2,1024,128]{2,1,0:T(8,128)(2,1)S(1)}, bf16[2,1024,128]{2,1,0:T(8,128)(2,1)S(1)}, bf16[2,1024,128]{2,1,0:T(8,128)(2,1)S(1)}) custom-call(s32[8]{0:T(128)S(1)} %iota_xor_fusion.order, bf16[4,1088,128]{2,1,0:T(8,128)(2,1)S(1)} %shard_map.38.near, bf16[4,1088,128]{2,1,0:T(8,128)(2,1)} %copy-done.3, ...), custom_call_target="tpu_custom_call" | custom-call | flops 6442450944 | bytes 16777216 | tf_op jit(solution)/shard_map/pallas_call | solution.py:69
  105.4 2.7 %collective-permute-start.10 = (bf16[2,1024,128]{2,1,0:T(8,128)(2,1)S(1)}, bf16[2,1024,128]{2,1,0:T(8,128)(2,1)S(1)}, u32[]{:S(2)}, u32[]{:S(2)}) collective-permute-start(bf16[2,1024,128]{2,1,0:T(8,128)(2,1)S(1)} %get-tuple-element.18), channel_id=1, source_target_pairs={{0,132},{1,133},{2,134},{3,135},{4,128},{5,129},{6,130},{7,131},{8... | collective-permute-start | bytes 1572872 | tf_op jit(solution)/shard_map/ppermute | solution.py:34
  110.8 2.2 %shard_map.49.rest_1_.rest_0_ = bf16[4,128,32,128]{3,2,1,0:T(8,128)(2,1)} custom-call(s32[8]{0:T(128)S(1)} %iota_xor_fusion.order, bf16[64,32,128]{2,1,0:T(8,128)(2,1)S(1)} %shard_map.46.rest_0_.own, bf16[64,32,128]{2,1,0:T(8,128)(2,1)S(1)} %collective-permute-done.12.other, bf16[3,2,2,128,128]{4,3,2,1,0:T(8,128)(2,1)S(1)} %copy-done.2, ...), custom_call_target="tpu_custom_call" | custom-call | flops 1073741824 | bytes 6291456 | tf_op jit(solution)/shard_map/pallas_call | solution.py:69
  113.1 1.9 shard_map.48.rest_0_.own
  115.0 2.7 %collective-permute-start.16 = (bf16[96,32,128]{2,1,0:T(8,128)(2,1)S(1)}, bf16[96,32,128]{2,1,0:T(8,128)(2,1)S(1)}, u32[]{:S(2)}, u32[]{:S(2)}) collective-permute-start(bf16[96,32,128]{2,1,0:T(8,128)(2,1)S(1)} %shard_map.48.rest_0_.own), channel_id=1, source_target_pairs={{0,4},{1,5},{2,6},{3,7},{4,0},{5,1},{6,2},{7,3},{8,12},{9,13},{10,... | collective-permute-start | bytes 2359304 | tf_op jit(solution)/shard_map/ppermute | solution.py:29
  117.7 14.1 %collective-permute-done.10.d.refs_3_ = bf16[2,1024,128]{2,1,0:T(8,128)(2,1)S(1)} collective-permute-done((bf16[2,1024,128]{2,1,0:T(8,128)(2,1)S(1)}, bf16[2,1024,128]{2,1,0:T(8,128)(2,1)S(1)}, u32[]{:S(2)}, u32[]{:S(2)}) %collective-permute-start.10) | collective-permute-done | bytes 524320 | tf_op jit(solution)/shard_map/ppermute | solution.py:34
  134.3 5.2 %collective-permute-start.13 = (bf16[4,1024,128]{2,1,0:T(8,128)(2,1)S(1)}, bf16[4,1024,128]{2,1,0:T(8,128)(2,1)S(1)}, u32[]{:S(2)}, u32[]{:S(2)}) collective-permute-start(bf16[4,1024,128]{2,1,0:T(8,128)(2,1)S(1)} %shard_map.50), channel_id=1, source_target_pairs={{0,64},{8,72},{16,80},{24,88},{32,96},{40,104},{48,112},{56,120},{... | collective-permute-start | bytes 3145736 | tf_op jit(solution)/shard_map/ppermute | solution.py:27
  139.5 2.0 shard_map.51.own
  141.5 2.9 %collective-permute-start.15 = (bf16[96,32,128]{2,1,0:T(8,128)(2,1)S(1)}, bf16[96,32,128]{2,1,0:T(8,128)(2,1)S(1)}, u32[]{:S(2)}, u32[]{:S(2)}) collective-permute-start(bf16[96,32,128]{2,1,0:T(8,128)(2,1)S(1)} %shard_map.51.own), channel_id=1, source_target_pairs={{0,4},{1,5},{2,6},{3,7},{4,0},{5,1},{6,2},{7,3},{8,12},{9,13},{10,... | collective-permute-start | bytes 2359304 | tf_op jit(solution)/shard_map/ppermute | solution.py:29
  144.4 8.1 %collective-permute-done.16.other = bf16[96,32,128]{2,1,0:T(8,128)(2,1)S(1)} collective-permute-done((bf16[96,32,128]{2,1,0:T(8,128)(2,1)S(1)}, bf16[96,32,128]{2,1,0:T(8,128)(2,1)S(1)}, u32[]{:S(2)}, u32[]{:S(2)}) %collective-permute-start.16) | collective-permute-done | bytes 786464 | tf_op jit(solution)/shard_map/ppermute | solution.py:29
  152.5 2.9 %shard_map.52.rest_0_ = bf16[4,128,32,128]{3,2,1,0:T(8,128)(2,1)} custom-call(s32[8]{0:T(128)S(1)} %iota_xor_fusion.order, bf16[96,32,128]{2,1,0:T(8,128)(2,1)S(1)} %shard_map.48.rest_0_.own, bf16[96,32,128]{2,1,0:T(8,128)(2,1)S(1)} %collective-permute-done.16.other, bf16[3,2,2,128,128]{4,3,2,1,0:T(8,128)(2,1)S(1)} %copy-done.2, ...), custom_call_target="tpu_custom_call", output_to_operand_aliasing={{}: (5, {})} | custom-call | flops 1610612736 | bytes 9437184 | tf_op jit(solution)/shard_map/pallas_call | solution.py:69
  155.5 12.6 %collective-permute-done.15.other = bf16[96,32,128]{2,1,0:T(8,128)(2,1)S(1)} collective-permute-done((bf16[96,32,128]{2,1,0:T(8,128)(2,1)S(1)}, bf16[96,32,128]{2,1,0:T(8,128)(2,1)S(1)}, u32[]{:S(2)}, u32[]{:S(2)}) %collective-permute-start.15) | collective-permute-done | bytes 786464 | tf_op jit(solution)/shard_map/ppermute | solution.py:29
  168.1 2.9 %shard_map.53.refs_5_ = bf16[4,128,32,128]{3,2,1,0:T(8,128)(2,1)} custom-call(s32[8]{0:T(128)S(1)} %iota_xor_fusion.order, bf16[96,32,128]{2,1,0:T(8,128)(2,1)S(1)} %shard_map.51.own, bf16[96,32,128]{2,1,0:T(8,128)(2,1)S(1)} %collective-permute-done.15.other, bf16[3,2,2,128,128]{4,3,2,1,0:T(8,128)(2,1)S(1)} %copy-done.2, ...), custom_call_target="tpu_custom_call", output_to_operand_aliasing={{}: (5, {})} | custom-call | flops 1610612736 | bytes 9437184 | tf_op jit(solution)/shard_map/pallas_call | solution.py:69
  171.0 2.7 %shard_map.54.refs_2_ = bf16[4,128,32,128]{3,2,1,0:T(8,128)(2,1)} custom-call(s32[8]{0:T(128)S(1)} %iota_xor_fusion.order, bf16[2,1024,128]{2,1,0:T(8,128)(2,1)S(1)} %get-tuple-element.15.a.refs_0_, bf16[2,1024,128]{2,1,0:T(8,128)(2,1)S(1)} %collective-permute-done.8.b.refs_1_, ...), custom_call_target="tpu_custom_call", output_to_operand_aliasing={{}: (6, {})} | custom-call | bytes 8388608 | tf_op jit(solution)/shard_map/pallas_call | solution.py:69
  173.7 24.1 %collective-permute-done.13.refs_0_ = bf16[4,1024,128]{2,1,0:T(8,128)(2,1)S(1)} collective-permute-done((bf16[4,1024,128]{2,1,0:T(8,128)(2,1)S(1)}, bf16[4,1024,128]{2,1,0:T(8,128)(2,1)S(1)}, u32[]{:S(2)}, u32[]{:S(2)}) %collective-permute-start.13) | collective-permute-done | bytes 1048608 | tf_op jit(solution)/shard_map/ppermute | solution.py:27
  197.9 2.7 %shard_map.55 = bf16[4,128,32,128]{3,2,1,0:T(8,128)(2,1)} custom-call(s32[8]{0:T(128)S(1)} %iota_xor_fusion.order, bf16[4,1024,128]{2,1,0:T(8,128)(2,1)S(1)} %collective-permute-done.13.refs_0_, f32[4,4,128,128]{3,2,1,0:T(8,128)S(1)} %copy-done.1, bf16[4,128,32,128]{3,2,1,0:T(8,128)(2,1)} %shard_map.54.refs_2_), custom_call_target="tpu_custom_call", output_to_operand_aliasing={{}: (3, {})} | custom-call | bytes 8388608 | tf_op jit(solution)/shard_map/pallas_call | solution.py:69
  (30 shorter events, 18.9 us)
Async XLA Ops:
  0.0 1.2 copy-start
  4.5 66.3 %collective-permute-start = (bf16[4,1088,128]{2,1,0:T(8,128)(2,1)S(1)}, bf16[4,1088,128]{2,1,0:T(8,128)(2,1)S(1)}, u32[]{:S(2)}, u32[]{:S(2)}) collective-permute-start(bf16[4,1088,128]{2,1,0:T(8,128)(2,1)S(1)} %shard_map.37.rest_0_._), channel_id=1, source_target_pairs={{0,64},{8,72},{16,80},{24,88},{32,96},{40,104},{48,112},{56,120},{... | collective-permute-start | bytes 3342344 | tf_op jit(solution)/shard_map/ppermute | solution.py:27
  11.9 14.9 %collective-permute-start.1 = (bf16[64,32,128]{2,1,0:T(8,128)(2,1)S(1)}, bf16[64,32,128]{2,1,0:T(8,128)(2,1)S(1)}, u32[]{:S(2)}, u32[]{:S(2)}) collective-permute-start(bf16[64,32,128]{2,1,0:T(8,128)(2,1)S(1)} %shard_map.39.own._), channel_id=1, source_target_pairs={{0,128},{8,136},{16,144},{24,152},{32,160},{40,168},{48,176},{56,1... | collective-permute-start | bytes 1572872 | tf_op jit(solution)/shard_map/ppermute | solution.py:27
  16.4 10.4 %copy-start.2 = (bf16[3,2,2,128,128]{4,3,2,1,0:T(8,128)(2,1)S(1)}, bf16[3,2,2,128,128]{4,3,2,1,0:T(8,128)(2,1)}, u32[]{:S(2)}) copy-start(bf16[3,2,2,128,128]{4,3,2,1,0:T(8,128)(2,1)} %maps.19) | copy-start | bytes 1179652
  16.4 27.3 %collective-permute-start.2 = (bf16[96,32,128]{2,1,0:T(8,128)(2,1)S(1)}, bf16[96,32,128]{2,1,0:T(8,128)(2,1)S(1)}, u32[]{:S(2)}, u32[]{:S(2)}) collective-permute-start(bf16[96,32,128]{2,1,0:T(8,128)(2,1)S(1)} %shard_map.41.own._), channel_id=1, source_target_pairs={{0,128},{8,136},{16,144},{24,152},{32,160},{40,168},{48,176},{56,1... | collective-permute-start | bytes 2359304 | tf_op jit(solution)/shard_map/ppermute | solution.py:27
  20.0 39.1 %collective-permute-start.3 = (bf16[96,32,128]{2,1,0:T(8,128)(2,1)S(1)}, bf16[96,32,128]{2,1,0:T(8,128)(2,1)S(1)}, u32[]{:S(2)}, u32[]{:S(2)}) collective-permute-start(bf16[96,32,128]{2,1,0:T(8,128)(2,1)S(1)} %shard_map.43.own), channel_id=1, source_target_pairs={{0,128},{8,136},{16,144},{24,152},{32,160},{40,168},{48,176},{56,1... | collective-permute-start | bytes 2359304 | tf_op jit(solution)/shard_map/ppermute | solution.py:27
  28.4 53.7 %collective-permute-start.7 = (bf16[64,32,128]{2,1,0:T(8,128)(2,1)S(1)}, bf16[64,32,128]{2,1,0:T(8,128)(2,1)S(1)}, u32[]{:S(2)}, u32[]{:S(2)}) collective-permute-start(bf16[64,32,128]{2,1,0:T(8,128)(2,1)S(1)} %shard_map.40.rest_0_.own), channel_id=1, source_target_pairs={{0,64},{8,72},{16,80},{24,88},{32,96},{40,104},{48,112},{56,120},{... | collective-permute-start | bytes 1572872 | tf_op jit(solution)/shard_map/ppermute | solution.py:27
  45.7 41.5 %copy-start.1 = (f32[4,4,128,128]{3,2,1,0:T(8,128)S(1)}, f32[4,4,128,128]{3,2,1,0:T(8,128)}, u32[]{:S(2)}) copy-start(f32[4,4,128,128]{3,2,1,0:T(8,128)} %refs_1_.1) | copy-start | bytes 3145732
  70.8 29.9 %copy-start.3 = (bf16[4,1088,128]{2,1,0:T(8,128)(2,1)}, bf16[4,1088,128]{2,1,0:T(8,128)(2,1)S(1)}, u32[]{:S(2)}) copy-start(bf16[4,1088,128]{2,1,0:T(8,128)(2,1)S(1)} %collective-permute-done.far) | copy-start | bytes 3342340
  71.4 17.3 %collective-permute-start.4 = (bf16[2,1088,128]{2,1,0:T(8,128)(2,1)S(1)}, bf16[2,1088,128]{2,1,0:T(8,128)(2,1)S(1)}, u32[]{:S(2)}, u32[]{:S(2)}) collective-permute-start(bf16[2,1088,128]{2,1,0:T(8,128)(2,1)S(1)} %get-tuple-element.12), channel_id=1, source_target_pairs={{0,4},{1,5},{2,6},{3,7},{4,0},{5,1},{6,2},{7,3},{8,12},{9,13},{10,... | collective-permute-start | bytes 1671176 | tf_op jit(solution)/shard_map/ppermute | solution.py:29
  74.5 26.1 %collective-permute-start.5 = (bf16[2,1088,128]{2,1,0:T(8,128)(2,1)S(1)}, bf16[2,1088,128]{2,1,0:T(8,128)(2,1)S(1)}, u32[]{:S(2)}, u32[]{:S(2)}) collective-permute-start(bf16[2,1088,128]{2,1,0:T(8,128)(2,1)S(1)} %get-tuple-element.13), channel_id=1, source_target_pairs={{0,128},{8,136},{16,144},{24,152},{32,160},{40,168},{48,176},{56,1... | collective-permute-start | bytes 1671176 | tf_op jit(solution)/shard_map/ppermute | solution.py:27
  75.1 25.5 %collective-permute-start.6 = (bf16[2,1088,128]{2,1,0:T(8,128)(2,1)S(1)}, bf16[2,1088,128]{2,1,0:T(8,128)(2,1)S(1)}, u32[]{:S(2)}, u32[]{:S(2)}) collective-permute-start(bf16[2,1088,128]{2,1,0:T(8,128)(2,1)S(1)} %get-tuple-element.14), channel_id=1, source_target_pairs={{0,132},{1,133},{2,134},{3,135},{4,128},{5,129},{6,130},{7,131},{8... | collective-permute-start | bytes 1671176 | tf_op jit(solution)/shard_map/ppermute | solution.py:34
  75.7 37.4 %collective-permute-start.11 = (bf16[96,32,128]{2,1,0:T(8,128)(2,1)S(1)}, bf16[96,32,128]{2,1,0:T(8,128)(2,1)S(1)}, u32[]{:S(2)}, u32[]{:S(2)}) collective-permute-start(bf16[96,32,128]{2,1,0:T(8,128)(2,1)S(1)} %shard_map.42.rest_0_.rest_1_.own), channel_id=1, source_target_pairs={{0,64},{8,72},{16,80},{24,88},{32,96},{40,104},{48,112},{56,120},{... | collective-permute-start | bytes 2359304 | tf_op jit(solution)/shard_map/ppermute | solution.py:27
  82.1 57.5 %collective-permute-start.14 = (bf16[96,32,128]{2,1,0:T(8,128)(2,1)S(1)}, bf16[96,32,128]{2,1,0:T(8,128)(2,1)S(1)}, u32[]{:S(2)}, u32[]{:S(2)}) collective-permute-start(bf16[96,32,128]{2,1,0:T(8,128)(2,1)S(1)} %shard_map.44.rest_2_.own), channel_id=1, source_target_pairs={{0,64},{8,72},{16,80},{24,88},{32,96},{40,104},{48,112},{56,120},{... | collective-permute-start | bytes 2359304 | tf_op jit(solution)/shard_map/ppermute | solution.py:27
  88.7 20.5 %collective-permute-start.12 = (bf16[64,32,128]{2,1,0:T(8,128)(2,1)S(1)}, bf16[64,32,128]{2,1,0:T(8,128)(2,1)S(1)}, u32[]{:S(2)}, u32[]{:S(2)}) collective-permute-start(bf16[64,32,128]{2,1,0:T(8,128)(2,1)S(1)} %shard_map.46.rest_0_.own), channel_id=1, source_target_pairs={{0,4},{1,5},{2,6},{3,7},{4,0},{5,1},{6,2},{7,3},{8,12},{9,13},{10,... | collective-permute-start | bytes 1572872 | tf_op jit(solution)/shard_map/ppermute | solution.py:29
  105.4 26.4 %collective-permute-start.10 = (bf16[2,1024,128]{2,1,0:T(8,128)(2,1)S(1)}, bf16[2,1024,128]{2,1,0:T(8,128)(2,1)S(1)}, u32[]{:S(2)}, u32[]{:S(2)}) collective-permute-start(bf16[2,1024,128]{2,1,0:T(8,128)(2,1)S(1)} %get-tuple-element.18), channel_id=1, source_target_pairs={{0,132},{1,133},{2,134},{3,135},{4,128},{5,129},{6,130},{7,131},{8... | collective-permute-start | bytes 1572872 | tf_op jit(solution)/shard_map/ppermute | solution.py:34
  108.1 23.7 %collective-permute-start.8 = (bf16[2,1024,128]{2,1,0:T(8,128)(2,1)S(1)}, bf16[2,1024,128]{2,1,0:T(8,128)(2,1)S(1)}, u32[]{:S(2)}, u32[]{:S(2)}) collective-permute-start(bf16[2,1024,128]{2,1,0:T(8,128)(2,1)S(1)} %get-tuple-element.16), channel_id=1, source_target_pairs={{0,4},{1,5},{2,6},{3,7},{4,0},{5,1},{6,2},{7,3},{8,12},{9,13},{10,... | collective-permute-start | bytes 1572872 | tf_op jit(solution)/shard_map/ppermute | solution.py:29
  109.2 24.5 %collective-permute-start.9 = (bf16[2,1024,128]{2,1,0:T(8,128)(2,1)S(1)}, bf16[2,1024,128]{2,1,0:T(8,128)(2,1)S(1)}, u32[]{:S(2)}, u32[]{:S(2)}) collective-permute-start(bf16[2,1024,128]{2,1,0:T(8,128)(2,1)S(1)} %get-tuple-element.17), channel_id=1, source_target_pairs={{0,128},{8,136},{16,144},{24,152},{32,160},{40,168},{48,176},{56,1... | collective-permute-start | bytes 1572872 | tf_op jit(solution)/shard_map/ppermute | solution.py:27
  115.0 37.5 %collective-permute-start.16 = (bf16[96,32,128]{2,1,0:T(8,128)(2,1)S(1)}, bf16[96,32,128]{2,1,0:T(8,128)(2,1)S(1)}, u32[]{:S(2)}, u32[]{:S(2)}) collective-permute-start(bf16[96,32,128]{2,1,0:T(8,128)(2,1)S(1)} %shard_map.48.rest_0_.own), channel_id=1, source_target_pairs={{0,4},{1,5},{2,6},{3,7},{4,0},{5,1},{6,2},{7,3},{8,12},{9,13},{10,... | collective-permute-start | bytes 2359304 | tf_op jit(solution)/shard_map/ppermute | solution.py:29
  134.3 63.6 %collective-permute-start.13 = (bf16[4,1024,128]{2,1,0:T(8,128)(2,1)S(1)}, bf16[4,1024,128]{2,1,0:T(8,128)(2,1)S(1)}, u32[]{:S(2)}, u32[]{:S(2)}) collective-permute-start(bf16[4,1024,128]{2,1,0:T(8,128)(2,1)S(1)} %shard_map.50), channel_id=1, source_target_pairs={{0,64},{8,72},{16,80},{24,88},{32,96},{40,104},{48,112},{56,120},{... | collective-permute-start | bytes 3145736 | tf_op jit(solution)/shard_map/ppermute | solution.py:27
  141.5 26.6 %collective-permute-start.15 = (bf16[96,32,128]{2,1,0:T(8,128)(2,1)S(1)}, bf16[96,32,128]{2,1,0:T(8,128)(2,1)S(1)}, u32[]{:S(2)}, u32[]{:S(2)}) collective-permute-start(bf16[96,32,128]{2,1,0:T(8,128)(2,1)S(1)} %shard_map.51.own), channel_id=1, source_target_pairs={{0,4},{1,5},{2,6},{3,7},{4,0},{5,1},{6,2},{7,3},{8,12},{9,13},{10,... | collective-permute-start | bytes 2359304 | tf_op jit(solution)/shard_map/ppermute | solution.py:29

commit v4 on v3

--- a/solution.py
+++ b/solution.py
@@ -34,10 +34,13 @@
     return lax.ppermute(block, ("src", "tgt"), route)
 
 
+def my_place():
+    n_src, n_tgt = lax.axis_size("src"), lax.axis_size("tgt")
+    return lax.div(lax.axis_index("src"), n_src // 4) * 2 + lax.div(lax.axis_index("tgt"), n_tgt // 2)
+
+
 def my_order():
-    n_src, n_tgt = lax.axis_size("src"), lax.axis_size("tgt")
-    place = lax.axis_index("src") // (n_src // 4) * 2 + lax.axis_index("tgt") // (n_tgt // 2)
-    return jnp.bitwise_xor(place.astype(jnp.int32), jnp.arange(8, dtype=jnp.int32))
+    return jnp.bitwise_xor(my_place().astype(jnp.int32), jnp.arange(8, dtype=jnp.int32))
 
 
 def roll_half(block):
@@ -65,17 +68,18 @@
     return twist(block.astype(jnp.float32), turned, rows)
 
 
-def call(kernel, out_shape, grid, in_specs, out_specs, args, order, scratch=(), aliases=None, cost=COST, flops=0, nbytes=0):
+def call(kernel, out_shape, grid, in_specs, out_specs, args, order, scratch=(), aliases=None, vmem=VMEM, cost=COST, flops=0, nbytes=0):
+    known = () if order is None else (order,)
     return pl.pallas_call(
         kernel,
         out_shape=out_shape,
         grid_spec=pltpu.PrefetchScalarGridSpec(
-            num_scalar_prefetch=1, grid=grid, in_specs=in_specs, out_specs=out_specs, scratch_shapes=list(scratch)
+            num_scalar_prefetch=len(known), grid=grid, in_specs=in_specs, out_specs=out_specs, scratch_shapes=list(scratch)
         ),
         input_output_aliases=aliases or {},
-        compiler_params=pltpu.CompilerParams(vmem_limit_bytes=VMEM),
+        compiler_params=pltpu.CompilerParams(vmem_limit_bytes=vmem),
         cost_estimate=pl.CostEstimate(flops=cost * flops, bytes_accessed=cost * nbytes, transcendentals=0),
-    )(order, *args)
+    )(*known, *args)
 
 
 def pieces(targets, slots):
@@ -174,38 +178,43 @@
 PLANE = (0, THIRD, FIRST, FIRST | THIRD)
 
 
-def pack_kernel(order, w, t, *rest):
-    out = rest[-1]
-    targets, slots, laws, width = w.shape
-    rows = slots * laws
-    for target in range(targets):
-        block = twist_16(w[target].reshape(rows, width), t[0, target])
-        out[0, target * rows : (target + 1) * rows, :] = block.astype(out.dtype)
-        for later in range(2):
-            start = targets * rows + (later * targets + target) * slots
-            out[0, start : start + slots, :] = t[1 + later, target].astype(out.dtype)
-
-
-def pack(order, weights, twiddles, far, after=()):
+def pack_kernel(*refs):
+    blocks, factors, out = refs[:4], refs[4:8], refs[-1]
+    for i, (w, t) in enumerate(zip(blocks, factors)):
+        targets, slots, laws, width = w.shape
+        rows = slots * laws
+        for target in range(targets):
+            block = twist_16(w[target].reshape(rows, width), t[0, target])
+            out[i, target * rows : (target + 1) * rows, :] = block.astype(out.dtype)
+            for later in range(2):
+                start = targets * rows + (later * targets + target) * slots
+                out[i, start : start + slots, :] = t[1 + later, target].astype(out.dtype)
+
+
+def pack(weights, twiddles, far, after=()):
     _, slots, laws, width = weights.shape
     eighth = slots // 8
     rows = GATHERED * eighth * (laws + 2)
 
-    def which(i, o):
-        return o[lax.div(i, 2) * FIRST + lax.rem(i, 2) * THIRD + far]
+    def weights_of(place):
+        return pl.BlockSpec((GATHERED, eighth, laws, width), lambda i: (0, my_place() ^ place, 0, 0))
+
+    def factors_of(place):
+        return pl.BlockSpec((3, GATHERED, eighth, width), lambda i: (0, 0, my_place() ^ place, 0))
 
     return call(
         pack_kernel,
         jax.ShapeDtypeStruct((4, rows, width), weights.dtype),
-        (4,),
+        (1,),
         [
-            pl.BlockSpec((GATHERED, eighth, laws, width), lambda i, o: (0, which(i, o), 0, 0)),
-            pl.BlockSpec((3, GATHERED, eighth, width), lambda i, o: (0, 0, which(i, o), 0)),
+            *[weights_of(place + far) for place in PLANE],
+            *[factors_of(place + far) for place in PLANE],
             *[pl.BlockSpec(memory_space=pl.ANY)] * len(after),
         ],
-        pl.BlockSpec((1, rows, width), lambda i, o: (i, 0, 0)),
-        (weights, twiddles, *after),
-        order,
+        pl.BlockSpec((4, rows, width), lambda i: (0, 0, 0)),
+        (*[weights] * 4, *[twiddles] * 4, *after),
+        None,
+        vmem=60 * 2**20 if far else VMEM,
         cost=NCOST,
         nbytes=16 * rows * width,
     )
@@ -326,21 +335,21 @@
     )
 
 
-def unpack_kernel(order, *refs):
-    *blocks, t, _, out = refs
-    targets, slots, laws, width = out.shape
-    rows = slots * laws
-
-    def write(block):
+def unpack_kernel(far, order, *refs):
+    blocks, factors, (out, ready, done) = refs[:-8], refs[-8:-4], refs[-3:]
+    copies = []
+    for i, (place, t) in enumerate(zip(PLANE, factors)):
+        targets, slots, laws, width = ready.shape[1:]
+        rows = slots * laws
+        state = blocks[0][i] if len(blocks) == 1 else blocks[i][0]
         for target in range(targets):
-            state = block[0, target * rows : (target + 1) * rows, :]
-            out[target] = twist_16(state, t[0, target]).astype(out.dtype).reshape(out.shape[1:])
-
-    if len(blocks) == 1:
-        write(blocks[0])
-    else:
-        for i, block in enumerate(blocks):
-            pl.when(pl.program_id(0) == i)(functools.partial(write, block))
+            block = twist_16(state[target * rows : (target + 1) * rows, :], t[target])
+            ready[i, target] = block.astype(out.dtype).reshape(slots, laws, width)
+        at = pl.ds(pl.multiple_of(order[place + far] * slots, slots), slots)
+        copies.append(pltpu.make_async_copy(ready.at[i], out.at[pl.ds(0, targets), at], done.at[i]))
+        copies[-1].start()
+    for copy in copies:
+        copy.wait()
 
 
 def unpack(order, blocks, twiddles, whole, far):
@@ -348,26 +357,24 @@
     eighth = slots // 8
     rows = GATHERED * eighth * laws
 
-    def which(i, o):
-        return o[lax.div(i, 2) * FIRST + lax.rem(i, 2) * THIRD + far]
-
-    if len(blocks) == 1:
-        block_specs = [pl.BlockSpec((1, rows, width), lambda i, o: (i, 0, 0))]
-    else:
-        block_specs = [pl.BlockSpec((1, rows, width), lambda i, o: (0, 0, 0))] * 4
-    return call(
-        unpack_kernel,
+    def factors_of(place):
+        return pl.BlockSpec((None, GATHERED, eighth, width), lambda i, o: (3, 0, o[place], 0))
+
+    count = 4 // len(blocks)
+    return call(
+        functools.partial(unpack_kernel, far),
         jax.ShapeDtypeStruct(whole.shape, whole.dtype),
-        (4,),
+        (1,),
         [
-            *block_specs,
-            pl.BlockSpec((1, GATHERED, eighth, width), lambda i, o: (3, 0, which(i, o), 0)),
+            *[pl.BlockSpec((count, rows, width), lambda i, o: (0, 0, 0))] * len(blocks),
+            *[factors_of(place + far) for place in PLANE],
             pl.BlockSpec(memory_space=pl.ANY),
         ],
-        pl.BlockSpec((GATHERED, eighth, laws, width), lambda i, o: (0, which(i, o), 0, 0)),
-        (*blocks, twiddles, whole),
-        order,
-        aliases={len(blocks) + 2: 0},
+        pl.BlockSpec(memory_space=pl.ANY),
+        (*blocks, *[twiddles] * 4, whole),
+        order,
+        scratch=[pltpu.VMEM((4, GATHERED, eighth, laws, width), whole.dtype), pltpu.SemaphoreType.DMA((4,))],
+        aliases={len(blocks) + 5: 0},
         nbytes=16 * rows * width,
     )
 
@@ -375,9 +382,9 @@
 def body(weights_in, twiddles, kernels):
     targets, slots, laws, _ = weights_in.shape
     order = my_order()
-    far_send = pack(order, weights_in, twiddles, SECOND)
+    far_send = pack(weights_in, twiddles, SECOND)
     far = swap(far_send, SECOND)
-    near = pack(order, weights_in, twiddles, 0, [far_send])
+    near = pack(weights_in, twiddles, 0, [far_send])
     cuts = pieces(targets, slots)
     own, after = [None] * len(cuts), far_send
     for i in FIRST_ORDER:

time: 201 us -> 199 us (0.990)
  Pallas kernels: 44.7 us -> 41.1 us
    pallas_call x19, Pallas kernels: 44.7 us -> 41.1 us  [call(): pl.pallas_call(kernel, out_shape=out_shape, grid_spec=pltpu.PrefetchScala...]
  transfers between devices with their start and end apart: 17 -> 17, of which waited for: 12 -> 12; matrix products, arithmetic and copies ran while one was open for 0% -> 0% of each run, Pallas kernels for 19% -> 18%
where the time goes in v4:
time: 199 us; the launch traced here: 198 us
  waiting for transfers between devices  112 us (56%)
  starting transfers between devices  43.5 us (22%)
  Pallas kernels  41.1 us (21%)
    ppermute x10, waiting for transfers between devices, swap(): return lax.ppermute(block, 'src', [(i, i ^ flip_src) for i in range(n_src)])  77.2 us
    pallas_call x19, Pallas kernels, call(): pl.pallas_call(kernel, out_shape=out_shape, grid_spec=pltpu.PrefetchScala...  41.1 us
    ppermute x10, starting transfers between devices, swap(): return lax.ppermute(block, 'src', [(i, i ^ flip_src) for i in range(n_src)])  27.5 us
    ppermute x5, waiting for transfers between devices, swap(): return lax.ppermute(block, 'tgt', [(i, i ^ flip_tgt) for i in range(n_tgt)])  21 us
    ppermute x2, waiting for transfers between devices, swap(): return lax.ppermute(block, ('src', 'tgt'), route)  14 us
    ppermute x5, starting transfers between devices, swap(): return lax.ppermute(block, 'tgt', [(i, i ^ flip_tgt) for i in range(n_tgt)])  12.8 us
  transfers between devices with their start and end apart: 17, of which 12 were waited for; matrix products, arithmetic and copies ran while one was open for 0% of the time, Pallas kernels for 18%

profile of v4, /device:TPU:80, one launch (start us, length us, event | category | flops | bytes accessed | tf_op | source)
XLA Modules:
  0.0 198.4 jit_solution(10268668760710496210)
XLA Ops:
  0.0 2.8 %shard_map.37.refs_8_._ = bf16[4,1088,128]{2,1,0:T(8,128)(2,1)} custom-call(bf16[4,128,32,128]{3,2,1,0:T(8,128)(2,1)} %w.5, bf16[4,128,32,128]{3,2,1,0:T(8,128)(2,1)} %w.5, bf16[4,128,32,128]{3,2,1,0:T(8,128)(2,1)} %w.5, bf16[4,128,32,128]{3,2,1,0:T(8,128)(2,1)} %w.5, f32[4,4,128,128]{3,2,1,0:T(8,128)} %refs_4_.7, f32[4,4,128,128]{3,2,1,0:T(8,128)} %refs_4_.7, ...), custom_call_target="tpu_custom_call" | custom-call | bytes 8912896 | tf_op jit(solution)/shard_map/pallas_call | solution.py:73
  2.8 5.4 %collective-permute-start = (bf16[4,1088,128]{2,1,0:T(8,128)(2,1)}, bf16[4,1088,128]{2,1,0:T(8,128)(2,1)S(1)}, u32[]{:S(2)}, u32[]{:S(2)}) collective-permute-start(bf16[4,1088,128]{2,1,0:T(8,128)(2,1)} %shard_map.37.refs_8_._), channel_id=1, source_target_pairs={{0,64},{8,72},{16,80},{24,88},{32,96},{40,104},{48,112},{56,120},{... | collective-permute-start | bytes 3342344 | tf_op jit(solution)/shard_map/ppermute | solution.py:27
  9.5 2.0 shard_map.39.own._
  13.1 2.9 %shard_map.41.own._ = bf16[96,32,128]{2,1,0:T(8,128)(2,1)S(1)} custom-call(s32[8]{0:T(128)S(1)} %iota_xor_fusion.order, bf16[4,128,32,128]{3,2,1,0:T(8,128)(2,1)} %w.5, f32[4,4,128,128]{3,2,1,0:T(8,128)S(1)} %copy-done, bf16[64,32,128]{2,1,0:T(8,128)(2,1)S(1)} %shard_map.39.own._), custom_call_target="tpu_custom_call" | custom-call | tf_op jit(solution)/shard_map/pallas_call | solution.py:73
  16.7 2.9 %shard_map.43.own = bf16[96,32,128]{2,1,0:T(8,128)(2,1)S(1)} custom-call(s32[8]{0:T(128)S(1)} %iota_xor_fusion.order, bf16[4,128,32,128]{3,2,1,0:T(8,128)(2,1)} %w.5, f32[4,4,128,128]{3,2,1,0:T(8,128)S(1)} %copy-done, bf16[96,32,128]{2,1,0:T(8,128)(2,1)S(1)} %shard_map.41.own._), custom_call_target="tpu_custom_call" | custom-call | tf_op jit(solution)/shard_map/pallas_call | solution.py:73
  21.2 5.3 %collective-permute-done.1.other = bf16[64,32,128]{2,1,0:T(8,128)(2,1)S(1)} collective-permute-done((bf16[64,32,128]{2,1,0:T(8,128)(2,1)S(1)}, bf16[64,32,128]{2,1,0:T(8,128)(2,1)S(1)}, u32[]{:S(2)}, u32[]{:S(2)}) %collective-permute-start.1) | collective-permute-done | bytes 524320 | tf_op jit(solution)/shard_map/ppermute | solution.py:27
  30.4 12.9 %collective-permute-done.2.other = bf16[96,32,128]{2,1,0:T(8,128)(2,1)S(1)} collective-permute-done((bf16[96,32,128]{2,1,0:T(8,128)(2,1)S(1)}, bf16[96,32,128]{2,1,0:T(8,128)(2,1)S(1)}, u32[]{:S(2)}, u32[]{:S(2)}) %collective-permute-start.2) | collective-permute-done | bytes 786464 | tf_op jit(solution)/shard_map/ppermute | solution.py:27
  43.3 1.9 shard_map.42.rest_0_.rest_1_.own
  45.2 13.4 %collective-permute-done.3.other = bf16[96,32,128]{2,1,0:T(8,128)(2,1)S(1)} collective-permute-done((bf16[96,32,128]{2,1,0:T(8,128)(2,1)S(1)}, bf16[96,32,128]{2,1,0:T(8,128)(2,1)S(1)}, u32[]{:S(2)}, u32[]{:S(2)}) %collective-permute-start.3) | collective-permute-done | bytes 786464 | tf_op jit(solution)/shard_map/ppermute | solution.py:27
  58.7 2.0 shard_map.44.rest_2_.own
  60.7 8.6 %collective-permute-done.far = bf16[4,1088,128]{2,1,0:T(8,128)(2,1)S(1)} collective-permute-done((bf16[4,1088,128]{2,1,0:T(8,128)(2,1)}, bf16[4,1088,128]{2,1,0:T(8,128)(2,1)S(1)}, u32[]{:S(2)}, u32[]{:S(2)}) %collective-permute-start) | collective-permute-done | bytes 1114144 | tf_op jit(solution)/shard_map/ppermute | solution.py:27
  69.9 3.1 %collective-permute-start.4 = (bf16[2,1088,128]{2,1,0:T(8,128)(2,1)S(1)}, bf16[2,1088,128]{2,1,0:T(8,128)(2,1)S(1)}, u32[]{:S(2)}, u32[]{:S(2)}) collective-permute-start(bf16[2,1088,128]{2,1,0:T(8,128)(2,1)S(1)} %get-tuple-element.12), channel_id=1, source_target_pairs={{0,4},{1,5},{2,6},{3,7},{4,0},{5,1},{6,2},{7,3},{8,12},{9,13},{10,... | collective-permute-start | bytes 1671176 | tf_op jit(solution)/shard_map/ppermute | solution.py:29
  74.2 5.2 %collective-permute-start.11 = (bf16[96,32,128]{2,1,0:T(8,128)(2,1)S(1)}, bf16[96,32,128]{2,1,0:T(8,128)(2,1)S(1)}, u32[]{:S(2)}, u32[]{:S(2)}) collective-permute-start(bf16[96,32,128]{2,1,0:T(8,128)(2,1)S(1)} %shard_map.42.rest_0_.rest_1_.own), channel_id=1, source_target_pairs={{0,64},{8,72},{16,80},{24,88},{32,96},{40,104},{48,112},{56,120},{... | collective-permute-start | bytes 2359304 | tf_op jit(solution)/shard_map/ppermute | solution.py:27
  80.5 5.1 %collective-permute-start.14 = (bf16[96,32,128]{2,1,0:T(8,128)(2,1)S(1)}, bf16[96,32,128]{2,1,0:T(8,128)(2,1)S(1)}, u32[]{:S(2)}, u32[]{:S(2)}) collective-permute-start(bf16[96,32,128]{2,1,0:T(8,128)(2,1)S(1)} %shard_map.44.rest_2_.own), channel_id=1, source_target_pairs={{0,64},{8,72},{16,80},{24,88},{32,96},{40,104},{48,112},{56,120},{... | collective-permute-start | bytes 2359304 | tf_op jit(solution)/shard_map/ppermute | solution.py:27
  87.2 3.1 %collective-permute-start.12 = (bf16[64,32,128]{2,1,0:T(8,128)(2,1)S(1)}, bf16[64,32,128]{2,1,0:T(8,128)(2,1)S(1)}, u32[]{:S(2)}, u32[]{:S(2)}) collective-permute-start(bf16[64,32,128]{2,1,0:T(8,128)(2,1)S(1)} %shard_map.46.rest_0_.own), channel_id=1, source_target_pairs={{0,4},{1,5},{2,6},{3,7},{4,0},{5,1},{6,2},{7,3},{8,12},{9,13},{10,... | collective-permute-start | bytes 1572872 | tf_op jit(solution)/shard_map/ppermute | solution.py:29
  90.3 8.8 %collective-permute-done.5.two = bf16[2,1088,128]{2,1,0:T(8,128)(2,1)S(1)} collective-permute-done((bf16[2,1088,128]{2,1,0:T(8,128)(2,1)S(1)}, bf16[2,1088,128]{2,1,0:T(8,128)(2,1)S(1)}, u32[]{:S(2)}, u32[]{:S(2)}) %collective-permute-start.5) | collective-permute-done | bytes 557088 | tf_op jit(solution)/shard_map/ppermute | solution.py:27
  99.1 4.8 %shard_map.47 = (bf16[2,1024,128]{2,1,0:T(8,128)(2,1)S(1)}, bf16[2,1024,128]{2,1,0:T(8,128)(2,1)S(1)}, bf16[2,1024,128]{2,1,0:T(8,128)(2,1)S(1)}, bf16[2,1024,128]{2,1,0:T(8,128)(2,1)S(1)}) custom-call(s32[8]{0:T(128)S(1)} %iota_xor_fusion.order, bf16[4,1088,128]{2,1,0:T(8,128)(2,1)S(1)} %shard_map.38.near, bf16[4,1088,128]{2,1,0:T(8,128)(2,1)} %copy-done.4, ...), custom_call_target="tpu_custom_call" | custom-call | flops 6442450944 | bytes 16777216 | tf_op jit(solution)/shard_map/pallas_call | solution.py:73
  103.9 2.7 %collective-permute-start.10 = (bf16[2,1024,128]{2,1,0:T(8,128)(2,1)S(1)}, bf16[2,1024,128]{2,1,0:T(8,128)(2,1)S(1)}, u32[]{:S(2)}, u32[]{:S(2)}) collective-permute-start(bf16[2,1024,128]{2,1,0:T(8,128)(2,1)S(1)} %get-tuple-element.18), channel_id=1, source_target_pairs={{0,132},{1,133},{2,134},{3,135},{4,128},{5,129},{6,130},{7,131},{8... | collective-permute-start | bytes 1572872 | tf_op jit(solution)/shard_map/ppermute | solution.py:34
  109.3 2.3 %shard_map.49.rest_1_.rest_0_ = bf16[4,128,32,128]{3,2,1,0:T(8,128)(2,1)} custom-call(s32[8]{0:T(128)S(1)} %iota_xor_fusion.order, bf16[64,32,128]{2,1,0:T(8,128)(2,1)S(1)} %shard_map.46.rest_0_.own, bf16[64,32,128]{2,1,0:T(8,128)(2,1)S(1)} %collective-permute-done.12.other, bf16[3,2,2,128,128]{4,3,2,1,0:T(8,128)(2,1)S(1)} %copy-done.3, ...), custom_call_target="tpu_custom_call" | custom-call | flops 1073741824 | bytes 6291456 | tf_op jit(solution)/shard_map/pallas_call | solution.py:73
  111.6 1.9 shard_map.48.rest_0_.own
  113.5 2.7 %collective-permute-start.16 = (bf16[96,32,128]{2,1,0:T(8,128)(2,1)S(1)}, bf16[96,32,128]{2,1,0:T(8,128)(2,1)S(1)}, u32[]{:S(2)}, u32[]{:S(2)}) collective-permute-start(bf16[96,32,128]{2,1,0:T(8,128)(2,1)S(1)} %shard_map.48.rest_0_.own), channel_id=1, source_target_pairs={{0,4},{1,5},{2,6},{3,7},{4,0},{5,1},{6,2},{7,3},{8,12},{9,13},{10,... | collective-permute-start | bytes 2359304 | tf_op jit(solution)/shard_map/ppermute | solution.py:29
  116.3 14.0 %collective-permute-done.10.d.refs_3_ = bf16[2,1024,128]{2,1,0:T(8,128)(2,1)S(1)} collective-permute-done((bf16[2,1024,128]{2,1,0:T(8,128)(2,1)S(1)}, bf16[2,1024,128]{2,1,0:T(8,128)(2,1)S(1)}, u32[]{:S(2)}, u32[]{:S(2)}) %collective-permute-start.10) | collective-permute-done | bytes 524320 | tf_op jit(solution)/shard_map/ppermute | solution.py:34
  130.2 1.9 collective-permute-done.9.c.refs_2_
  132.8 5.2 %collective-permute-start.13 = (bf16[4,1024,128]{2,1,0:T(8,128)(2,1)S(1)}, bf16[4,1024,128]{2,1,0:T(8,128)(2,1)S(1)}, u32[]{:S(2)}, u32[]{:S(2)}) collective-permute-start(bf16[4,1024,128]{2,1,0:T(8,128)(2,1)S(1)} %shard_map.50), channel_id=1, source_target_pairs={{0,64},{8,72},{16,80},{24,88},{32,96},{40,104},{48,112},{56,120},{... | collective-permute-start | bytes 3145736 | tf_op jit(solution)/shard_map/ppermute | solution.py:27
  138.0 2.0 shard_map.51.own
  140.0 2.9 %collective-permute-start.15 = (bf16[96,32,128]{2,1,0:T(8,128)(2,1)S(1)}, bf16[96,32,128]{2,1,0:T(8,128)(2,1)S(1)}, u32[]{:S(2)}, u32[]{:S(2)}) collective-permute-start(bf16[96,32,128]{2,1,0:T(8,128)(2,1)S(1)} %shard_map.51.own), channel_id=1, source_target_pairs={{0,4},{1,5},{2,6},{3,7},{4,0},{5,1},{6,2},{7,3},{8,12},{9,13},{10,... | collective-permute-start | bytes 2359304 | tf_op jit(solution)/shard_map/ppermute | solution.py:29
  142.9 8.1 %collective-permute-done.16.other = bf16[96,32,128]{2,1,0:T(8,128)(2,1)S(1)} collective-permute-done((bf16[96,32,128]{2,1,0:T(8,128)(2,1)S(1)}, bf16[96,32,128]{2,1,0:T(8,128)(2,1)S(1)}, u32[]{:S(2)}, u32[]{:S(2)}) %collective-permute-start.16) | collective-permute-done | bytes 786464 | tf_op jit(solution)/shard_map/ppermute | solution.py:29
  151.0 2.9 %shard_map.52.rest_0_ = bf16[4,128,32,128]{3,2,1,0:T(8,128)(2,1)} custom-call(s32[8]{0:T(128)S(1)} %iota_xor_fusion.order, bf16[96,32,128]{2,1,0:T(8,128)(2,1)S(1)} %shard_map.48.rest_0_.own, bf16[96,32,128]{2,1,0:T(8,128)(2,1)S(1)} %collective-permute-done.16.other, bf16[3,2,2,128,128]{4,3,2,1,0:T(8,128)(2,1)S(1)} %copy-done.3, ...), custom_call_target="tpu_custom_call", output_to_operand_aliasing={{}: (5, {})} | custom-call | flops 1610612736 | bytes 9437184 | tf_op jit(solution)/shard_map/pallas_call | solution.py:73
  153.9 12.6 %collective-permute-done.15.other = bf16[96,32,128]{2,1,0:T(8,128)(2,1)S(1)} collective-permute-done((bf16[96,32,128]{2,1,0:T(8,128)(2,1)S(1)}, bf16[96,32,128]{2,1,0:T(8,128)(2,1)S(1)}, u32[]{:S(2)}, u32[]{:S(2)}) %collective-permute-start.15) | collective-permute-done | bytes 786464 | tf_op jit(solution)/shard_map/ppermute | solution.py:29
  166.5 2.9 %shard_map.53.refs_8_ = bf16[4,128,32,128]{3,2,1,0:T(8,128)(2,1)} custom-call(s32[8]{0:T(128)S(1)} %iota_xor_fusion.order, bf16[96,32,128]{2,1,0:T(8,128)(2,1)S(1)} %shard_map.51.own, bf16[96,32,128]{2,1,0:T(8,128)(2,1)S(1)} %collective-permute-done.15.other, bf16[3,2,2,128,128]{4,3,2,1,0:T(8,128)(2,1)S(1)} %copy-done.3, ...), custom_call_target="tpu_custom_call", output_to_operand_aliasing={{}: (5, {})} | custom-call | flops 1610612736 | bytes 9437184 | tf_op jit(solution)/shard_map/pallas_call | solution.py:73
  169.5 1.8 shard_map.54.refs_5_
  171.3 25.1 %collective-permute-done.13.refs_0_ = bf16[4,1024,128]{2,1,0:T(8,128)(2,1)S(1)} collective-permute-done((bf16[4,1024,128]{2,1,0:T(8,128)(2,1)S(1)}, bf16[4,1024,128]{2,1,0:T(8,128)(2,1)S(1)}, u32[]{:S(2)}, u32[]{:S(2)}) %collective-permute-start.13) | collective-permute-done | bytes 1048608 | tf_op jit(solution)/shard_map/ppermute | solution.py:27
  (32 shorter events, 18.7 us)
Async XLA Ops:
  0.0 8.2 %copy-start = (f32[4,4,128,128]{3,2,1,0:T(8,128)S(1)}, f32[4,4,128,128]{3,2,1,0:T(8,128)}, u32[]{:S(2)}) copy-start(f32[4,4,128,128]{3,2,1,0:T(8,128)} %refs_4_.7) | copy-start | bytes 3145732
  2.8 66.4 %collective-permute-start = (bf16[4,1088,128]{2,1,0:T(8,128)(2,1)}, bf16[4,1088,128]{2,1,0:T(8,128)(2,1)S(1)}, u32[]{:S(2)}, u32[]{:S(2)}) collective-permute-start(bf16[4,1088,128]{2,1,0:T(8,128)(2,1)} %shard_map.37.refs_8_._), channel_id=1, source_target_pairs={{0,64},{8,72},{16,80},{24,88},{32,96},{40,104},{48,112},{56,120},{... | collective-permute-start | bytes 3342344 | tf_op jit(solution)/shard_map/ppermute | solution.py:27
  8.2 1.3 copy-start.1
  11.5 14.9 %collective-permute-start.1 = (bf16[64,32,128]{2,1,0:T(8,128)(2,1)S(1)}, bf16[64,32,128]{2,1,0:T(8,128)(2,1)S(1)}, u32[]{:S(2)}, u32[]{:S(2)}) collective-permute-start(bf16[64,32,128]{2,1,0:T(8,128)(2,1)S(1)} %shard_map.39.own._), channel_id=1, source_target_pairs={{0,128},{8,136},{16,144},{24,152},{32,160},{40,168},{48,176},{56,1... | collective-permute-start | bytes 1572872 | tf_op jit(solution)/shard_map/ppermute | solution.py:27
  16.0 10.4 %copy-start.3 = (bf16[3,2,2,128,128]{4,3,2,1,0:T(8,128)(2,1)S(1)}, bf16[3,2,2,128,128]{4,3,2,1,0:T(8,128)(2,1)}, u32[]{:S(2)}) copy-start(bf16[3,2,2,128,128]{4,3,2,1,0:T(8,128)(2,1)} %maps.19) | copy-start | bytes 1179652
  16.0 27.3 %collective-permute-start.2 = (bf16[96,32,128]{2,1,0:T(8,128)(2,1)S(1)}, bf16[96,32,128]{2,1,0:T(8,128)(2,1)S(1)}, u32[]{:S(2)}, u32[]{:S(2)}) collective-permute-start(bf16[96,32,128]{2,1,0:T(8,128)(2,1)S(1)} %shard_map.41.own._), channel_id=1, source_target_pairs={{0,128},{8,136},{16,144},{24,152},{32,160},{40,168},{48,176},{56,1... | collective-permute-start | bytes 2359304 | tf_op jit(solution)/shard_map/ppermute | solution.py:27
  19.6 9.0 %copy-start.2 = (bf16[4,1088,128]{2,1,0:T(8,128)(2,1)S(1)}, bf16[4,1088,128]{2,1,0:T(8,128)(2,1)}, u32[]{:S(2)}) copy-start(bf16[4,1088,128]{2,1,0:T(8,128)(2,1)} %shard_map.37.refs_8_._) | copy-start | bytes 3342340
  19.6 39.1 %collective-permute-start.3 = (bf16[96,32,128]{2,1,0:T(8,128)(2,1)S(1)}, bf16[96,32,128]{2,1,0:T(8,128)(2,1)S(1)}, u32[]{:S(2)}, u32[]{:S(2)}) collective-permute-start(bf16[96,32,128]{2,1,0:T(8,128)(2,1)S(1)} %shard_map.43.own), channel_id=1, source_target_pairs={{0,128},{8,136},{16,144},{24,152},{32,160},{40,168},{48,176},{56,1... | collective-permute-start | bytes 2359304 | tf_op jit(solution)/shard_map/ppermute | solution.py:27
  28.0 52.6 %collective-permute-start.7 = (bf16[64,32,128]{2,1,0:T(8,128)(2,1)S(1)}, bf16[64,32,128]{2,1,0:T(8,128)(2,1)S(1)}, u32[]{:S(2)}, u32[]{:S(2)}) collective-permute-start(bf16[64,32,128]{2,1,0:T(8,128)(2,1)S(1)} %shard_map.40.rest_0_.own), channel_id=1, source_target_pairs={{0,64},{8,72},{16,80},{24,88},{32,96},{40,104},{48,112},{56,120},{... | collective-permute-start | bytes 1572872 | tf_op jit(solution)/shard_map/ppermute | solution.py:27
  69.3 29.9 %copy-start.4 = (bf16[4,1088,128]{2,1,0:T(8,128)(2,1)}, bf16[4,1088,128]{2,1,0:T(8,128)(2,1)S(1)}, u32[]{:S(2)}) copy-start(bf16[4,1088,128]{2,1,0:T(8,128)(2,1)S(1)} %collective-permute-done.far) | copy-start | bytes 3342340
  69.9 17.3 %collective-permute-start.4 = (bf16[2,1088,128]{2,1,0:T(8,128)(2,1)S(1)}, bf16[2,1088,128]{2,1,0:T(8,128)(2,1)S(1)}, u32[]{:S(2)}, u32[]{:S(2)}) collective-permute-start(bf16[2,1088,128]{2,1,0:T(8,128)(2,1)S(1)} %get-tuple-element.12), channel_id=1, source_target_pairs={{0,4},{1,5},{2,6},{3,7},{4,0},{5,1},{6,2},{7,3},{8,12},{9,13},{10,... | collective-permute-start | bytes 1671176 | tf_op jit(solution)/shard_map/ppermute | solution.py:29
  73.0 26.1 %collective-permute-start.5 = (bf16[2,1088,128]{2,1,0:T(8,128)(2,1)S(1)}, bf16[2,1088,128]{2,1,0:T(8,128)(2,1)S(1)}, u32[]{:S(2)}, u32[]{:S(2)}) collective-permute-start(bf16[2,1088,128]{2,1,0:T(8,128)(2,1)S(1)} %get-tuple-element.13), channel_id=1, source_target_pairs={{0,128},{8,136},{16,144},{24,152},{32,160},{40,168},{48,176},{56,1... | collective-permute-start | bytes 1671176 | tf_op jit(solution)/shard_map/ppermute | solution.py:27
  73.6 25.5 %collective-permute-start.6 = (bf16[2,1088,128]{2,1,0:T(8,128)(2,1)S(1)}, bf16[2,1088,128]{2,1,0:T(8,128)(2,1)S(1)}, u32[]{:S(2)}, u32[]{:S(2)}) collective-permute-start(bf16[2,1088,128]{2,1,0:T(8,128)(2,1)S(1)} %get-tuple-element.14), channel_id=1, source_target_pairs={{0,132},{1,133},{2,134},{3,135},{4,128},{5,129},{6,130},{7,131},{8... | collective-permute-start | bytes 1671176 | tf_op jit(solution)/shard_map/ppermute | solution.py:34
  74.2 37.4 %collective-permute-start.11 = (bf16[96,32,128]{2,1,0:T(8,128)(2,1)S(1)}, bf16[96,32,128]{2,1,0:T(8,128)(2,1)S(1)}, u32[]{:S(2)}, u32[]{:S(2)}) collective-permute-start(bf16[96,32,128]{2,1,0:T(8,128)(2,1)S(1)} %shard_map.42.rest_0_.rest_1_.own), channel_id=1, source_target_pairs={{0,64},{8,72},{16,80},{24,88},{32,96},{40,104},{48,112},{56,120},{... | collective-permute-start | bytes 2359304 | tf_op jit(solution)/shard_map/ppermute | solution.py:27
  80.5 57.5 %collective-permute-start.14 = (bf16[96,32,128]{2,1,0:T(8,128)(2,1)S(1)}, bf16[96,32,128]{2,1,0:T(8,128)(2,1)S(1)}, u32[]{:S(2)}, u32[]{:S(2)}) collective-permute-start(bf16[96,32,128]{2,1,0:T(8,128)(2,1)S(1)} %shard_map.44.rest_2_.own), channel_id=1, source_target_pairs={{0,64},{8,72},{16,80},{24,88},{32,96},{40,104},{48,112},{56,120},{... | collective-permute-start | bytes 2359304 | tf_op jit(solution)/shard_map/ppermute | solution.py:27
  87.2 20.5 %collective-permute-start.12 = (bf16[64,32,128]{2,1,0:T(8,128)(2,1)S(1)}, bf16[64,32,128]{2,1,0:T(8,128)(2,1)S(1)}, u32[]{:S(2)}, u32[]{:S(2)}) collective-permute-start(bf16[64,32,128]{2,1,0:T(8,128)(2,1)S(1)} %shard_map.46.rest_0_.own), channel_id=1, source_target_pairs={{0,4},{1,5},{2,6},{3,7},{4,0},{5,1},{6,2},{7,3},{8,12},{9,13},{10,... | collective-permute-start | bytes 1572872 | tf_op jit(solution)/shard_map/ppermute | solution.py:29
  103.9 26.3 %collective-permute-start.10 = (bf16[2,1024,128]{2,1,0:T(8,128)(2,1)S(1)}, bf16[2,1024,128]{2,1,0:T(8,128)(2,1)S(1)}, u32[]{:S(2)}, u32[]{:S(2)}) collective-permute-start(bf16[2,1024,128]{2,1,0:T(8,128)(2,1)S(1)} %get-tuple-element.18), channel_id=1, source_target_pairs={{0,132},{1,133},{2,134},{3,135},{4,128},{5,129},{6,130},{7,131},{8... | collective-permute-start | bytes 1572872 | tf_op jit(solution)/shard_map/ppermute | solution.py:34
  106.6 23.7 %collective-permute-start.8 = (bf16[2,1024,128]{2,1,0:T(8,128)(2,1)S(1)}, bf16[2,1024,128]{2,1,0:T(8,128)(2,1)S(1)}, u32[]{:S(2)}, u32[]{:S(2)}) collective-permute-start(bf16[2,1024,128]{2,1,0:T(8,128)(2,1)S(1)} %get-tuple-element.16), channel_id=1, source_target_pairs={{0,4},{1,5},{2,6},{3,7},{4,0},{5,1},{6,2},{7,3},{8,12},{9,13},{10,... | collective-permute-start | bytes 1572872 | tf_op jit(solution)/shard_map/ppermute | solution.py:29
  107.8 24.4 %collective-permute-start.9 = (bf16[2,1024,128]{2,1,0:T(8,128)(2,1)S(1)}, bf16[2,1024,128]{2,1,0:T(8,128)(2,1)S(1)}, u32[]{:S(2)}, u32[]{:S(2)}) collective-permute-start(bf16[2,1024,128]{2,1,0:T(8,128)(2,1)S(1)} %get-tuple-element.17), channel_id=1, source_target_pairs={{0,128},{8,136},{16,144},{24,152},{32,160},{40,168},{48,176},{56,1... | collective-permute-start | bytes 1572872 | tf_op jit(solution)/shard_map/ppermute | solution.py:27
  113.5 37.5 %collective-permute-start.16 = (bf16[96,32,128]{2,1,0:T(8,128)(2,1)S(1)}, bf16[96,32,128]{2,1,0:T(8,128)(2,1)S(1)}, u32[]{:S(2)}, u32[]{:S(2)}) collective-permute-start(bf16[96,32,128]{2,1,0:T(8,128)(2,1)S(1)} %shard_map.48.rest_0_.own), channel_id=1, source_target_pairs={{0,4},{1,5},{2,6},{3,7},{4,0},{5,1},{6,2},{7,3},{8,12},{9,13},{10,... | collective-permute-start | bytes 2359304 | tf_op jit(solution)/shard_map/ppermute | solution.py:29
  132.8 63.6 %collective-permute-start.13 = (bf16[4,1024,128]{2,1,0:T(8,128)(2,1)S(1)}, bf16[4,1024,128]{2,1,0:T(8,128)(2,1)S(1)}, u32[]{:S(2)}, u32[]{:S(2)}) collective-permute-start(bf16[4,1024,128]{2,1,0:T(8,128)(2,1)S(1)} %shard_map.50), channel_id=1, source_target_pairs={{0,64},{8,72},{16,80},{24,88},{32,96},{40,104},{48,112},{56,120},{... | collective-permute-start | bytes 3145736 | tf_op jit(solution)/shard_map/ppermute | solution.py:27
  140.0 26.6 %collective-permute-start.15 = (bf16[96,32,128]{2,1,0:T(8,128)(2,1)S(1)}, bf16[96,32,128]{2,1,0:T(8,128)(2,1)S(1)}, u32[]{:S(2)}, u32[]{:S(2)}) collective-permute-start(bf16[96,32,128]{2,1,0:T(8,128)(2,1)S(1)} %shard_map.51.own), channel_id=1, source_target_pairs={{0,4},{1,5},{2,6},{3,7},{4,0},{5,1},{6,2},{7,3},{8,12},{9,13},{10,... | collective-permute-start | bytes 2359304 | tf_op jit(solution)/shard_map/ppermute | solution.py:29

commit v5 on v4

--- a/solution.py
+++ b/solution.py
@@ -179,7 +179,8 @@
 
 
 def pack_kernel(*refs):
-    blocks, factors, out = refs[:4], refs[4:8], refs[-1]
+    blocks, factors, (whole, out, done) = refs[:4], refs[4:8], refs[-3:]
+    copies = []
     for i, (w, t) in enumerate(zip(blocks, factors)):
         targets, slots, laws, width = w.shape
         rows = slots * laws
@@ -189,6 +190,10 @@
             for later in range(2):
                 start = targets * rows + (later * targets + target) * slots
                 out[i, start : start + slots, :] = t[1 + later, target].astype(out.dtype)
+        copies.append(pltpu.make_async_copy(out.at[i], whole.at[i], done.at[i]))
+        copies[-1].start()
+    for copy in copies:
+        copy.wait()
 
 
 def pack(weights, twiddles, far, after=()):
@@ -211,9 +216,10 @@
             *[factors_of(place + far) for place in PLANE],
             *[pl.BlockSpec(memory_space=pl.ANY)] * len(after),
         ],
-        pl.BlockSpec((4, rows, width), lambda i: (0, 0, 0)),
+        pl.BlockSpec(memory_space=pl.ANY),
         (*[weights] * 4, *[twiddles] * 4, *after),
         None,
+        scratch=[pltpu.VMEM((4, rows, width), weights.dtype), pltpu.SemaphoreType.DMA((4,))],
         vmem=60 * 2**20 if far else VMEM,
         cost=NCOST,
         nbytes=16 * rows * width,

time: 199 us -> 199 us (level)
  transfers between devices with their start and end apart: 17 -> 17, of which waited for: 12 -> 12; matrix products, arithmetic and copies ran while one was open for 0% -> 0% of each run, Pallas kernels for 18% -> 19%
where the time goes in v5:
time: 199 us; the launch traced here: 198 us
  waiting for transfers between devices  111 us (56%)
  starting transfers between devices  43.7 us (22%)
  Pallas kernels  41.4 us (21%)
    ppermute x10, waiting for transfers between devices, swap(): return lax.ppermute(block, 'src', [(i, i ^ flip_src) for i in range(n_src)])  76.6 us
    pallas_call x19, Pallas kernels, call(): pl.pallas_call(kernel, out_shape=out_shape, grid_spec=pltpu.PrefetchScala...  41.4 us
    ppermute x10, starting transfers between devices, swap(): return lax.ppermute(block, 'src', [(i, i ^ flip_src) for i in range(n_src)])  27.5 us
    ppermute x5, waiting for transfers between devices, swap(): return lax.ppermute(block, 'tgt', [(i, i ^ flip_tgt) for i in range(n_tgt)])  20.8 us
    ppermute x2, waiting for transfers between devices, swap(): return lax.ppermute(block, ('src', 'tgt'), route)  14 us
    ppermute x5, starting transfers between devices, swap(): return lax.ppermute(block, 'tgt', [(i, i ^ flip_tgt) for i in range(n_tgt)])  12.8 us
  transfers between devices with their start and end apart: 17, of which 12 were waited for; matrix products, arithmetic and copies ran while one was open for 0% of the time, Pallas kernels for 19%

profile of v5, /device:TPU:80, one launch (start us, length us, event | category | flops | bytes accessed | tf_op | source)
XLA Modules:
  0.0 198.2 jit_solution(15463004584869792459)
XLA Ops:
  0.0 2.6 %shard_map.37.refs_8_._ = bf16[4,1088,128]{2,1,0:T(8,128)(2,1)} custom-call(bf16[4,128,32,128]{3,2,1,0:T(8,128)(2,1)} %w.5, bf16[4,128,32,128]{3,2,1,0:T(8,128)(2,1)} %w.5, bf16[4,128,32,128]{3,2,1,0:T(8,128)(2,1)} %w.5, bf16[4,128,32,128]{3,2,1,0:T(8,128)(2,1)} %w.5, f32[4,4,128,128]{3,2,1,0:T(8,128)} %refs_4_.7, f32[4,4,128,128]{3,2,1,0:T(8,128)} %refs_4_.7, ...), custom_call_target="tpu_custom_call" | custom-call | bytes 8912896 | tf_op jit(solution)/shard_map/pallas_call | solution.py:73
  2.6 5.5 %collective-permute-start = (bf16[4,1088,128]{2,1,0:T(8,128)(2,1)}, bf16[4,1088,128]{2,1,0:T(8,128)(2,1)S(1)}, u32[]{:S(2)}, u32[]{:S(2)}) collective-permute-start(bf16[4,1088,128]{2,1,0:T(8,128)(2,1)} %shard_map.37.refs_8_._), channel_id=1, source_target_pairs={{0,64},{8,72},{16,80},{24,88},{32,96},{40,104},{48,112},{56,120},{... | collective-permute-start | bytes 3342344 | tf_op jit(solution)/shard_map/ppermute | solution.py:27
  9.4 2.0 %shard_map.39.own._ = bf16[64,32,128]{2,1,0:T(8,128)(2,1)S(1)} custom-call(s32[8]{0:T(128)S(1)} %iota_xor_fusion.order, bf16[4,128,32,128]{3,2,1,0:T(8,128)(2,1)} %w.5, f32[4,4,128,128]{3,2,1,0:T(8,128)S(1)} %copy-done, bf16[4,1088,128]{2,1,0:T(8,128)(2,1)S(1)} %copy-done.1), custom_call_target="tpu_custom_call" | custom-call | tf_op jit(solution)/shard_map/pallas_call | solution.py:73
  12.9 2.9 %shard_map.41.own._ = bf16[96,32,128]{2,1,0:T(8,128)(2,1)S(1)} custom-call(s32[8]{0:T(128)S(1)} %iota_xor_fusion.order, bf16[4,128,32,128]{3,2,1,0:T(8,128)(2,1)} %w.5, f32[4,4,128,128]{3,2,1,0:T(8,128)S(1)} %copy-done, bf16[64,32,128]{2,1,0:T(8,128)(2,1)S(1)} %shard_map.39.own._), custom_call_target="tpu_custom_call" | custom-call | tf_op jit(solution)/shard_map/pallas_call | solution.py:73
  16.5 2.9 %shard_map.43.own = bf16[96,32,128]{2,1,0:T(8,128)(2,1)S(1)} custom-call(s32[8]{0:T(128)S(1)} %iota_xor_fusion.order, bf16[4,128,32,128]{3,2,1,0:T(8,128)(2,1)} %w.5, f32[4,4,128,128]{3,2,1,0:T(8,128)S(1)} %copy-done, bf16[96,32,128]{2,1,0:T(8,128)(2,1)S(1)} %shard_map.41.own._), custom_call_target="tpu_custom_call" | custom-call | tf_op jit(solution)/shard_map/pallas_call | solution.py:73
  21.0 5.3 %collective-permute-done.1.other = bf16[64,32,128]{2,1,0:T(8,128)(2,1)S(1)} collective-permute-done((bf16[64,32,128]{2,1,0:T(8,128)(2,1)S(1)}, bf16[64,32,128]{2,1,0:T(8,128)(2,1)S(1)}, u32[]{:S(2)}, u32[]{:S(2)}) %collective-permute-start.1) | collective-permute-done | bytes 524320 | tf_op jit(solution)/shard_map/ppermute | solution.py:27
  28.5 2.3 %shard_map.38.near = bf16[4,1088,128]{2,1,0:T(8,128)(2,1)S(1)} custom-call(bf16[4,128,32,128]{3,2,1,0:T(8,128)(2,1)} %w.5, bf16[4,128,32,128]{3,2,1,0:T(8,128)(2,1)} %w.5, bf16[4,128,32,128]{3,2,1,0:T(8,128)(2,1)} %w.5, bf16[4,128,32,128]{3,2,1,0:T(8,128)(2,1)} %w.5, f32[4,4,128,128]{3,2,1,0:T(8,128)S(1)} %copy-done, f32[4,4,128,128]{3,2,1,0:T(8,128)S(1)} %copy-done, ...), custom_call_target="tpu_custom_call" | custom-call | bytes 8912896 | tf_op jit(solution)/shard_map/pallas_call | solution.py:73
  30.7 12.4 %collective-permute-done.2.other = bf16[96,32,128]{2,1,0:T(8,128)(2,1)S(1)} collective-permute-done((bf16[96,32,128]{2,1,0:T(8,128)(2,1)S(1)}, bf16[96,32,128]{2,1,0:T(8,128)(2,1)S(1)}, u32[]{:S(2)}, u32[]{:S(2)}) %collective-permute-start.2) | collective-permute-done | bytes 786464 | tf_op jit(solution)/shard_map/ppermute | solution.py:27
  43.1 2.0 shard_map.42.rest_0_.rest_1_.own
  45.1 13.4 %collective-permute-done.3.other = bf16[96,32,128]{2,1,0:T(8,128)(2,1)S(1)} collective-permute-done((bf16[96,32,128]{2,1,0:T(8,128)(2,1)S(1)}, bf16[96,32,128]{2,1,0:T(8,128)(2,1)S(1)}, u32[]{:S(2)}, u32[]{:S(2)}) %collective-permute-start.3) | collective-permute-done | bytes 786464 | tf_op jit(solution)/shard_map/ppermute | solution.py:27
  58.5 2.0 shard_map.44.rest_2_.own
  60.5 8.6 %collective-permute-done.far = bf16[4,1088,128]{2,1,0:T(8,128)(2,1)S(1)} collective-permute-done((bf16[4,1088,128]{2,1,0:T(8,128)(2,1)}, bf16[4,1088,128]{2,1,0:T(8,128)(2,1)S(1)}, u32[]{:S(2)}, u32[]{:S(2)}) %collective-permute-start) | collective-permute-done | bytes 1114144 | tf_op jit(solution)/shard_map/ppermute | solution.py:27
  69.8 3.1 %collective-permute-start.4 = (bf16[2,1088,128]{2,1,0:T(8,128)(2,1)S(1)}, bf16[2,1088,128]{2,1,0:T(8,128)(2,1)S(1)}, u32[]{:S(2)}, u32[]{:S(2)}) collective-permute-start(bf16[2,1088,128]{2,1,0:T(8,128)(2,1)S(1)} %get-tuple-element.12), channel_id=1, source_target_pairs={{0,4},{1,5},{2,6},{3,7},{4,0},{5,1},{6,2},{7,3},{8,12},{9,13},{10,... | collective-permute-start | bytes 1671176 | tf_op jit(solution)/shard_map/ppermute | solution.py:29
  74.0 5.2 %collective-permute-start.11 = (bf16[96,32,128]{2,1,0:T(8,128)(2,1)S(1)}, bf16[96,32,128]{2,1,0:T(8,128)(2,1)S(1)}, u32[]{:S(2)}, u32[]{:S(2)}) collective-permute-start(bf16[96,32,128]{2,1,0:T(8,128)(2,1)S(1)} %shard_map.42.rest_0_.rest_1_.own), channel_id=1, source_target_pairs={{0,64},{8,72},{16,80},{24,88},{32,96},{40,104},{48,112},{56,120},{... | collective-permute-start | bytes 2359304 | tf_op jit(solution)/shard_map/ppermute | solution.py:27
  80.4 5.1 %collective-permute-start.14 = (bf16[96,32,128]{2,1,0:T(8,128)(2,1)S(1)}, bf16[96,32,128]{2,1,0:T(8,128)(2,1)S(1)}, u32[]{:S(2)}, u32[]{:S(2)}) collective-permute-start(bf16[96,32,128]{2,1,0:T(8,128)(2,1)S(1)} %shard_map.44.rest_2_.own), channel_id=1, source_target_pairs={{0,64},{8,72},{16,80},{24,88},{32,96},{40,104},{48,112},{56,120},{... | collective-permute-start | bytes 2359304 | tf_op jit(solution)/shard_map/ppermute | solution.py:27
  87.1 3.1 %collective-permute-start.12 = (bf16[64,32,128]{2,1,0:T(8,128)(2,1)S(1)}, bf16[64,32,128]{2,1,0:T(8,128)(2,1)S(1)}, u32[]{:S(2)}, u32[]{:S(2)}) collective-permute-start(bf16[64,32,128]{2,1,0:T(8,128)(2,1)S(1)} %shard_map.46.rest_0_.own), channel_id=1, source_target_pairs={{0,4},{1,5},{2,6},{3,7},{4,0},{5,1},{6,2},{7,3},{8,12},{9,13},{10,... | collective-permute-start | bytes 1572872 | tf_op jit(solution)/shard_map/ppermute | solution.py:29
  90.2 8.8 %collective-permute-done.5.two = bf16[2,1088,128]{2,1,0:T(8,128)(2,1)S(1)} collective-permute-done((bf16[2,1088,128]{2,1,0:T(8,128)(2,1)S(1)}, bf16[2,1088,128]{2,1,0:T(8,128)(2,1)S(1)}, u32[]{:S(2)}, u32[]{:S(2)}) %collective-permute-start.5) | collective-permute-done | bytes 557088 | tf_op jit(solution)/shard_map/ppermute | solution.py:27
  99.0 4.8 %shard_map.47 = (bf16[2,1024,128]{2,1,0:T(8,128)(2,1)S(1)}, bf16[2,1024,128]{2,1,0:T(8,128)(2,1)S(1)}, bf16[2,1024,128]{2,1,0:T(8,128)(2,1)S(1)}, bf16[2,1024,128]{2,1,0:T(8,128)(2,1)S(1)}) custom-call(s32[8]{0:T(128)S(1)} %iota_xor_fusion.order, bf16[4,1088,128]{2,1,0:T(8,128)(2,1)S(1)} %shard_map.38.near, bf16[4,1088,128]{2,1,0:T(8,128)(2,1)} %copy-done.4, ...), custom_call_target="tpu_custom_call" | custom-call | flops 6442450944 | bytes 16777216 | tf_op jit(solution)/shard_map/pallas_call | solution.py:73
  103.7 2.8 %collective-permute-start.10 = (bf16[2,1024,128]{2,1,0:T(8,128)(2,1)S(1)}, bf16[2,1024,128]{2,1,0:T(8,128)(2,1)S(1)}, u32[]{:S(2)}, u32[]{:S(2)}) collective-permute-start(bf16[2,1024,128]{2,1,0:T(8,128)(2,1)S(1)} %get-tuple-element.18), channel_id=1, source_target_pairs={{0,132},{1,133},{2,134},{3,135},{4,128},{5,129},{6,130},{7,131},{8... | collective-permute-start | bytes 1572872 | tf_op jit(solution)/shard_map/ppermute | solution.py:34
  109.2 2.3 %shard_map.49.rest_1_.rest_0_ = bf16[4,128,32,128]{3,2,1,0:T(8,128)(2,1)} custom-call(s32[8]{0:T(128)S(1)} %iota_xor_fusion.order, bf16[64,32,128]{2,1,0:T(8,128)(2,1)S(1)} %shard_map.46.rest_0_.own, bf16[64,32,128]{2,1,0:T(8,128)(2,1)S(1)} %collective-permute-done.12.other, bf16[3,2,2,128,128]{4,3,2,1,0:T(8,128)(2,1)S(1)} %copy-done.3, ...), custom_call_target="tpu_custom_call" | custom-call | flops 1073741824 | bytes 6291456 | tf_op jit(solution)/shard_map/pallas_call | solution.py:73
  111.4 1.9 shard_map.48.rest_0_.own
  113.4 2.7 %collective-permute-start.16 = (bf16[96,32,128]{2,1,0:T(8,128)(2,1)S(1)}, bf16[96,32,128]{2,1,0:T(8,128)(2,1)S(1)}, u32[]{:S(2)}, u32[]{:S(2)}) collective-permute-start(bf16[96,32,128]{2,1,0:T(8,128)(2,1)S(1)} %shard_map.48.rest_0_.own), channel_id=1, source_target_pairs={{0,4},{1,5},{2,6},{3,7},{4,0},{5,1},{6,2},{7,3},{8,12},{9,13},{10,... | collective-permute-start | bytes 2359304 | tf_op jit(solution)/shard_map/ppermute | solution.py:29
  116.1 14.0 %collective-permute-done.10.d.refs_3_ = bf16[2,1024,128]{2,1,0:T(8,128)(2,1)S(1)} collective-permute-done((bf16[2,1024,128]{2,1,0:T(8,128)(2,1)S(1)}, bf16[2,1024,128]{2,1,0:T(8,128)(2,1)S(1)}, u32[]{:S(2)}, u32[]{:S(2)}) %collective-permute-start.10) | collective-permute-done | bytes 524320 | tf_op jit(solution)/shard_map/ppermute | solution.py:34
  130.1 2.1 %collective-permute-done.9.c.refs_2_ = bf16[2,1024,128]{2,1,0:T(8,128)(2,1)S(1)} collective-permute-done((bf16[2,1024,128]{2,1,0:T(8,128)(2,1)S(1)}, bf16[2,1024,128]{2,1,0:T(8,128)(2,1)S(1)}, u32[]{:S(2)}, u32[]{:S(2)}) %collective-permute-start.9) | collective-permute-done | bytes 524320 | tf_op jit(solution)/shard_map/ppermute | solution.py:27
  132.8 5.2 %collective-permute-start.13 = (bf16[4,1024,128]{2,1,0:T(8,128)(2,1)S(1)}, bf16[4,1024,128]{2,1,0:T(8,128)(2,1)S(1)}, u32[]{:S(2)}, u32[]{:S(2)}) collective-permute-start(bf16[4,1024,128]{2,1,0:T(8,128)(2,1)S(1)} %shard_map.50), channel_id=1, source_target_pairs={{0,64},{8,72},{16,80},{24,88},{32,96},{40,104},{48,112},{56,120},{... | collective-permute-start | bytes 3145736 | tf_op jit(solution)/shard_map/ppermute | solution.py:27
  138.0 2.0 shard_map.51.own
  140.0 2.9 %collective-permute-start.15 = (bf16[96,32,128]{2,1,0:T(8,128)(2,1)S(1)}, bf16[96,32,128]{2,1,0:T(8,128)(2,1)S(1)}, u32[]{:S(2)}, u32[]{:S(2)}) collective-permute-start(bf16[96,32,128]{2,1,0:T(8,128)(2,1)S(1)} %shard_map.51.own), channel_id=1, source_target_pairs={{0,4},{1,5},{2,6},{3,7},{4,0},{5,1},{6,2},{7,3},{8,12},{9,13},{10,... | collective-permute-start | bytes 2359304 | tf_op jit(solution)/shard_map/ppermute | solution.py:29
  142.9 8.1 %collective-permute-done.16.other = bf16[96,32,128]{2,1,0:T(8,128)(2,1)S(1)} collective-permute-done((bf16[96,32,128]{2,1,0:T(8,128)(2,1)S(1)}, bf16[96,32,128]{2,1,0:T(8,128)(2,1)S(1)}, u32[]{:S(2)}, u32[]{:S(2)}) %collective-permute-start.16) | collective-permute-done | bytes 786464 | tf_op jit(solution)/shard_map/ppermute | solution.py:29
  151.0 2.9 %shard_map.52.rest_0_ = bf16[4,128,32,128]{3,2,1,0:T(8,128)(2,1)} custom-call(s32[8]{0:T(128)S(1)} %iota_xor_fusion.order, bf16[96,32,128]{2,1,0:T(8,128)(2,1)S(1)} %shard_map.48.rest_0_.own, bf16[96,32,128]{2,1,0:T(8,128)(2,1)S(1)} %collective-permute-done.16.other, bf16[3,2,2,128,128]{4,3,2,1,0:T(8,128)(2,1)S(1)} %copy-done.3, ...), custom_call_target="tpu_custom_call", output_to_operand_aliasing={{}: (5, {})} | custom-call | flops 1610612736 | bytes 9437184 | tf_op jit(solution)/shard_map/pallas_call | solution.py:73
  154.0 12.6 %collective-permute-done.15.other = bf16[96,32,128]{2,1,0:T(8,128)(2,1)S(1)} collective-permute-done((bf16[96,32,128]{2,1,0:T(8,128)(2,1)S(1)}, bf16[96,32,128]{2,1,0:T(8,128)(2,1)S(1)}, u32[]{:S(2)}, u32[]{:S(2)}) %collective-permute-start.15) | collective-permute-done | bytes 786464 | tf_op jit(solution)/shard_map/ppermute | solution.py:29
  166.5 2.9 %shard_map.53.refs_8_ = bf16[4,128,32,128]{3,2,1,0:T(8,128)(2,1)} custom-call(s32[8]{0:T(128)S(1)} %iota_xor_fusion.order, bf16[96,32,128]{2,1,0:T(8,128)(2,1)S(1)} %shard_map.51.own, bf16[96,32,128]{2,1,0:T(8,128)(2,1)S(1)} %collective-permute-done.15.other, bf16[3,2,2,128,128]{4,3,2,1,0:T(8,128)(2,1)S(1)} %copy-done.3, ...), custom_call_target="tpu_custom_call", output_to_operand_aliasing={{}: (5, {})} | custom-call | flops 1610612736 | bytes 9437184 | tf_op jit(solution)/shard_map/pallas_call | solution.py:73
  171.3 24.9 %collective-permute-done.13.refs_0_ = bf16[4,1024,128]{2,1,0:T(8,128)(2,1)S(1)} collective-permute-done((bf16[4,1024,128]{2,1,0:T(8,128)(2,1)S(1)}, bf16[4,1024,128]{2,1,0:T(8,128)(2,1)S(1)}, u32[]{:S(2)}, u32[]{:S(2)}) %collective-permute-start.13) | collective-permute-done | bytes 1048608 | tf_op jit(solution)/shard_map/ppermute | solution.py:27
  (32 shorter events, 18.6 us)
Async XLA Ops:
  0.0 8.1 %copy-start = (f32[4,4,128,128]{3,2,1,0:T(8,128)S(1)}, f32[4,4,128,128]{3,2,1,0:T(8,128)}, u32[]{:S(2)}) copy-start(f32[4,4,128,128]{3,2,1,0:T(8,128)} %refs_4_.7) | copy-start | bytes 3145732
  2.6 66.5 %collective-permute-start = (bf16[4,1088,128]{2,1,0:T(8,128)(2,1)}, bf16[4,1088,128]{2,1,0:T(8,128)(2,1)S(1)}, u32[]{:S(2)}, u32[]{:S(2)}) collective-permute-start(bf16[4,1088,128]{2,1,0:T(8,128)(2,1)} %shard_map.37.refs_8_._), channel_id=1, source_target_pairs={{0,64},{8,72},{16,80},{24,88},{32,96},{40,104},{48,112},{56,120},{... | collective-permute-start | bytes 3342344 | tf_op jit(solution)/shard_map/ppermute | solution.py:27
  8.1 1.3 copy-start.1
  11.3 14.9 %collective-permute-start.1 = (bf16[64,32,128]{2,1,0:T(8,128)(2,1)S(1)}, bf16[64,32,128]{2,1,0:T(8,128)(2,1)S(1)}, u32[]{:S(2)}, u32[]{:S(2)}) collective-permute-start(bf16[64,32,128]{2,1,0:T(8,128)(2,1)S(1)} %shard_map.39.own._), channel_id=1, source_target_pairs={{0,128},{8,136},{16,144},{24,152},{32,160},{40,168},{48,176},{56,1... | collective-permute-start | bytes 1572872 | tf_op jit(solution)/shard_map/ppermute | solution.py:27
  15.9 10.4 %copy-start.3 = (bf16[3,2,2,128,128]{4,3,2,1,0:T(8,128)(2,1)S(1)}, bf16[3,2,2,128,128]{4,3,2,1,0:T(8,128)(2,1)}, u32[]{:S(2)}) copy-start(bf16[3,2,2,128,128]{4,3,2,1,0:T(8,128)(2,1)} %maps.19) | copy-start | bytes 1179652
  15.9 27.3 %collective-permute-start.2 = (bf16[96,32,128]{2,1,0:T(8,128)(2,1)S(1)}, bf16[96,32,128]{2,1,0:T(8,128)(2,1)S(1)}, u32[]{:S(2)}, u32[]{:S(2)}) collective-permute-start(bf16[96,32,128]{2,1,0:T(8,128)(2,1)S(1)} %shard_map.41.own._), channel_id=1, source_target_pairs={{0,128},{8,136},{16,144},{24,152},{32,160},{40,168},{48,176},{56,1... | collective-permute-start | bytes 2359304 | tf_op jit(solution)/shard_map/ppermute | solution.py:27
  19.4 9.0 %copy-start.2 = (bf16[4,1088,128]{2,1,0:T(8,128)(2,1)S(1)}, bf16[4,1088,128]{2,1,0:T(8,128)(2,1)}, u32[]{:S(2)}) copy-start(bf16[4,1088,128]{2,1,0:T(8,128)(2,1)} %shard_map.37.refs_8_._) | copy-start | bytes 3342340
  19.4 39.1 %collective-permute-start.3 = (bf16[96,32,128]{2,1,0:T(8,128)(2,1)S(1)}, bf16[96,32,128]{2,1,0:T(8,128)(2,1)S(1)}, u32[]{:S(2)}, u32[]{:S(2)}) collective-permute-start(bf16[96,32,128]{2,1,0:T(8,128)(2,1)S(1)} %shard_map.43.own), channel_id=1, source_target_pairs={{0,128},{8,136},{16,144},{24,152},{32,160},{40,168},{48,176},{56,1... | collective-permute-start | bytes 2359304 | tf_op jit(solution)/shard_map/ppermute | solution.py:27
  27.8 52.5 %collective-permute-start.7 = (bf16[64,32,128]{2,1,0:T(8,128)(2,1)S(1)}, bf16[64,32,128]{2,1,0:T(8,128)(2,1)S(1)}, u32[]{:S(2)}, u32[]{:S(2)}) collective-permute-start(bf16[64,32,128]{2,1,0:T(8,128)(2,1)S(1)} %shard_map.40.rest_0_.own), channel_id=1, source_target_pairs={{0,64},{8,72},{16,80},{24,88},{32,96},{40,104},{48,112},{56,120},{... | collective-permute-start | bytes 1572872 | tf_op jit(solution)/shard_map/ppermute | solution.py:27
  69.1 29.9 %copy-start.4 = (bf16[4,1088,128]{2,1,0:T(8,128)(2,1)}, bf16[4,1088,128]{2,1,0:T(8,128)(2,1)S(1)}, u32[]{:S(2)}) copy-start(bf16[4,1088,128]{2,1,0:T(8,128)(2,1)S(1)} %collective-permute-done.far) | copy-start | bytes 3342340
  69.8 17.3 %collective-permute-start.4 = (bf16[2,1088,128]{2,1,0:T(8,128)(2,1)S(1)}, bf16[2,1088,128]{2,1,0:T(8,128)(2,1)S(1)}, u32[]{:S(2)}, u32[]{:S(2)}) collective-permute-start(bf16[2,1088,128]{2,1,0:T(8,128)(2,1)S(1)} %get-tuple-element.12), channel_id=1, source_target_pairs={{0,4},{1,5},{2,6},{3,7},{4,0},{5,1},{6,2},{7,3},{8,12},{9,13},{10,... | collective-permute-start | bytes 1671176 | tf_op jit(solution)/shard_map/ppermute | solution.py:29
  72.9 26.1 %collective-permute-start.5 = (bf16[2,1088,128]{2,1,0:T(8,128)(2,1)S(1)}, bf16[2,1088,128]{2,1,0:T(8,128)(2,1)S(1)}, u32[]{:S(2)}, u32[]{:S(2)}) collective-permute-start(bf16[2,1088,128]{2,1,0:T(8,128)(2,1)S(1)} %get-tuple-element.13), channel_id=1, source_target_pairs={{0,128},{8,136},{16,144},{24,152},{32,160},{40,168},{48,176},{56,1... | collective-permute-start | bytes 1671176 | tf_op jit(solution)/shard_map/ppermute | solution.py:27
  73.5 25.5 %collective-permute-start.6 = (bf16[2,1088,128]{2,1,0:T(8,128)(2,1)S(1)}, bf16[2,1088,128]{2,1,0:T(8,128)(2,1)S(1)}, u32[]{:S(2)}, u32[]{:S(2)}) collective-permute-start(bf16[2,1088,128]{2,1,0:T(8,128)(2,1)S(1)} %get-tuple-element.14), channel_id=1, source_target_pairs={{0,132},{1,133},{2,134},{3,135},{4,128},{5,129},{6,130},{7,131},{8... | collective-permute-start | bytes 1671176 | tf_op jit(solution)/shard_map/ppermute | solution.py:34
  74.0 37.4 %collective-permute-start.11 = (bf16[96,32,128]{2,1,0:T(8,128)(2,1)S(1)}, bf16[96,32,128]{2,1,0:T(8,128)(2,1)S(1)}, u32[]{:S(2)}, u32[]{:S(2)}) collective-permute-start(bf16[96,32,128]{2,1,0:T(8,128)(2,1)S(1)} %shard_map.42.rest_0_.rest_1_.own), channel_id=1, source_target_pairs={{0,64},{8,72},{16,80},{24,88},{32,96},{40,104},{48,112},{56,120},{... | collective-permute-start | bytes 2359304 | tf_op jit(solution)/shard_map/ppermute | solution.py:27
  80.4 57.6 %collective-permute-start.14 = (bf16[96,32,128]{2,1,0:T(8,128)(2,1)S(1)}, bf16[96,32,128]{2,1,0:T(8,128)(2,1)S(1)}, u32[]{:S(2)}, u32[]{:S(2)}) collective-permute-start(bf16[96,32,128]{2,1,0:T(8,128)(2,1)S(1)} %shard_map.44.rest_2_.own), channel_id=1, source_target_pairs={{0,64},{8,72},{16,80},{24,88},{32,96},{40,104},{48,112},{56,120},{... | collective-permute-start | bytes 2359304 | tf_op jit(solution)/shard_map/ppermute | solution.py:27
  87.1 20.5 %collective-permute-start.12 = (bf16[64,32,128]{2,1,0:T(8,128)(2,1)S(1)}, bf16[64,32,128]{2,1,0:T(8,128)(2,1)S(1)}, u32[]{:S(2)}, u32[]{:S(2)}) collective-permute-start(bf16[64,32,128]{2,1,0:T(8,128)(2,1)S(1)} %shard_map.46.rest_0_.own), channel_id=1, source_target_pairs={{0,4},{1,5},{2,6},{3,7},{4,0},{5,1},{6,2},{7,3},{8,12},{9,13},{10,... | collective-permute-start | bytes 1572872 | tf_op jit(solution)/shard_map/ppermute | solution.py:29
  103.7 26.3 %collective-permute-start.10 = (bf16[2,1024,128]{2,1,0:T(8,128)(2,1)S(1)}, bf16[2,1024,128]{2,1,0:T(8,128)(2,1)S(1)}, u32[]{:S(2)}, u32[]{:S(2)}) collective-permute-start(bf16[2,1024,128]{2,1,0:T(8,128)(2,1)S(1)} %get-tuple-element.18), channel_id=1, source_target_pairs={{0,132},{1,133},{2,134},{3,135},{4,128},{5,129},{6,130},{7,131},{8... | collective-permute-start | bytes 1572872 | tf_op jit(solution)/shard_map/ppermute | solution.py:34
  106.6 23.5 %collective-permute-start.8 = (bf16[2,1024,128]{2,1,0:T(8,128)(2,1)S(1)}, bf16[2,1024,128]{2,1,0:T(8,128)(2,1)S(1)}, u32[]{:S(2)}, u32[]{:S(2)}) collective-permute-start(bf16[2,1024,128]{2,1,0:T(8,128)(2,1)S(1)} %get-tuple-element.16), channel_id=1, source_target_pairs={{0,4},{1,5},{2,6},{3,7},{4,0},{5,1},{6,2},{7,3},{8,12},{9,13},{10,... | collective-permute-start | bytes 1572872 | tf_op jit(solution)/shard_map/ppermute | solution.py:29
  107.6 24.6 %collective-permute-start.9 = (bf16[2,1024,128]{2,1,0:T(8,128)(2,1)S(1)}, bf16[2,1024,128]{2,1,0:T(8,128)(2,1)S(1)}, u32[]{:S(2)}, u32[]{:S(2)}) collective-permute-start(bf16[2,1024,128]{2,1,0:T(8,128)(2,1)S(1)} %get-tuple-element.17), channel_id=1, source_target_pairs={{0,128},{8,136},{16,144},{24,152},{32,160},{40,168},{48,176},{56,1... | collective-permute-start | bytes 1572872 | tf_op jit(solution)/shard_map/ppermute | solution.py:27
  113.4 37.6 %collective-permute-start.16 = (bf16[96,32,128]{2,1,0:T(8,128)(2,1)S(1)}, bf16[96,32,128]{2,1,0:T(8,128)(2,1)S(1)}, u32[]{:S(2)}, u32[]{:S(2)}) collective-permute-start(bf16[96,32,128]{2,1,0:T(8,128)(2,1)S(1)} %shard_map.48.rest_0_.own), channel_id=1, source_target_pairs={{0,4},{1,5},{2,6},{3,7},{4,0},{5,1},{6,2},{7,3},{8,12},{9,13},{10,... | collective-permute-start | bytes 2359304 | tf_op jit(solution)/shard_map/ppermute | solution.py:29
  132.8 63.4 %collective-permute-start.13 = (bf16[4,1024,128]{2,1,0:T(8,128)(2,1)S(1)}, bf16[4,1024,128]{2,1,0:T(8,128)(2,1)S(1)}, u32[]{:S(2)}, u32[]{:S(2)}) collective-permute-start(bf16[4,1024,128]{2,1,0:T(8,128)(2,1)S(1)} %shard_map.50), channel_id=1, source_target_pairs={{0,64},{8,72},{16,80},{24,88},{32,96},{40,104},{48,112},{56,120},{... | collective-permute-start | bytes 3145736 | tf_op jit(solution)/shard_map/ppermute | solution.py:27
  140.0 26.6 %collective-permute-start.15 = (bf16[96,32,128]{2,1,0:T(8,128)(2,1)S(1)}, bf16[96,32,128]{2,1,0:T(8,128)(2,1)S(1)}, u32[]{:S(2)}, u32[]{:S(2)}) collective-permute-start(bf16[96,32,128]{2,1,0:T(8,128)(2,1)S(1)} %shard_map.51.own), channel_id=1, source_target_pairs={{0,4},{1,5},{2,6},{3,7},{4,0},{5,1},{6,2},{7,3},{8,12},{9,13},{10,... | collective-permute-start | bytes 2359304 | tf_op jit(solution)/shard_map/ppermute | solution.py:29
